TPU v7x, 32 devices: a whole 2x2x4 slice. The times are simulated.
32 devices in a mesh: gx: 4 (over x, core), gy: 8 (over z, y).
Axes of the slice: x: 2, y: 2, z: 4, core: 2. Of those that a mesh axis runs over, the one named last changes fastest.
Arguments:
- xy_noisy: bfloat16 [256, 128, 128], P('gx', 'gy'), may hold values from -6 to 6
- xz_plane: bfloat16 [256, 64, 128], P('gy'), may hold values from -6 to 6
- yz_plane: bfloat16 [128, 64, 128], P('gx'), may hold values from -6 to 6
- labels: int32 [256, 128, 4], P('gx', 'gy'), may hold values from 0 to 19
- timestep: int32 [1], replicated, may hold values from 0 to 999
- conv1_weight: bfloat16 [3, 3, 128, 128], replicated, may hold values from -0.1875 to 0.1875
- conv2_weight: bfloat16 [3, 3, 128, 128], replicated, may hold values from -0.1875 to 0.1875
- time_weight: bfloat16 [128, 128], replicated, may hold values from -0.5 to 0.5
- w1: bfloat16 [128, 256], replicated, may hold values from -0.5 to 0.5
- w2: bfloat16 [256, 256], replicated, may hold values from -0.375 to 0.375
- w3: bfloat16 [256, 20], replicated, may hold values from -0.375 to 0.375
Outputs:
- grad_conv1: float32 [3, 3, 128, 128], replicated
- grad_conv2: float32 [3, 3, 128, 128], replicated
- grad_time: float32 [128, 128], replicated
- grad_w1: float32 [128, 256], replicated
- grad_w2: float32 [256, 256], replicated
- grad_w3: float32 [256, 20], replicated
- grad_xz: float32 [256, 4, 128], P('gy')
- grad_yz: float32 [128, 4, 128], P('gx')
All inputs are finite; a program needn't handle non-finite values.
Results may differ from a plain program's by a relative error of at most 0.014.
Values may be sent and summed in bfloat16 or wider, within the bound.
No kernel may reach another device: no remote copies, remote signals or barrier semaphores. Data moves between devices by JAX's collectives and lax.ppermute only.
A program may use at most 64 MiB of HBM per device.

v0:
```python
import math

import jax
import jax.numpy as jnp
from jax import lax
from jax.sharding import PartitionSpec as P

loss_weight = 1.0 / 256.0


def extended(array, sides, width):
    for axis, dim in sides:
        size, length = (lax.axis_size(axis), array.shape[dim])
        up = [(i, (i + 1) % size) for i in range(size - 1)]
        down = [(j, i) for i, j in up]
        last = lax.slice_in_dim(array, length - width, length, axis=dim)
        first = lax.slice_in_dim(array, 0, width, axis=dim)
        before = lax.ppermute(last, axis, up)
        after = lax.ppermute(first, axis, down)
        array = jnp.concatenate([before, array, after], axis=dim)
    return array


def broadcast(array, axis, root):
    mine = lax.axis_index(axis) == root
    return lax.psum(jnp.where(mine, array, jnp.zeros_like(array)), axis)


def silu_grad(value):
    sig = jax.nn.sigmoid(value)
    return sig * (1.0 + value * (1.0 - sig))


def patches(padded, nrows, ncols):
    taps = [padded[a : a + nrows, b : b + ncols] for a in range(3) for b in range(3)]
    return jnp.concatenate(taps, axis=-1).reshape(nrows * ncols, -1)


def time_embedding(timestep, width):
    half = width // 2
    freqs = jnp.exp(-math.log(10000.0) * jnp.arange(half, dtype=jnp.float32) / half)
    angle = timestep.astype(jnp.float32)[0] * freqs
    return jnp.concatenate([jnp.cos(angle), jnp.sin(angle)])


def decode(feat, label_flat, w1, w2, w3):
    u1 = jnp.dot(feat, w1, preferred_element_type=jnp.float32)
    g1 = jax.nn.silu(u1).astype(jnp.bfloat16)
    u2 = jnp.dot(g1, w2, preferred_element_type=jnp.float32)
    g2 = jax.nn.silu(u2).astype(jnp.bfloat16)
    logits = jnp.dot(g2, w3, preferred_element_type=jnp.float32)
    prob = jax.nn.softmax(logits, axis=-1)
    onehot = (label_flat[:, None] == jnp.arange(w3.shape[1], dtype=jnp.int32)[None, :]).astype(
        jnp.float32
    )
    dlogits = (loss_weight * (prob - onehot)).astype(jnp.bfloat16)
    dw3 = jnp.dot(g2.T, dlogits, preferred_element_type=jnp.float32)
    dg2 = jnp.dot(dlogits, w3.T, preferred_element_type=jnp.float32)
    du2 = (dg2 * silu_grad(u2)).astype(jnp.bfloat16)
    dw2 = jnp.dot(g1.T, du2, preferred_element_type=jnp.float32)
    dg1 = jnp.dot(du2, w2.T, preferred_element_type=jnp.float32)
    du1 = (dg1 * silu_grad(u1)).astype(jnp.bfloat16)
    dw1 = jnp.dot(feat.T, du1, preferred_element_type=jnp.float32)
    dfeat = jnp.dot(du1, w1.T, preferred_element_type=jnp.float32)
    return (dfeat, dw1, dw2, dw3)


def local(
    xy_noisy,
    xz_plane,
    yz_plane,
    labels,
    timestep,
    conv1_weight,
    conv2_weight,
    time_weight,
    w1,
    w2,
    w3,
):
    nrows, ncols, width = xy_noisy.shape
    depth = labels.shape[2]
    gx_index = lax.axis_index("gx")
    gy_index = lax.axis_index("gy")
    emb = time_embedding(timestep, width)
    temb = jnp.dot(emb, time_weight.astype(jnp.float32), precision=lax.Precision.HIGHEST)
    flat_one = conv1_weight.reshape(9 * width, width)
    flat_two = conv2_weight.reshape(9 * width, width)
    input_pad = extended(xy_noisy, (("gx", 0), ("gy", 1)), 1)
    input_patch = patches(input_pad, nrows, ncols)
    h1 = (
        jnp.dot(input_patch, flat_one, preferred_element_type=jnp.float32).reshape(
            nrows, ncols, width
        )
        + temb
    )
    hidden_pad = extended(jax.nn.silu(h1).astype(jnp.bfloat16), (("gx", 0), ("gy", 1)), 1)
    hidden_patch = patches(hidden_pad, nrows, ncols)
    xyd = jnp.dot(hidden_patch, flat_two, preferred_element_type=jnp.float32).astype(jnp.bfloat16)
    slab_count = xz_plane.shape[1] // depth
    start = timestep[0] % slab_count * depth
    xz_local = lax.dynamic_slice_in_dim(xz_plane, start, depth, 1)
    share = xz_local.shape[0]
    count = nrows // share
    xz_pieces = []
    for half in range(count):
        xz_pieces.append(broadcast(xz_local, "gy", gx_index * count + half))
    xz_rows = jnp.concatenate(xz_pieces, axis=0).astype(jnp.float32)
    yz_local = lax.dynamic_slice_in_dim(yz_plane, start, depth, 1)
    count_cols = yz_local.shape[0] // ncols
    yz_own = lax.dynamic_slice_in_dim(yz_local, gy_index % count_cols * ncols, ncols, 0)
    yz_cols = broadcast(yz_own, "gx", gy_index // count_cols).astype(jnp.float32)
    xy_tile = xyd.reshape(nrows, ncols, width).astype(jnp.float32)
    feat = xy_tile[:, :, None, :] + xz_rows[:, None, :, :] + yz_cols[None, :, :, :]
    feat = feat.astype(jnp.bfloat16).reshape(-1, width)
    dfeat, dw1, dw2, dw3 = decode(feat, labels.reshape(-1), w1, w2, w3)
    dfeat = dfeat.reshape(nrows, ncols, depth, width)
    dxz_local = jnp.sum(dfeat, axis=1)
    dyz_local = jnp.sum(dfeat, axis=0)
    dxyd = jnp.sum(dfeat, axis=2).astype(jnp.bfloat16)
    grad_conv2 = jnp.dot(
        hidden_patch.T, dxyd.reshape(-1, width), preferred_element_type=jnp.float32
    )
    grad_pad = extended(dxyd, (("gx", 0), ("gy", 1)), 1)
    back_flat = jnp.transpose(conv2_weight[::-1, ::-1], (0, 1, 3, 2)).reshape(9 * width, width)
    da1 = jnp.dot(
        patches(grad_pad, nrows, ncols), back_flat, preferred_element_type=jnp.float32
    ).reshape(nrows, ncols, width)
    dh1 = (da1 * silu_grad(h1)).astype(jnp.bfloat16)
    grad_conv1 = jnp.dot(input_patch.T, dh1.reshape(-1, width), preferred_element_type=jnp.float32)
    time_total = jnp.sum(dh1.astype(jnp.float32), axis=(0, 1))
    summed = lax.psum((grad_conv1, grad_conv2, time_total, dw1, dw2, dw3), ("gx", "gy"))
    grad_time = jnp.outer(emb, summed[2])
    xz_full = jnp.zeros((nrows * lax.axis_size("gx"), depth, width), jnp.float32)
    xz_full = lax.dynamic_update_slice_in_dim(xz_full, dxz_local, gx_index * nrows, 0)
    grad_xz = lax.psum(
        lax.psum_scatter(xz_full.astype(jnp.bfloat16), "gy", scatter_dimension=0, tiled=True), "gx"
    ).astype(jnp.float32)
    yz_full = jnp.zeros((ncols * lax.axis_size("gy"), depth, width), jnp.float32)
    yz_full = lax.dynamic_update_slice_in_dim(yz_full, dyz_local, gy_index * ncols, 0)
    grad_yz = lax.psum(
        lax.psum_scatter(yz_full.astype(jnp.bfloat16), "gx", scatter_dimension=0, tiled=True), "gy"
    ).astype(jnp.float32)
    return (
        summed[0].reshape(3, 3, width, width),
        summed[1].reshape(3, 3, width, width),
        grad_time,
        summed[3],
        summed[4],
        summed[5],
        grad_xz,
        grad_yz,
    )


def solution(mesh):
    placed = (
        P("gx", "gy", None),
        P("gy", None, None),
        P("gx", None, None),
        P("gx", "gy", None),
        P(),
        P(),
        P(),
        P(),
        P(),
        P(),
        P(),
    )
    return jax.shard_map(
        local,
        mesh=mesh,
        in_specs=placed,
        out_specs=(P(), P(), P(), P(), P(), P(), P("gy", None, None), P("gx", None, None)),
        check_vma=False,
    )
```

profile of v0, /device:TPU:0, one launch (start us, length us, event | category | flops | bytes accessed | tf_op | source)
XLA Modules:
  0.0 365.0 jit_solution(6712642686233982864)
XLA Ops:
  7.2 0.8 fusion.28
  8.0 2.3 collective-permute-start
  10.4 1.3 collective-permute-start.1
  12.3 1.5 broadcast_select_fusion.1
  14.1 1.0 constant_dynamic-update-slice_fusion.1
  15.6 3.8 %collective-permute-start.2 = (bf16[66,1,128]{2,1,0:T(2,128)(2,1)S(1)}, bf16[66,1,128]{2,1,0:T(2,128)(2,1)S(1)}, u32[]{:S(2)}, u32[]{:S(2)}) collective-permute-start(bf16[66,1,128]{2,1,0:T(2,128)(2,1)S(1)} %get-tuple-element.30), channel_id=1, source_target_pairs={{0,1},{1,2},{2,3},{3,4},{4,5},{5,6},{6,7},{8,9},{9,10},{10,11},{11... | collective-permute-start | bytes 50696 | tf_op jit(solution)/shard_map/ppermute | solution.py:18
  19.4 0.9 convolution_bitcast_fusion
  20.3 1.3 collective-permute-start.3
  21.7 1.0 fusion.19
  22.7 3.5 collective-permute-done.3
  27.3 1.6 multiply_convert_fusion.2
  28.9 3.3 collective-permute-start.4
  32.2 1.3 collective-permute-start.5
  33.5 0.9 dynamic-slice_select_fusion
  34.4 3.1 collective-permute-done.5
  37.6 4.4 %collective-permute-start.6 = (bf16[66,1,128]{2,1,0:T(2,128)(2,1)S(1)}, bf16[66,1,128]{2,1,0:T(2,128)(2,1)S(1)}, u32[]{:S(2)}, u32[]{:S(2)}) collective-permute-start(bf16[66,1,128]{2,1,0:T(2,128)(2,1)S(1)} %get-tuple-element.28), channel_id=1, source_target_pairs={{0,1},{1,2},{2,3},{3,4},{4,5},{5,6},{6,7},{8,9},{9,10},{10,11},{11... | collective-permute-start | bytes 50696 | tf_op jit(solution)/shard_map/ppermute | solution.py:18
  41.9 1.3 collective-permute-start.7
  43.2 12.2 %psum.79 = bf16[16,4,128]{2,1,0:T(4,128)(2,1)S(1)} all-reduce(bf16[16,4,128]{2,1,0:T(4,128)(2,1)S(1)} %dynamic-slice_select_fusion), channel_id=1, replica_groups=mesh['gx'=4,'gy'=8] {'gx'}, use_global_device_ids=true, to_apply=%region_2.3 | all-reduce | flops 8192 | bytes 32768 | tf_op jit(solution)/shard_map/psum | solution.py:26
  60.5 0.8 convolution_convert_fusion
  62.0 25.4 %all-reduce.16.cloned.1.call-done = (bf16[32,4,128]{2,1,0:T(4,128)(2,1)}, bf16[32,4,128]{2,1,0:T(4,128)(2,1)}) async-done(((bf16[32,4,128]{2,1,0:T(4,128)(2,1)}, bf16[32,4,128]{2,1,0:T(4,128)(2,1)}), (bf16[32,4,128]{2,1,0:T(4,128)(2,1)}, bf16[32,4,128]{2,1,0:T(4,128)(2,1)})) %all-reduce.16.cloned.1.call-update) | async-done | bytes 65552 | tf_op jit(solution)/shard_map/psum | solution.py:26
  87.4 0.8 maximum_convert_fusion
  88.9 1.2 multiply_convert_fusion.1
  90.1 1.2 multiply_convert_fusion
  92.2 1.8 fusion
  94.0 1.4 fusion.34
  95.4 1.8 fusion.1
  97.9 1.2 fusion.33
  99.1 2.0 fusion.24
  101.1 1.6 fusion.32
  102.8 1.3 collective-permute-start.8
  104.0 1.3 collective-permute-start.9
  106.2 2.7 collective-permute-done.9
  108.9 3.3 collective-permute-start.10
  112.2 1.3 collective-permute-start.11
  114.5 3.7 %collective-permute-done.11 = bf16[66,1,128]{2,1,0:T(2,128)(2,1)} collective-permute-done((bf16[66,1,128]{2,1,0:T(2,128)(2,1)S(1)}, bf16[66,1,128]{2,1,0:T(2,128)(2,1)}, u32[]{:S(2)}, u32[]{:S(2)}) %collective-permute-start.11) | collective-permute-done | bytes 16928 | tf_op jit(solution)/shard_map/ppermute | solution.py:19
  118.2 1.0 pad_maximum_fusion.1
  120.3 0.8 convert_reduce_fusion
  121.2 0.8 copy-done.11
  122.0 1.6 fusion.31
  124.1 41.8 %all-reduce.2 = (f32[128]{0:T(128)S(1)}, f32[256,20]{0,1:T(8,128)}) all-reduce(f32[128]{0:T(128)S(1)} %get-tuple-element.45, f32[256,20]{0,1:T(8,128)S(1)} %fusion.23), channel_id=1, replica_groups=mesh['gx'=4,'gy'=8] {'gx','gy'}, use_global_device_ids=true, to_apply=%region_9.10 | all-reduce | flops 5248 | bytes 41984 | tf_op jit(solution)/shard_map/psum | solution.py:132
  166.6 0.8 constant_dynamic-slice_fusion
  167.4 36.9 %psum.87 = bf16[32,4,128]{2,1,0:T(4,128)(2,1)S(1)} all-reduce(bf16[32,4,128]{2,1,0:T(4,128)(2,1)S(1)} %constant_dynamic-slice_fusion), channel_id=1, replica_groups=mesh['gx'=4,'gy'=8] {'gy'}, use_global_device_ids=true, to_apply=%region_18.19 | all-reduce | flops 16384 | bytes 65536 | tf_op jit(solution)/shard_map/psum | solution.py:141
  205.0 10.1 %all-reduce.10.cloned.1.call-done = bf16[256,4,128]{2,1,0:T(4,128)(2,1)} async-done(((bf16[256,4,128]{2,1,0:T(4,128)(2,1)}), bf16[256,4,128]{2,1,0:T(4,128)(2,1)}) %all-reduce.10.cloned.1.call-update) | async-done | bytes 262160
  215.0 0.8 constant_dynamic-slice_fusion.1
  215.8 10.3 %psum.86 = bf16[32,4,128]{2,1,0:T(4,128)(2,1)S(1)} all-reduce(bf16[32,4,128]{2,1,0:T(4,128)(2,1)S(1)} %constant_dynamic-slice_fusion.1), channel_id=1, replica_groups=mesh['gx'=4,'gy'=8] {'gx'}, use_global_device_ids=true, to_apply=%region_15.16 | all-reduce | flops 16384 | bytes 65536 | tf_op jit(solution)/shard_map/psum | solution.py:136
  226.7 126.5 %all-reduce.14.cloned.1.call-done = (f32[3,3,128,128]{3,2,1,0:T(8,128)}, f32[3,3,128,128]{3,2,1,0:T(8,128)}, f32[128,256]{1,0:T(8,128)}, f32[256,256]{1,0:T(8,128)}) async-done(((f32[3,3,128,128]{3,2,1,0:T(8,128)}, f32[3,3,128,128]{3,2,1,0:T(8,128)}, f32[128,256]{1,0:T(8,128)}, f32[256,256]{1,0:T(8,128)}), (f32[3,3,128,128]{3,2,1,0:T(8,128)}, f32[3,3,128,128]{3,2,1,0:T(8,128)}, f32[128,256]{1,0:T(8,128)}, ...) | async-done | bytes 1572880 | tf_op jit(solution)/shard_map/psum | solution.py:132
  353.3 2.0 copy.68
  355.2 1.9 copy.69
  (116 shorter events, 15.0 us)
Async XLA Ops:
  7.2 20.1 %copy-start = (bf16[3,3,128,128]{3,2,1,0:T(8,128)(2,1)S(1)}, bf16[3,3,128,128]{3,2,1,0:T(8,128)(2,1)}, u32[]{:S(2)}) copy-start(bf16[3,3,128,128]{3,2,1,0:T(8,128)(2,1)} %param.16) | copy-start | bytes 884740
  7.2 19.4 %copy-start.1 = (bf16[64,16,128]{2,1,0:T(8,128)(2,1)S(1)}, bf16[64,16,128]{2,1,0:T(8,128)(2,1)}, u32[]{:S(2)}) copy-start(bf16[64,16,128]{2,1,0:T(8,128)(2,1)} %param.11) | copy-start | bytes 786436
  7.2 80.2 %all-reduce.16.cloned.1.call-start = ((), (), s32[]{:S(2)}) async-start(), calls=%async_computation.3 | async-start | bytes 131072 | tf_op jit(solution)/shard_map/psum | solution.py:26
  8.0 6.0 %collective-permute-start = (bf16[1,16,128]{2,1,0:T(8,128)(2,1)S(1)}, bf16[1,16,128]{2,1,0:T(8,128)(2,1)S(1)}, u32[]{:S(2)}, u32[]{:S(2)}) collective-permute-start(bf16[1,16,128]{2,1,0:T(8,128)(2,1)S(1)} %get-tuple-element.36), channel_id=1, source_target_pairs={{0,8},{8,16},{16,24},{1,9},{9,17},{17,25},{2,10},{10,18},{18,26},{... | collective-permute-start | bytes 12296 | tf_op jit(solution)/shard_map/ppermute | solution.py:18
  10.4 5.2 %collective-permute-start.1 = (bf16[1,16,128]{2,1,0:T(8,128)(2,1)S(1)}, bf16[1,16,128]{2,1,0:T(8,128)(2,1)S(1)}, u32[]{:S(2)}, u32[]{:S(2)}) collective-permute-start(bf16[1,16,128]{2,1,0:T(8,128)(2,1)S(1)} %get-tuple-element.35), channel_id=1, source_target_pairs={{8,0},{16,8},{24,16},{9,1},{17,9},{25,17},{10,2},{18,10},{26,18},{... | collective-permute-start | bytes 12296 | tf_op jit(solution)/shard_map/ppermute | solution.py:19
  13.9 152.7 %all-reduce.12.cloned.1.call-start = ((), (), s32[]{:S(2)}) async-start(), calls=%async_computation.1 | async-start | bytes 262144
  15.6 6.0 %collective-permute-start.2 = (bf16[66,1,128]{2,1,0:T(2,128)(2,1)S(1)}, bf16[66,1,128]{2,1,0:T(2,128)(2,1)S(1)}, u32[]{:S(2)}, u32[]{:S(2)}) collective-permute-start(bf16[66,1,128]{2,1,0:T(2,128)(2,1)S(1)} %get-tuple-element.30), channel_id=1, source_target_pairs={{0,1},{1,2},{2,3},{3,4},{4,5},{5,6},{6,7},{8,9},{9,10},{10,11},{11... | collective-permute-start | bytes 50696 | tf_op jit(solution)/shard_map/ppermute | solution.py:18
  20.3 6.0 %collective-permute-start.3 = (bf16[66,1,128]{2,1,0:T(2,128)(2,1)S(1)}, bf16[66,1,128]{2,1,0:T(2,128)(2,1)S(1)}, u32[]{:S(2)}, u32[]{:S(2)}) collective-permute-start(bf16[66,1,128]{2,1,0:T(2,128)(2,1)S(1)} %get-tuple-element.29), channel_id=1, source_target_pairs={{1,0},{2,1},{3,2},{4,3},{5,4},{6,5},{7,6},{9,8},{10,9},{11,10},{12... | collective-permute-start | bytes 50696 | tf_op jit(solution)/shard_map/ppermute | solution.py:19
  27.2 1.6 copy-start.10
  27.3 28.2 %copy-start.9 = (s32[64,16,4]{0,2,1:T(4,128)S(1)}, s32[64,16,4]{0,2,1:T(4,128)}, u32[]{:S(2)}) copy-start(s32[64,16,4]{0,2,1:T(4,128)} %param.14) | copy-start | bytes 49156
  27.3 28.7 %copy-start.4 = (bf16[3,3,128,128]{3,2,1,0:T(8,128)(2,1)S(1)}, bf16[3,3,128,128]{3,2,1,0:T(8,128)(2,1)}, u32[]{:S(2)}) copy-start(bf16[3,3,128,128]{3,2,1,0:T(8,128)(2,1)} %param.17) | copy-start | bytes 884740
  28.9 28.1 %copy-start.19 = (u32[32]{0:T(128)S(1)}, u32[32]{0:T(128)}, u32[]{:S(2)}) copy-start(u32[32]{0:T(128)} %constant.97) | copy-start | bytes 388
  28.9 29.3 %copy-start.18 = (u32[32]{0:T(128)S(1)}, u32[32]{0:T(128)}, u32[]{:S(2)}) copy-start(u32[32]{0:T(128)} %constant.101) | copy-start | bytes 388
  28.9 5.5 %collective-permute-start.4 = (bf16[1,16,128]{2,1,0:T(8,128)(2,1)S(1)}, bf16[1,16,128]{2,1,0:T(8,128)(2,1)S(1)}, u32[]{:S(2)}, u32[]{:S(2)}) collective-permute-start(bf16[1,16,128]{2,1,0:T(8,128)(2,1)S(1)} %get-tuple-element.33), channel_id=1, source_target_pairs={{0,8},{8,16},{16,24},{1,9},{9,17},{17,25},{2,10},{10,18},{18,26},{... | collective-permute-start | bytes 12296 | tf_op jit(solution)/shard_map/ppermute | solution.py:18
  32.2 5.3 %collective-permute-start.5 = (bf16[1,16,128]{2,1,0:T(8,128)(2,1)S(1)}, bf16[1,16,128]{2,1,0:T(8,128)(2,1)S(1)}, u32[]{:S(2)}, u32[]{:S(2)}) collective-permute-start(bf16[1,16,128]{2,1,0:T(8,128)(2,1)S(1)} %get-tuple-element.34), channel_id=1, source_target_pairs={{8,0},{16,8},{24,16},{9,1},{17,9},{25,17},{10,2},{18,10},{26,18},{... | collective-permute-start | bytes 12296 | tf_op jit(solution)/shard_map/ppermute | solution.py:19
  37.6 21.9 %collective-permute-start.6 = (bf16[66,1,128]{2,1,0:T(2,128)(2,1)S(1)}, bf16[66,1,128]{2,1,0:T(2,128)(2,1)S(1)}, u32[]{:S(2)}, u32[]{:S(2)}) collective-permute-start(bf16[66,1,128]{2,1,0:T(2,128)(2,1)S(1)} %get-tuple-element.28), channel_id=1, source_target_pairs={{0,1},{1,2},{2,3},{3,4},{4,5},{5,6},{6,7},{8,9},{9,10},{10,11},{11... | collective-permute-start | bytes 50696 | tf_op jit(solution)/shard_map/ppermute | solution.py:18
  41.9 17.5 %collective-permute-start.7 = (bf16[66,1,128]{2,1,0:T(2,128)(2,1)S(1)}, bf16[66,1,128]{2,1,0:T(2,128)(2,1)S(1)}, u32[]{:S(2)}, u32[]{:S(2)}) collective-permute-start(bf16[66,1,128]{2,1,0:T(2,128)(2,1)S(1)} %get-tuple-element.27), channel_id=1, source_target_pairs={{1,0},{2,1},{3,2},{4,3},{5,4},{6,5},{7,6},{9,8},{10,9},{11,10},{12... | collective-permute-start | bytes 50696 | tf_op jit(solution)/shard_map/ppermute | solution.py:19
  60.5 1.4 copy-start.12
  62.0 26.9 %copy-start.8 = (bf16[128,256]{1,0:T(8,128)(2,1)S(1)}, bf16[128,256]{1,0:T(8,128)(2,1)}, u32[]{:S(2)}) copy-start(bf16[128,256]{1,0:T(8,128)(2,1)} %param.19) | copy-start | bytes 196612
  88.8 1.3 copy-start.17
  90.1 1.3 copy-start.16
  92.2 1.8 copy-start.14
  97.9 3.2 copy-start.13
  102.8 3.4 collective-permute-start.8
  104.0 4.8 %collective-permute-start.9 = (bf16[1,16,128]{2,1,0:T(8,128)(2,1)S(1)}, bf16[1,16,128]{2,1,0:T(8,128)(2,1)S(1)}, u32[]{:S(2)}, u32[]{:S(2)}) collective-permute-start(bf16[1,16,128]{2,1,0:T(8,128)(2,1)S(1)} %get-tuple-element.32), channel_id=1, source_target_pairs={{8,0},{16,8},{24,16},{9,1},{17,9},{25,17},{10,2},{18,10},{26,18},{... | collective-permute-start | bytes 12296 | tf_op jit(solution)/shard_map/ppermute | solution.py:19
  105.4 0.7 copy-start.3
  106.1 108.9 %all-reduce.10.cloned.1.call-start = ((), (), s32[]{:S(2)}) async-start(), calls=%async_computation | async-start | bytes 524288
  108.9 5.6 %collective-permute-start.10 = (bf16[66,1,128]{2,1,0:T(2,128)(2,1)S(1)}, bf16[66,1,128]{2,1,0:T(2,128)(2,1)S(1)}, u32[]{:S(2)}, u32[]{:S(2)}) collective-permute-start(bf16[66,1,128]{2,1,0:T(2,128)(2,1)S(1)} %get-tuple-element.24), channel_id=1, source_target_pairs={{0,1},{1,2},{2,3},{3,4},{4,5},{5,6},{6,7},{8,9},{9,10},{10,11},{11... | collective-permute-start | bytes 50696 | tf_op jit(solution)/shard_map/ppermute | solution.py:18
  112.2 5.9 %collective-permute-start.11 = (bf16[66,1,128]{2,1,0:T(2,128)(2,1)S(1)}, bf16[66,1,128]{2,1,0:T(2,128)(2,1)}, u32[]{:S(2)}, u32[]{:S(2)}) collective-permute-start(bf16[66,1,128]{2,1,0:T(2,128)(2,1)S(1)} %get-tuple-element.23), channel_id=1, source_target_pairs={{1,0},{2,1},{3,2},{4,3},{5,4},{6,5},{7,6},{9,8},{10,9},{11,10},{12... | collective-permute-start | bytes 50696 | tf_op jit(solution)/shard_map/ppermute | solution.py:19
  113.7 0.7 copy-start.2
  114.4 238.8 %all-reduce.14.cloned.1.call-start = ((), (), s32[]{:S(2)}) async-start(), calls=%async_computation.2 | async-start | bytes 3145728 | tf_op jit(solution)/shard_map/psum | solution.py:132
  119.2 1.0 copy-start.5
  119.2 1.1 copy-start.20
  120.3 1.7 copy-start.11
  122.0 1.7 copy-start.15
  353.3 3.9 %copy-start.7 = (f32[128,256]{1,0:T(8,128)S(1)}, f32[128,256]{1,0:T(8,128)}, u32[]{:S(2)}) copy-start(f32[128,256]{1,0:T(8,128)} %get-tuple-element.52) | copy-start | bytes 393220
  353.3 4.5 %copy-start.6 = (f32[256,256]{1,0:T(8,128)S(1)}, f32[256,256]{1,0:T(8,128)}, u32[]{:S(2)}) copy-start(f32[256,256]{1,0:T(8,128)} %get-tuple-element.53) | copy-start | bytes 786436
Sparse Core Ops, SparseCore 0:
  14.0 73.3 all-reduce.15
  106.2 34.3 all-reduce.11
  144.3 70.6 all-reduce.9
  221.1 132.1 all-reduce.13
where the time goes:
time: 366 us; the launch traced here: 365 us
  waiting for transfers between devices  176 us (48%)
  blocking collectives  101 us (28%)
  starting transfers between devices  26.4 us (7%)
  matrix products  17.8 us (5%)
  between operations  16.4 us (4%)
  local copies, waits for them, and re-layouts  16 us (4%)
  other arithmetic  11.8 us (3%)
    psum x1, waiting for transfers between devices, local(): lax.psum((grad_conv1, grad_conv2, time_total, dw1, dw2, dw3), ('gx', 'gy'))  127 us
    psum x1, blocking collectives, local(): lax.psum((grad_conv1, grad_conv2, time_total, dw1, dw2, dw3), ('gx', 'gy'))  41.8 us
    psum x1, blocking collectives, local(): lax.psum(lax.psum_scatter(yz_full.astype(jnp.bfloat16), 'gx', scatter_dim...  36.9 us
    psum x1, waiting for transfers between devices, broadcast(): return lax.psum(jnp.where(mine, array, jnp.zeros_like(array)), axis)  25.4 us
    ppermute x6, starting transfers between devices, extended(): before = lax.ppermute(last, axis, up)  18.4 us
    unnamed x67, local copies, waits for them, and re-layouts  13.8 us
    ppermute x6, waiting for transfers between devices, extended(): after = lax.ppermute(first, axis, down)  13.5 us
    psum x1, blocking collectives, broadcast(): return lax.psum(jnp.where(mine, array, jnp.zeros_like(array)), axis)  12.2 us
  transfers between devices with their start and end apart: 16, of which 8 were waited for; matrix products, arithmetic and copies ran while one was open for 6% of the time, Pallas kernels for 0%

commit v1 on v0

v1 whole, which is shorter than its diff:
```python
import math

import jax
import jax.numpy as jnp
from jax import lax
from jax.sharding import PartitionSpec as P

loss_weight = 1.0 / 256.0
BOTH = ("gx", "gy")
LANES = 128


def silu_grad(value):
    sig = jax.nn.sigmoid(value)
    return sig * (1.0 + value * (1.0 - sig))


def patches(padded, nrows, ncols):
    taps = [padded[a : a + nrows, b : b + ncols] for a in range(3) for b in range(3)]
    return jnp.concatenate(taps, axis=-1).reshape(nrows * ncols, -1)


def time_embedding(timestep, width):
    half = width // 2
    freqs = jnp.exp(-math.log(10000.0) * jnp.arange(half, dtype=jnp.float32) / half)
    angle = timestep.astype(jnp.float32)[0] * freqs
    return jnp.concatenate([jnp.cos(angle), jnp.sin(angle)])


class Grid:
    def __init__(self):
        self.nx, self.ny = lax.axis_size("gx"), lax.axis_size("gy")
        self.count = self.ny // self.nx
        self.ix, self.iy = lax.axis_index("gx"), lax.axis_index("gy")

    def move(self, array, target):
        pairs = []
        for i in range(self.nx):
            for j in range(self.ny):
                k, m = target(i, j)
                if 0 <= k < self.nx and 0 <= m < self.ny:
                    pairs.append((i * self.ny + j, k * self.ny + m))
        return lax.ppermute(array, BOTH, pairs)

    def turned(self, shift):
        count = self.count
        return lambda i, j: (j // count, count * i + (j % count + shift) % count)


def decode_forward(feat, label_flat, w1, w2, w3):
    u1 = jnp.dot(feat, w1, preferred_element_type=jnp.float32)
    g1 = jax.nn.silu(u1).astype(jnp.bfloat16)
    u2 = jnp.dot(g1, w2, preferred_element_type=jnp.float32)
    g2 = jax.nn.silu(u2).astype(jnp.bfloat16)
    logits = jnp.dot(g2, w3, preferred_element_type=jnp.float32)
    prob = jax.nn.softmax(logits, axis=-1)
    onehot = (label_flat[:, None] == jnp.arange(w3.shape[1], dtype=jnp.int32)[None, :]).astype(
        jnp.float32
    )
    dlogits = (loss_weight * (prob - onehot)).astype(jnp.bfloat16)
    dg2 = jnp.dot(dlogits, w3.T, preferred_element_type=jnp.float32)
    du2 = (dg2 * silu_grad(u2)).astype(jnp.bfloat16)
    dg1 = jnp.dot(du2, w2.T, preferred_element_type=jnp.float32)
    du1 = (dg1 * silu_grad(u1)).astype(jnp.bfloat16)
    dfeat = jnp.dot(du1, w1.T, preferred_element_type=jnp.float32)
    return g1, g2, dlogits, du2, du1, dfeat


def local(
    xy_noisy,
    xz_plane,
    yz_plane,
    labels,
    timestep,
    conv1_weight,
    conv2_weight,
    time_weight,
    w1,
    w2,
    w3,
):
    f32, bf16 = jnp.float32, jnp.bfloat16
    grid = Grid()
    nrows, ncols, width = xy_noisy.shape
    depth = labels.shape[2]
    count = grid.count
    side = grid.iy % count
    emb = time_embedding(timestep, width)
    temb = jnp.dot(emb, time_weight.astype(f32), precision=lax.Precision.HIGHEST)
    flat_one = conv1_weight.reshape(9 * width, width)
    flat_two = conv2_weight.reshape(9 * width, width)

    slab_count = xz_plane.shape[1] // depth
    start = timestep[0] % slab_count * depth
    xz_local = lax.dynamic_slice_in_dim(xz_plane, start, depth, 1)
    yz_local = lax.dynamic_slice_in_dim(yz_plane, start, depth, 1)
    share = xz_local.shape[0]
    yz_half = lax.dynamic_slice_in_dim(yz_local, side * ncols, ncols, 0)

    label_bf = labels.astype(bf16)
    up = lambda i, j: (i + 1, j)
    down = lambda i, j: (i - 1, j)
    left = lambda i, j: (i, j - 1)
    right = lambda i, j: (i, j + 1)
    reach = 3

    def pack(parts):
        flat = []
        for part in parts:
            part = part.reshape(-1)
            flat.append(jnp.pad(part, (0, -part.size % LANES)).reshape(-1, LANES))
        return jnp.concatenate(flat, axis=0)

    def unpack(packed, shapes):
        out, at = [], 0
        for shape in shapes:
            size = math.prod(shape)
            rows = -(-size // LANES)
            out.append(packed[at : at + rows].reshape(-1)[:size].reshape(shape))
            at += rows
        return out

    row_shapes = ((reach, ncols, width), (1, ncols, depth))
    above, label_above = unpack(
        grid.move(pack([xy_noisy[nrows - reach :], label_bf[nrows - 1 :]]), up), row_shapes
    )
    below, label_below = unpack(
        grid.move(pack([xy_noisy[:reach], label_bf[:1]]), down), row_shapes
    )
    first = grid.move(pack([yz_half, xz_local]), grid.turned(0))
    second = grid.move(xz_local, grid.turned(1))
    yz_cols, xz_same = unpack(first, ((ncols, depth, width), (share, depth, width)))
    xz_rows = jnp.where(
        side == 0,
        jnp.concatenate([xz_same, second], axis=0),
        jnp.concatenate([second, xz_same], axis=0),
    )
    edge = jnp.where(side == 0, xz_local[:1], xz_local[share - 1 :])
    rim_a = grid.move(
        edge, lambda i, j: (j // count - 1, count * i + 1) if j % count == 0 else (j // count + 1, count * i)
    )
    rim_b = grid.move(
        edge, lambda i, j: (j // count - 1, count * i) if j % count == 0 else (j // count + 1, count * i + 1)
    )
    xz_above = jnp.where(side == 0, rim_a, rim_b)
    xz_below = jnp.where(side == 0, rim_b, rim_a)

    tall = jnp.concatenate([above, xy_noisy, below], axis=0)
    label_tall = jnp.concatenate([label_above, label_bf, label_below], axis=0)
    col_shapes = ((nrows + 2 * reach, reach, width), (nrows + 2, 1, depth), (1, depth, width))
    before, label_before, yz_before = unpack(
        grid.move(pack([tall[:, ncols - reach :], label_tall[:, ncols - 1 :], yz_cols[ncols - 1 :]]), right),
        col_shapes,
    )
    after, label_after, yz_after = unpack(
        grid.move(pack([tall[:, :reach], label_tall[:, :1], yz_cols[:1]]), left), col_shapes
    )
    wide = jnp.concatenate([before, tall, after], axis=1)

    def inside(margin):
        rows = jnp.arange(-margin, nrows + margin) + grid.ix * nrows
        cols = jnp.arange(-margin, ncols + margin) + grid.iy * ncols
        row_ok = (rows >= 0) & (rows < nrows * grid.nx)
        col_ok = (cols >= 0) & (cols < ncols * grid.ny)
        return (row_ok[:, None] & col_ok[None, :])[:, :, None]

    h1 = (
        jnp.dot(patches(wide, nrows + 4, ncols + 4), flat_one, preferred_element_type=f32).reshape(
            nrows + 4, ncols + 4, width
        )
        + temb
    )
    a1 = jnp.where(inside(2), jax.nn.silu(h1), 0.0).astype(bf16)
    xyd = jnp.dot(patches(a1, nrows + 2, ncols + 2), flat_two, preferred_element_type=f32)
    xyd = xyd.astype(bf16).reshape(nrows + 2, ncols + 2, width)

    xz_all = jnp.concatenate([xz_above, xz_rows, xz_below], axis=0).astype(f32)
    yz_all = jnp.concatenate([yz_before, yz_cols, yz_after], axis=0).astype(f32)
    label_all = jnp.concatenate([label_before, label_tall, label_after], axis=1).astype(jnp.int32)

    def features(rows, cols):
        tile = xyd[rows, cols].astype(f32)
        feat = tile[:, :, None, :] + xz_all[rows, None, :, :] + yz_all[None, cols, :, :]
        return feat.astype(bf16).reshape(-1, width), label_all[rows, cols].reshape(-1)

    mid_r, mid_c = slice(1, nrows + 1), slice(1, ncols + 1)
    feat, lab = features(mid_r, mid_c)
    g1, g2, dlogits, du2, du1, dfeat = decode_forward(feat, lab, w1, w2, w3)
    dw3 = jnp.dot(g2.T, dlogits, preferred_element_type=f32)
    dw2 = jnp.dot(g1.T, du2, preferred_element_type=f32)
    dw1 = jnp.dot(feat.T, du1, preferred_element_type=f32)
    dfeat = dfeat.reshape(nrows, ncols, depth, width)
    dxz = jnp.sum(dfeat, axis=1)
    dyz = jnp.sum(dfeat, axis=0)
    dxyd = jnp.sum(dfeat, axis=2).astype(bf16)

    rims = (
        (slice(0, 1), slice(0, ncols + 2)),
        (slice(nrows + 1, nrows + 2), slice(0, ncols + 2)),
        (mid_r, slice(0, 1)),
        (mid_r, slice(ncols + 1, ncols + 2)),
    )
    rim_feat, rim_lab = zip(*[features(*r) for r in rims])
    *_, rim_dfeat = decode_forward(jnp.concatenate(rim_feat), jnp.concatenate(rim_lab), w1, w2, w3)
    rim_d = jnp.sum(rim_dfeat.reshape(-1, depth, width), axis=1).astype(bf16)
    n = ncols + 2
    top, bottom = rim_d[:n].reshape(1, n, width), rim_d[n : 2 * n].reshape(1, n, width)
    west = rim_d[2 * n : 2 * n + nrows].reshape(nrows, 1, width)
    east = rim_d[2 * n + nrows :].reshape(nrows, 1, width)
    dxyd_all = jnp.concatenate([top, jnp.concatenate([west, dxyd, east], axis=1), bottom], axis=0)
    dxyd_all = jnp.where(inside(1), dxyd_all, jnp.zeros_like(dxyd_all))

    grad_conv2 = jnp.dot(
        patches(a1[1:-1, 1:-1], nrows, ncols).T, dxyd.reshape(-1, width), preferred_element_type=f32
    )
    back_flat = jnp.transpose(conv2_weight[::-1, ::-1], (0, 1, 3, 2)).reshape(9 * width, width)
    da1 = jnp.dot(
        patches(dxyd_all, nrows, ncols), back_flat, preferred_element_type=f32
    ).reshape(nrows, ncols, width)
    dh1 = (da1 * silu_grad(h1[2:-2, 2:-2])).astype(bf16)
    grad_conv1 = jnp.dot(
        patches(wide[2:-2, 2:-2], nrows, ncols).T, dh1.reshape(-1, width), preferred_element_type=f32
    )
    time_total = jnp.sum(dh1.astype(f32), axis=(0, 1))

    def both(own, got):
        return own.astype(f32) + got.astype(f32)

    dxz = dxz.astype(bf16)
    low, high = dxz[:share], dxz[share:]
    keep = jnp.where(side == 0, low, high)
    give = jnp.where(side == 0, high, low)
    xz_sum = both(keep, grid.move(give, lambda i, j: (i, j ^ 1)))
    bit = 2
    while bit < grid.ny:
        own = xz_sum.astype(bf16)
        xz_sum = both(own, grid.move(own, lambda i, j, bit=bit: (i, j ^ bit)))
        bit *= 2
    grad_xz = grid.move(xz_sum.astype(bf16), grid.turned(0)).astype(f32)
    yz_sum = dyz
    bit = 1
    while bit < grid.nx:
        own = yz_sum.astype(bf16)
        yz_sum = both(own, grid.move(own, lambda i, j, bit=bit: (i ^ bit, j)))
        bit *= 2
    yz_sum = yz_sum.astype(bf16)
    yz_same = grid.move(yz_sum, grid.turned(0))
    yz_other = grid.move(yz_sum, grid.turned(1))
    grad_yz = jnp.where(
        side == 0,
        jnp.concatenate([yz_same, yz_other], axis=0),
        jnp.concatenate([yz_other, yz_same], axis=0),
    ).astype(f32)

    parts = (grad_conv1, grad_conv2, dw1, dw2, dw3, time_total)
    chips = grid.nx * grid.ny // 2
    rows = sum(-(-p.size // LANES) for p in parts)
    each = -(-rows // (2 * chips * 8)) * 8
    packed = pack(parts)
    packed = jnp.pad(packed, ((0, 2 * chips * each - rows), (0, 0))).reshape(2, chips, each, LANES)
    core = grid.ix % 2
    own = lax.dynamic_index_in_dim(packed, core, 0, keepdims=False)
    other = lax.dynamic_index_in_dim(packed, 1 - core, 0, keepdims=False).astype(bf16)
    own = own + grid.move(other, lambda i, j: (i ^ 1, j)).astype(f32)
    groups = [
        [i * grid.ny + j for i in range(c, grid.nx, 2) for j in range(grid.ny)] for c in range(2)
    ]
    pieces = lax.all_to_all(own.astype(bf16), BOTH, 0, 0, axis_index_groups=groups)
    total = jnp.sum(pieces.astype(f32), axis=0).astype(bf16)
    spread = jnp.broadcast_to(total[None], (chips, each, LANES))
    half = lax.all_to_all(spread, BOTH, 0, 0, axis_index_groups=groups)
    partner = grid.move(half, lambda i, j: (i ^ 1, j))
    whole = jnp.where(core == 0, jnp.stack([half, partner]), jnp.stack([partner, half]))
    whole = whole.reshape(-1, LANES)
    summed = [s.astype(f32) for s in unpack(whole, [p.shape for p in parts])]
    return (
        summed[0].reshape(3, 3, width, width),
        summed[1].reshape(3, 3, width, width),
        jnp.outer(emb, summed[5]),
        summed[2],
        summed[3],
        summed[4],
        grad_xz,
        grad_yz,
    )


def solution(mesh):
    placed = (
        P("gx", "gy", None),
        P("gy", None, None),
        P("gx", None, None),
        P("gx", "gy", None),
        P(),
        P(),
        P(),
        P(),
        P(),
        P(),
        P(),
    )
    return jax.shard_map(
        local,
        mesh=mesh,
        in_specs=placed,
        out_specs=(P(), P(), P(), P(), P(), P(), P("gy", None, None), P("gx", None, None)),
        check_vma=False,
    )
```

time: 366 us -> 180 us (0.49)
  the two profiles are of different devices: /device:TPU:0 before, /device:TPU:3 now
where the time goes in v1:
time: 180 us; the launch traced here: 178 us
  starting transfers between devices  50.8 us (28%)
  local copies, waits for them, and re-layouts  49.1 us (27%)
  matrix products  28.1 us (16%)
  other arithmetic  19.7 us (11%)
  blocking collectives  16.1 us (9%)
  waiting for transfers between devices  11.2 us (6%)
  between operations  2.85 us (2%)
    ppermute x18, starting transfers between devices, move(): return lax.ppermute(array, BOTH, pairs)  46.1 us
    unnamed x146, local copies, waits for them, and re-layouts  17.3 us
    all_to_all x1, blocking collectives, local(): lax.all_to_all(own.astype(bf16), BOTH, 0, 0, axis_index_groups=groups)  16.1 us
    ppermute x18, waiting for transfers between devices, move(): return lax.ppermute(array, BOTH, pairs)  11.2 us
    reshape x1, local copies, waits for them, and re-layouts, patches(): return jnp.concatenate(taps, axis=-1).reshape(nrows * ncols, -1)  5.55 us
    all_to_all x1, starting transfers between devices, local(): half = lax.all_to_all(spread, BOTH, 0, 0, axis_index_groups=groups)  4.67 us
    reshape x4, local copies, waits for them, and re-layouts, features(): label_all[rows, cols].reshape(-1)  4.39 us
    dot_general x2, matrix products, decode_forward(): dg2 = jnp.dot(dlogits, w3.T, preferred_element_type=jnp.float32)  4.01 us
  transfers between devices with their start and end apart: 19, of which 8 were waited for; matrix products, arithmetic and copies ran while one was open for 6% of the time, Pallas kernels for 0%

profile of v1, /device:TPU:3, one launch (start us, length us, event | category | flops | bytes accessed | tf_op | source)
XLA Modules:
  0.0 177.8 jit_solution(5057135037995736095)
XLA Ops:
  2.1 1.3 collective-permute-start.5
  4.9 4.9 %collective-permute-start.7 = (bf16[32,4,128]{2,1,0:T(4,128)(2,1)S(1)}, bf16[32,4,128]{2,1,0:T(4,128)(2,1)S(1)}, u32[]{:S(2)}, u32[]{:S(2)}) collective-permute-start(bf16[32,4,128]{2,1,0:T(4,128)(2,1)S(1)} %constant_dynamic-slice_fusion.2), channel_id=1, source_target_pairs={{0,1},{1,0},{2,9},{3,8},{4,17},{5,16},{6,25},{7,24},{8,3},{9,2},{1... | collective-permute-start | bytes 98312 | tf_op jit(solution)/shard_map/ppermute | solution.py:43
  9.8 7.6 %collective-permute-start.2 = (bf16[192,128]{1,0:T(8,128)(2,1)S(1)}, bf16[192,128]{1,0:T(8,128)(2,1)S(1)}, u32[]{:S(2)}, u32[]{:S(2)}) collective-permute-start(bf16[192,128]{1,0:T(8,128)(2,1)S(1)} %pad_maximum_fusion.11), channel_id=1, source_target_pairs={{0,0},{1,1},{2,8},{3,9},{4,16},{5,17},{6,24},{7,25},{8,2},{9,3},{1... | collective-permute-start | bytes 147464 | tf_op jit(solution)/shard_map/ppermute | solution.py:43
  19.3 1.3 collective-permute-start
  23.6 1.2 copy.56
  24.8 3.0 %collective-permute-start.1 = (bf16[49,128]{1,0:T(8,128)(2,1)S(1)}, bf16[49,128]{1,0:T(8,128)(2,1)S(1)}, u32[]{:S(2)}, u32[]{:S(2)}) collective-permute-start(bf16[49,128]{1,0:T(8,128)(2,1)S(1)} %pad_maximum_fusion.16), channel_id=1, source_target_pairs={{8,0},{9,1},{10,2},{11,3},{12,4},{13,5},{14,6},{15,7},{16,8},{17,9... | collective-permute-start | bytes 37640 | tf_op jit(solution)/shard_map/ppermute | solution.py:43
  29.9 1.3 collective-permute-start.3
  31.2 1.3 collective-permute-start.4
  33.9 2.3 %collective-permute-done.4 = bf16[217,128]{1,0:T(8,128)(2,1)S(1)} collective-permute-done((bf16[217,128]{1,0:T(8,128)(2,1)S(1)}, bf16[217,128]{1,0:T(8,128)(2,1)S(1)}, u32[]{:S(2)}, u32[]{:S(2)}) %collective-permute-start.4) | collective-permute-done | bytes 55584 | tf_op jit(solution)/shard_map/ppermute | solution.py:43
  37.6 2.0 %select_convert_fusion = (bf16[68,20,128]{2,0,1:T(8,128)(2,1)S(1)}, f32[68,20,128]{2,0,1:T(8,128)}) fusion(pred[68,20]{0,1:T(8,128)(4,1)S(1)} %broadcast_and_fusion.1, f32[128]{0:T(128)S(1)} %convolution_bitcast_fusion.2, bf16[68,20,1152]{2,0,1:T(8,128)(2,1)S(1)} %slice_dynamic-update-slice_fusion, bf16[1152,128,1]{1,0,2:T(8,128)(2,1)S(1)} %bitcast.175), kind=kOutput, calls=%fused_computation.25 | convolution fusion | flops 402298880 | bytes 4474704 | tf_op jit(solution)/shard_map/dot_general | solution.py:168
  40.7 2.3 %copy.48 = bf16[66,18,1152]{2,1,0:T(8,128)(2,1)} copy(bf16[66,18,1152]{2,0,1:T(8,128)(2,1)S(1)} %slice_dynamic-update-slice_fusion.9) | data formatting | bytes 5474304 | tf_op jit(solution)/shard_map/concatenate | solution.py:20
  43.0 5.5 %reshape.405 = bf16[1188,1152]{1,0:T(8,128)(2,1)} reshape(bf16[66,18,1152]{2,1,0:T(8,128)(2,1)} %copy.48) | data formatting | bytes 5474304 | tf_op jit(solution)/shard_map/reshape | solution.py:20
  48.5 2.7 %convolution_convert_fusion = bf16[1188,128]{1,0:T(8,128)(2,1)S(1)} fusion(bf16[1188,1152]{1,0:T(8,128)(2,1)} %reshape.405, bf16[1152,128]{1,0:T(8,128)(2,1)S(1)} %bitcast.156), kind=kOutput, calls=%fused_computation.12 | convolution fusion | flops 350507520 | bytes 3336192 | tf_op jit(solution)/shard_map/dot_general | solution.py:174
  55.3 1.2 multiply_convert_fusion.1
  56.6 1.3 multiply_convert_fusion
  58.6 1.4 fusion.49
  60.0 1.7 fusion
  61.8 1.5 fusion.60
  63.2 1.7 fusion.1
  65.8 1.2 fusion.59
  69.5 1.3 slice_reduce_fusion.1
  72.5 1.5 fusion.55
  74.0 1.4 reshape.410
  75.4 1.3 reshape.411
  81.5 2.3 %fusion.5 = bf16[656,256]{1,0:T(8,128)(2,1)} fusion(bf16[256,20]{0,1:T(8,128)(2,1)} %param.21, f32[656,256]{1,0:T(8,128)} %copy-done.50, f32[656,20]{0,1:T(8,128)} %get-tuple-element.64, s32[656]{0:T(1024)S(1)} %pad_add_fusion, f32[656]{0:T(1024)S(1)} %fusion.30, f32[656]{0:T(1024)} %get-tuple-element.63), kind=kOutput, calls=%fused_computation.18 | convolution fusion | flops 8320704 | bytes 1078208 | tf_op jit(solution)/shard_map/dot_general | solution.py:61
  83.8 2.5 %fusion.6 = f32[656,128]{1,0:T(8,128)} fusion(bf16[128,256]{1,0:T(8,128)(2,1)} %param.19, bf16[656,256]{1,0:T(8,128)(2,1)} %fusion.5, bf16[256,256]{1,0:T(8,128)(2,1)} %param.20, f32[656,256]{1,0:T(8,128)} %copy-done.8), kind=kOutput, calls=%fused_computation.19 | convolution fusion | flops 130486272 | bytes 1540096 | tf_op jit(solution)/shard_map/dot_general | solution.py:65
  86.3 1.8 %reduce_sum.76 = bf16[164,128]{1,0:T(8,128)(2,1)} reduce(f32[164,4,128]{2,1,0:T(4,128)} %bitcast.155, f32[]{:T(128)} %constant.110.clone.1), dimensions={1}, to_apply=%region_2.3 | reduce | flops 62976 | bytes 377860 | tf_op jit(solution)/shard_map/reduce_sum | solution.py:205
  88.1 1.4 slice_bitcast_fusion.1
  89.5 1.4 slice_bitcast_fusion.3
  90.9 1.9 %pad_maximum_fusion.1 = (bf16[70,19,128]{2,0,1:T(8,128)(2,1)}, bf16[70,19,128]{2,0,1:T(8,128)(2,1)}) fusion(bf16[70,3,128]{2,0,1:T(8,128)(2,1)} %copy-done.15, bf16[3,16,128]{2,0,1:T(4,128)(2,1)} %copy-done.16, bf16[64,16,128]{2,0,1:T(8,128)(2,1)S(1)} %copy.31, bf16[3,16,128]{2,0,1:T(4,128)(2,1)} %copy-done.18, bf16[70,3,128]{2,0,1:T(8,128)(2,1)} %copy-done.14), kind=kLoop, calls=%fused_computation.53 | loop fusion | flops 2723840 | bytes 1075200 | tf_op jit(solution)/shard_map/concatenate | solution.py:158
  92.8 2.5 %fusion.50 = (bf16[16,4,128]{2,1,0:T(4,128)(2,1)}, bf16[64,4,128]{2,1,0:T(4,128)(2,1)}, bf16[64,16,128]{2,1,0:T(8,128)(2,1)}) fusion(f32[64,16,4,128]{3,2,1,0:T(4,128)S(1)} %bitcast.140), kind=kLoop, calls=%fused_computation.212 | loop fusion | flops 1400832 | bytes 2441216 | tf_op jit(solution)/shard_map/reduce_sum | solution.py:194
  108.4 1.6 fusion.3
  110.1 1.6 fusion.2
  113.7 1.3 dynamic-update-slice.5
  115.0 1.5 pad.22
  116.6 3.7 %collective-permute-start.8 = (bf16[16,104,128]{2,1,0:T(8,128)(2,1)S(1)}, bf16[16,104,128]{2,1,0:T(8,128)(2,1)S(1)}, u32[]{:S(2)}, u32[]{:S(2)}) collective-permute-start(bf16[16,104,128]{2,1,0:T(8,128)(2,1)S(1)} %fusion.13), channel_id=1, source_target_pairs={{0,8},{1,9},{2,10},{3,11},{4,12},{5,13},{6,14},{7,15},{8,0},{9,1},... | collective-permute-start | bytes 1277960 | tf_op jit(solution)/shard_map/ppermute | solution.py:43
  120.3 1.4 collective-permute-done.8
  121.8 16.1 %all_to_all.10 = bf16[16,104,128]{2,1,0:T(8,128)(2,1)S(1)} all-to-all(bf16[16,104,128]{2,1,0:T(8,128)(2,1)S(1)} %fusion.7), channel_id=1, replica_groups={{0,1,2,3,4,5,6,7,16,17,18,19,20,21,22,23},{8,9,10,11,12,13,14,15,24,25,..., dimensions={0} | all-to-all | bytes 851968 | tf_op jit(solution)/shard_map/all_to_all | solution.py:268
  138.7 4.7 %all-to-all-start.1 = ((bf16[16,104,128]{2,1,0:T(8,128)(2,1)}), bf16[16,104,128]{2,1,0:T(8,128)(2,1)S(1)}, u32[]{:S(2)}, u32[]{:S(2)}) async-start(bf16[16,104,128]{2,1,0:T(8,128)(2,1)} %broadcast_in_dim.25), calls=%async_computation.1 | async-start | bytes 851968 | tf_op jit(solution)/shard_map/all_to_all | solution.py:271
  143.4 1.2 collective-permute-start.10
  144.7 2.2 %collective-permute-start.14 = (bf16[16,4,128]{2,1,0:T(4,128)(2,1)S(1)}, bf16[16,4,128]{2,1,0:T(4,128)(2,1)S(1)}, u32[]{:S(2)}, u32[]{:S(2)}) collective-permute-start(bf16[16,4,128]{2,1,0:T(4,128)(2,1)S(1)} %copy-done.31), channel_id=1, source_target_pairs={{0,8},{1,9},{2,10},{3,11},{4,12},{5,13},{6,14},{7,15},{8,0},{9,1},... | collective-permute-start | bytes 49160 | tf_op jit(solution)/shard_map/ppermute | solution.py:43
  148.5 2.6 %collective-permute-done.11 = bf16[32,4,128]{2,1,0:T(4,128)(2,1)S(1)} collective-permute-done((bf16[32,4,128]{2,1,0:T(4,128)(2,1)S(1)}, bf16[32,4,128]{2,1,0:T(4,128)(2,1)S(1)}, u32[]{:S(2)}, u32[]{:S(2)}) %collective-permute-start.11) | collective-permute-done | bytes 32800 | tf_op jit(solution)/shard_map/ppermute | solution.py:43
  151.1 2.5 %collective-permute-start.12 = (bf16[32,4,128]{2,1,0:T(4,128)(2,1)S(1)}, bf16[32,4,128]{2,1,0:T(4,128)(2,1)S(1)}, u32[]{:S(2)}, u32[]{:S(2)}) collective-permute-start(bf16[32,4,128]{2,1,0:T(4,128)(2,1)S(1)} %add_convert_fusion.4), channel_id=1, source_target_pairs={{0,4},{1,5},{2,6},{3,7},{4,0},{5,1},{6,2},{7,3},{8,12},{9,13},{10,... | collective-permute-start | bytes 98312 | tf_op jit(solution)/shard_map/ppermute | solution.py:43
  153.6 4.1 %collective-permute-start.9 = (bf16[16,104,128]{2,1,0:T(8,128)(2,1)S(1)}, bf16[16,104,128]{2,1,0:T(8,128)(2,1)S(1)}, u32[]{:S(2)}, u32[]{:S(2)}) collective-permute-start(bf16[16,104,128]{2,1,0:T(8,128)(2,1)S(1)} %all-to-all-done.1), channel_id=1, source_target_pairs={{0,8},{1,9},{2,10},{3,11},{4,12},{5,13},{6,14},{7,15},{8,0},{9,1},... | collective-permute-start | bytes 1277960 | tf_op jit(solution)/shard_map/ppermute | solution.py:43
  157.8 3.2 %collective-permute-start.16 = (bf16[16,4,128]{2,1,0:T(4,128)(2,1)S(1)}, bf16[16,4,128]{2,1,0:T(4,128)(2,1)S(1)}, u32[]{:S(2)}, u32[]{:S(2)}) collective-permute-start(bf16[16,4,128]{2,1,0:T(4,128)(2,1)S(1)} %add_convert_fusion.6), channel_id=1, source_target_pairs={{0,0},{1,1},{2,8},{3,9},{4,16},{5,17},{6,24},{7,25},{8,2},{9,3},{1... | collective-permute-start | bytes 49160 | tf_op jit(solution)/shard_map/ppermute | solution.py:43
  161.0 3.2 %collective-permute-start.17 = (bf16[16,4,128]{2,1,0:T(4,128)(2,1)S(1)}, bf16[16,4,128]{2,1,0:T(4,128)(2,1)S(1)}, u32[]{:S(2)}, u32[]{:S(2)}) collective-permute-start(bf16[16,4,128]{2,1,0:T(4,128)(2,1)S(1)} %add_convert_fusion.6), channel_id=1, source_target_pairs={{0,1},{1,0},{2,9},{3,8},{4,17},{5,16},{6,25},{7,24},{8,3},{9,2},{1... | collective-permute-start | bytes 49160 | tf_op jit(solution)/shard_map/ppermute | solution.py:43
  164.2 3.2 %collective-permute-start.13 = (bf16[32,4,128]{2,1,0:T(4,128)(2,1)S(1)}, bf16[32,4,128]{2,1,0:T(4,128)(2,1)S(1)}, u32[]{:S(2)}, u32[]{:S(2)}) collective-permute-start(bf16[32,4,128]{2,1,0:T(4,128)(2,1)S(1)} %add_convert_fusion.3), channel_id=1, source_target_pairs={{0,0},{1,1},{2,8},{3,9},{4,16},{5,17},{6,24},{7,25},{8,2},{9,3},{1... | collective-permute-start | bytes 98312 | tf_op jit(solution)/shard_map/ppermute | solution.py:43
  168.5 3.6 %collective-permute-done.13 = bf16[32,4,128]{2,1,0:T(4,128)(2,1)S(1)} collective-permute-done((bf16[32,4,128]{2,1,0:T(4,128)(2,1)S(1)}, bf16[32,4,128]{2,1,0:T(4,128)(2,1)S(1)}, u32[]{:S(2)}, u32[]{:S(2)}) %collective-permute-start.13) | collective-permute-done | bytes 32800 | tf_op jit(solution)/shard_map/ppermute | solution.py:43
  (299 shorter events, 51.3 us)
Async XLA Ops:
  0.6 9.2 %copy-start = (bf16[32,64,128]{2,1,0:T(8,128)(2,1)S(1)}, bf16[32,64,128]{2,1,0:T(8,128)(2,1)}, u32[]{:S(2)}) copy-start(bf16[32,64,128]{2,1,0:T(8,128)(2,1)} %param.13) | copy-start | bytes 1572868
  2.1 22.7 %collective-permute-start.5 = (bf16[1,4,128]{2,1,0:T(4,128)(2,1)S(1)}, bf16[1,4,128]{2,1,0:T(4,128)(2,1)S(1)}, u32[]{:S(2)}, u32[]{:S(2)}) collective-permute-start(bf16[1,4,128]{2,1,0:T(4,128)(2,1)S(1)} %fusion.39), channel_id=1, source_target_pairs={{1,8},{2,1},{3,16},{4,9},{5,24},{6,17},{9,10},{10,3},{11,18},{12,1... | collective-permute-start | bytes 3080 | tf_op jit(solution)/shard_map/ppermute | solution.py:43
  3.4 24.4 %collective-permute-start.6 = (bf16[1,4,128]{2,1,0:T(4,128)(2,1)S(1)}, bf16[1,4,128]{2,1,0:T(4,128)(2,1)S(1)}, u32[]{:S(2)}, u32[]{:S(2)}) collective-permute-start(bf16[1,4,128]{2,1,0:T(4,128)(2,1)S(1)} %fusion.39), channel_id=1, source_target_pairs={{1,9},{2,0},{3,17},{4,8},{5,25},{6,16},{9,11},{10,2},{11,19},{12,1... | collective-permute-start | bytes 3080 | tf_op jit(solution)/shard_map/ppermute | solution.py:43
  4.9 27.6 %collective-permute-start.7 = (bf16[32,4,128]{2,1,0:T(4,128)(2,1)S(1)}, bf16[32,4,128]{2,1,0:T(4,128)(2,1)S(1)}, u32[]{:S(2)}, u32[]{:S(2)}) collective-permute-start(bf16[32,4,128]{2,1,0:T(4,128)(2,1)S(1)} %constant_dynamic-slice_fusion.2), channel_id=1, source_target_pairs={{0,1},{1,0},{2,9},{3,8},{4,17},{5,16},{6,25},{7,24},{8,3},{9,2},{1... | collective-permute-start | bytes 98312 | tf_op jit(solution)/shard_map/ppermute | solution.py:43
  9.8 20.0 %collective-permute-start.2 = (bf16[192,128]{1,0:T(8,128)(2,1)S(1)}, bf16[192,128]{1,0:T(8,128)(2,1)S(1)}, u32[]{:S(2)}, u32[]{:S(2)}) collective-permute-start(bf16[192,128]{1,0:T(8,128)(2,1)S(1)} %pad_maximum_fusion.11), channel_id=1, source_target_pairs={{0,0},{1,1},{2,8},{3,9},{4,16},{5,17},{6,24},{7,25},{8,2},{9,3},{1... | collective-permute-start | bytes 147464 | tf_op jit(solution)/shard_map/ppermute | solution.py:43
  18.2 34.5 %copy-start.9 = (bf16[64,16,4]{0,2,1:T(4,128)(2,1)}, bf16[64,16,4]{0,2,1:T(4,128)(2,1)S(1)}, u32[]{:S(2)}) copy-start(bf16[64,16,4]{0,2,1:T(4,128)(2,1)S(1)} %convert_element_type.220) | copy-start | bytes 24580
  19.3 8.6 %collective-permute-start = (bf16[49,128]{1,0:T(8,128)(2,1)S(1)}, bf16[49,128]{1,0:T(8,128)(2,1)S(1)}, u32[]{:S(2)}, u32[]{:S(2)}) collective-permute-start(bf16[49,128]{1,0:T(8,128)(2,1)S(1)} %pad_maximum_fusion.15), channel_id=1, source_target_pairs={{0,8},{1,9},{2,10},{3,11},{4,12},{5,13},{6,14},{7,15},{8,16},{9,17... | collective-permute-start | bytes 37640 | tf_op jit(solution)/shard_map/ppermute | solution.py:43
  20.9 7.0 %copy-start.46 = (f32[128]{0:T(128)}, f32[128]{0:T(128)S(1)}, u32[]{:S(2)}) copy-start(f32[128]{0:T(128)S(1)} %pad_maximum_fusion.20) | copy-start | bytes 1540
  24.8 3.9 %collective-permute-start.1 = (bf16[49,128]{1,0:T(8,128)(2,1)S(1)}, bf16[49,128]{1,0:T(8,128)(2,1)S(1)}, u32[]{:S(2)}, u32[]{:S(2)}) collective-permute-start(bf16[49,128]{1,0:T(8,128)(2,1)S(1)} %pad_maximum_fusion.16), channel_id=1, source_target_pairs={{8,0},{9,1},{10,2},{11,3},{12,4},{13,5},{14,6},{15,7},{16,8},{17,9... | collective-permute-start | bytes 37640 | tf_op jit(solution)/shard_map/ppermute | solution.py:43
  27.9 8.6 %copy-start.18 = (bf16[3,16,128]{2,0,1:T(4,128)(2,1)}, bf16[3,16,128]{2,0,1:T(4,128)(2,1)S(1)}, u32[]{:S(2)}) copy-start(bf16[3,16,128]{2,0,1:T(4,128)(2,1)S(1)} %copy.30) | copy-start | bytes 36868
  28.7 7.9 %copy-start.16 = (bf16[3,16,128]{2,0,1:T(4,128)(2,1)}, bf16[3,16,128]{2,0,1:T(4,128)(2,1)S(1)}, u32[]{:S(2)}) copy-start(bf16[3,16,128]{2,0,1:T(4,128)(2,1)S(1)} %copy.32) | copy-start | bytes 36868
  28.8 23.8 %copy-start.25 = (bf16[1,16,4]{0,2,1:T(4,128)(2,1)}, bf16[1,16,4]{0,2,1:T(4,128)(2,1)S(1)}, u32[]{:S(2)}) copy-start(bf16[1,16,4]{0,2,1:T(4,128)(2,1)S(1)} %reshape.447) | copy-start | bytes 388
  29.0 23.6 %copy-start.27 = (bf16[1,16,4]{0,2,1:T(4,128)(2,1)}, bf16[1,16,4]{0,2,1:T(4,128)(2,1)S(1)}, u32[]{:S(2)}) copy-start(bf16[1,16,4]{0,2,1:T(4,128)(2,1)S(1)} %reshape.448) | copy-start | bytes 388
  29.9 3.9 %collective-permute-start.3 = (bf16[217,128]{1,0:T(8,128)(2,1)S(1)}, bf16[217,128]{1,0:T(8,128)(2,1)S(1)}, u32[]{:S(2)}, u32[]{:S(2)}) collective-permute-start(bf16[217,128]{1,0:T(8,128)(2,1)S(1)} %pad_maximum_fusion.6), channel_id=1, source_target_pairs={{0,1},{1,2},{2,3},{3,4},{4,5},{5,6},{6,7},{8,9},{9,10},{10,11},{11... | collective-permute-start | bytes 166664 | tf_op jit(solution)/shard_map/ppermute | solution.py:43
  31.2 5.0 %collective-permute-start.4 = (bf16[217,128]{1,0:T(8,128)(2,1)S(1)}, bf16[217,128]{1,0:T(8,128)(2,1)S(1)}, u32[]{:S(2)}, u32[]{:S(2)}) collective-permute-start(bf16[217,128]{1,0:T(8,128)(2,1)S(1)} %pad_maximum_fusion.7), channel_id=1, source_target_pairs={{1,0},{2,1},{3,2},{4,3},{5,4},{6,5},{7,6},{9,8},{10,9},{11,10},{12... | collective-permute-start | bytes 166664 | tf_op jit(solution)/shard_map/ppermute | solution.py:43
  33.8 20.8 %copy-start.29 = (bf16[64,128]{1,0:T(8,128)(2,1)}, bf16[64,128]{1,0:T(8,128)(2,1)S(1)}, u32[]{:S(2)}) copy-start(bf16[64,128]{1,0:T(8,128)(2,1)S(1)} %slice.487) | copy-start | bytes 49156
  43.0 5.6 %copy-start.22 = (bf16[3,3,128,128]{3,2,1,0:T(8,128)(2,1)S(1)}, bf16[3,3,128,128]{3,2,1,0:T(8,128)(2,1)}, u32[]{:S(2)}) copy-start(bf16[3,3,128,128]{3,2,1,0:T(8,128)(2,1)} %param.17) | copy-start | bytes 884740
  65.7 3.8 %copy-start.30 = (bf16[64,128]{1,0:T(8,128)(2,1)S(1)}, bf16[64,128]{1,0:T(8,128)(2,1)}, u32[]{:S(2)}) copy-start(bf16[64,128]{1,0:T(8,128)(2,1)} %copy-done.29) | copy-start | bytes 49156
  65.7 3.8 %copy-start.13 = (s32[66,18,4]{0,2,1:T(4,128)S(1)}, s32[66,18,4]{0,2,1:T(4,128)}, u32[]{:S(2)}) copy-start(s32[66,18,4]{0,2,1:T(4,128)} %copy-done.12) | copy-start | bytes 57028
  65.7 5.1 %copy-start.10 = (bf16[64,16,4]{0,2,1:T(4,128)(2,1)S(1)}, bf16[64,16,4]{0,2,1:T(4,128)(2,1)}, u32[]{:S(2)}) copy-start(bf16[64,16,4]{0,2,1:T(4,128)(2,1)} %copy-done.9) | copy-start | bytes 24580
  65.7 5.1 %copy-start.26 = (bf16[1,16,4]{0,2,1:T(4,128)(2,1)S(1)}, bf16[1,16,4]{0,2,1:T(4,128)(2,1)}, u32[]{:S(2)}) copy-start(bf16[1,16,4]{0,2,1:T(4,128)(2,1)} %copy-done.25) | copy-start | bytes 388
  65.7 5.1 %copy-start.28 = (bf16[1,16,4]{0,2,1:T(4,128)(2,1)S(1)}, bf16[1,16,4]{0,2,1:T(4,128)(2,1)}, u32[]{:S(2)}) copy-start(bf16[1,16,4]{0,2,1:T(4,128)(2,1)} %copy-done.27) | copy-start | bytes 388
  65.7 5.1 %copy-start.39 = (bf16[66,1,4]{0,2,1:T(4,128)(2,1)S(1)}, bf16[66,1,4]{0,2,1:T(4,128)(2,1)}, u32[]{:S(2)}) copy-start(bf16[66,1,4]{0,2,1:T(4,128)(2,1)} %copy-done.38) | copy-start | bytes 1588
  65.7 5.1 %copy-start.41 = (bf16[66,1,4]{0,2,1:T(4,128)(2,1)S(1)}, bf16[66,1,4]{0,2,1:T(4,128)(2,1)}, u32[]{:S(2)}) copy-start(bf16[66,1,4]{0,2,1:T(4,128)(2,1)} %copy-done.40) | copy-start | bytes 1588
  65.7 5.8 %copy-start.45 = (f32[4,128]{1,0:T(4,128)S(1)}, f32[4,128]{1,0:T(4,128)}, u32[]{:S(2)}) copy-start(f32[4,128]{1,0:T(4,128)} %get-tuple-element.38) | copy-start | bytes 6148
  65.7 5.8 %copy-start.44 = (f32[4,128]{1,0:T(4,128)S(1)}, f32[4,128]{1,0:T(4,128)}, u32[]{:S(2)}) copy-start(f32[4,128]{1,0:T(4,128)} %get-tuple-element.37) | copy-start | bytes 6148
  65.7 5.8 %copy-start.7 = (bf16[64,4,128]{2,1,0:T(4,128)(2,1)S(1)}, bf16[64,4,128]{2,1,0:T(4,128)(2,1)}, u32[]{:S(2)}) copy-start(bf16[64,4,128]{2,1,0:T(4,128)(2,1)} %copy-done.6) | copy-start | bytes 196612
  71.9 4.8 %copy-start.43 = (s32[64,1,4]{0,2,1:T(4,128)S(1)}, s32[64,1,4]{0,2,1:T(4,128)}, u32[]{:S(2)}) copy-start(s32[64,1,4]{0,2,1:T(4,128)} %get-tuple-element.45) | copy-start | bytes 3076
  71.9 6.3 %copy-start.42 = (s32[64,1,4]{0,2,1:T(4,128)S(1)}, s32[64,1,4]{0,2,1:T(4,128)}, u32[]{:S(2)}) copy-start(s32[64,1,4]{0,2,1:T(4,128)} %get-tuple-element.46) | copy-start | bytes 3076
  97.2 7.6 %copy-start.33 = (bf16[64,1,128]{2,0,1:T(8,128)(2,1)S(1)}, bf16[64,1,128]{2,0,1:T(8,128)(2,1)}, u32[]{:S(2)}) copy-start(bf16[64,1,128]{2,0,1:T(8,128)(2,1)} %get-tuple-element.53) | copy-start | bytes 49156
  97.3 7.6 %copy-start.32 = (bf16[64,1,128]{2,0,1:T(8,128)(2,1)S(1)}, bf16[64,1,128]{2,0,1:T(8,128)(2,1)}, u32[]{:S(2)}) copy-start(bf16[64,1,128]{2,0,1:T(8,128)(2,1)} %get-tuple-element.54) | copy-start | bytes 49156
  97.3 7.6 %copy-start.5 = (bf16[64,16,128]{2,1,0:T(8,128)(2,1)S(1)}, bf16[64,16,128]{2,1,0:T(8,128)(2,1)}, u32[]{:S(2)}) copy-start(bf16[64,16,128]{2,1,0:T(8,128)(2,1)} %get-tuple-element.18) | copy-start | bytes 786436
  97.3 7.6 %copy-start.34 = (pred[66,18]{1,0:T(8,128)(4,1)S(1)}, pred[66,18]{1,0:T(8,128)(4,1)}, u32[]{:S(2)}) copy-start(pred[66,18]{1,0:T(8,128)(4,1)} %broadcast_and_fusion) | copy-start | bytes 3568
  97.3 7.6 %copy-start.36 = (bf16[1,18,128]{2,1,0:T(8,128)(2,1)S(1)}, bf16[1,18,128]{2,1,0:T(8,128)(2,1)}, u32[]{:S(2)}) copy-start(bf16[1,18,128]{2,1,0:T(8,128)(2,1)} %get-tuple-element.52) | copy-start | bytes 13828
  116.6 26.8 %copy-start.11 = (bf16[64,4,128]{2,1,0:T(4,128)(2,1)S(1)}, bf16[64,4,128]{2,1,0:T(4,128)(2,1)}, u32[]{:S(2)}) copy-start(bf16[64,4,128]{2,1,0:T(4,128)(2,1)} %get-tuple-element.17) | copy-start | bytes 196612
  116.6 28.1 %copy-start.31 = (bf16[16,4,128]{2,1,0:T(4,128)(2,1)S(1)}, bf16[16,4,128]{2,1,0:T(4,128)(2,1)}, u32[]{:S(2)}) copy-start(bf16[16,4,128]{2,1,0:T(4,128)(2,1)} %get-tuple-element.16) | copy-start | bytes 49156
  116.6 5.1 %collective-permute-start.8 = (bf16[16,104,128]{2,1,0:T(8,128)(2,1)S(1)}, bf16[16,104,128]{2,1,0:T(8,128)(2,1)S(1)}, u32[]{:S(2)}, u32[]{:S(2)}) collective-permute-start(bf16[16,104,128]{2,1,0:T(8,128)(2,1)S(1)} %fusion.13), channel_id=1, source_target_pairs={{0,8},{1,9},{2,10},{3,11},{4,12},{5,13},{6,14},{7,15},{8,0},{9,1},... | collective-permute-start | bytes 1277960 | tf_op jit(solution)/shard_map/ppermute | solution.py:43
  138.7 14.9 %all-to-all-start.1 = ((bf16[16,104,128]{2,1,0:T(8,128)(2,1)}), bf16[16,104,128]{2,1,0:T(8,128)(2,1)S(1)}, u32[]{:S(2)}, u32[]{:S(2)}) async-start(bf16[16,104,128]{2,1,0:T(8,128)(2,1)} %broadcast_in_dim.25), calls=%async_computation.1 | async-start | bytes 851968 | tf_op jit(solution)/shard_map/all_to_all | solution.py:271
  143.4 3.5 %collective-permute-start.10 = (bf16[32,4,128]{2,1,0:T(4,128)(2,1)S(1)}, bf16[32,4,128]{2,1,0:T(4,128)(2,1)S(1)}, u32[]{:S(2)}, u32[]{:S(2)}) collective-permute-start(bf16[32,4,128]{2,1,0:T(4,128)(2,1)S(1)} %broadcast_select_fusion), channel_id=1, source_target_pairs={{0,1},{1,0},{2,3},{3,2},{4,5},{5,4},{6,7},{7,6},{8,9},{9,8},{10,11... | collective-permute-start | bytes 98312 | tf_op jit(solution)/shard_map/ppermute | solution.py:43
  144.7 3.5 %collective-permute-start.14 = (bf16[16,4,128]{2,1,0:T(4,128)(2,1)S(1)}, bf16[16,4,128]{2,1,0:T(4,128)(2,1)S(1)}, u32[]{:S(2)}, u32[]{:S(2)}) collective-permute-start(bf16[16,4,128]{2,1,0:T(4,128)(2,1)S(1)} %copy-done.31), channel_id=1, source_target_pairs={{0,8},{1,9},{2,10},{3,11},{4,12},{5,13},{6,14},{7,15},{8,0},{9,1},... | collective-permute-start | bytes 49160 | tf_op jit(solution)/shard_map/ppermute | solution.py:43
  147.0 4.0 %collective-permute-start.11 = (bf16[32,4,128]{2,1,0:T(4,128)(2,1)S(1)}, bf16[32,4,128]{2,1,0:T(4,128)(2,1)S(1)}, u32[]{:S(2)}, u32[]{:S(2)}) collective-permute-start(bf16[32,4,128]{2,1,0:T(4,128)(2,1)S(1)} %add_convert_fusion.5), channel_id=1, source_target_pairs={{0,2},{1,3},{2,0},{3,1},{4,6},{5,7},{6,4},{7,5},{8,10},{9,11},{10,... | collective-permute-start | bytes 98312 | tf_op jit(solution)/shard_map/ppermute | solution.py:43
  148.2 9.6 %collective-permute-start.15 = (bf16[16,4,128]{2,1,0:T(4,128)(2,1)S(1)}, bf16[16,4,128]{2,1,0:T(4,128)(2,1)S(1)}, u32[]{:S(2)}, u32[]{:S(2)}) collective-permute-start(bf16[16,4,128]{2,1,0:T(4,128)(2,1)S(1)} %add_convert_fusion.7), channel_id=1, source_target_pairs={{0,16},{1,17},{2,18},{3,19},{4,20},{5,21},{6,22},{7,23},{8,24},{9,... | collective-permute-start | bytes 49160 | tf_op jit(solution)/shard_map/ppermute | solution.py:43
  151.1 13.2 %collective-permute-start.12 = (bf16[32,4,128]{2,1,0:T(4,128)(2,1)S(1)}, bf16[32,4,128]{2,1,0:T(4,128)(2,1)S(1)}, u32[]{:S(2)}, u32[]{:S(2)}) collective-permute-start(bf16[32,4,128]{2,1,0:T(4,128)(2,1)S(1)} %add_convert_fusion.4), channel_id=1, source_target_pairs={{0,4},{1,5},{2,6},{3,7},{4,0},{5,1},{6,2},{7,3},{8,12},{9,13},{10,... | collective-permute-start | bytes 98312 | tf_op jit(solution)/shard_map/ppermute | solution.py:43
  153.6 19.2 %collective-permute-start.9 = (bf16[16,104,128]{2,1,0:T(8,128)(2,1)S(1)}, bf16[16,104,128]{2,1,0:T(8,128)(2,1)S(1)}, u32[]{:S(2)}, u32[]{:S(2)}) collective-permute-start(bf16[16,104,128]{2,1,0:T(8,128)(2,1)S(1)} %all-to-all-done.1), channel_id=1, source_target_pairs={{0,8},{1,9},{2,10},{3,11},{4,12},{5,13},{6,14},{7,15},{8,0},{9,1},... | collective-permute-start | bytes 1277960 | tf_op jit(solution)/shard_map/ppermute | solution.py:43
  157.8 9.6 %collective-permute-start.16 = (bf16[16,4,128]{2,1,0:T(4,128)(2,1)S(1)}, bf16[16,4,128]{2,1,0:T(4,128)(2,1)S(1)}, u32[]{:S(2)}, u32[]{:S(2)}) collective-permute-start(bf16[16,4,128]{2,1,0:T(4,128)(2,1)S(1)} %add_convert_fusion.6), channel_id=1, source_target_pairs={{0,0},{1,1},{2,8},{3,9},{4,16},{5,17},{6,24},{7,25},{8,2},{9,3},{1... | collective-permute-start | bytes 49160 | tf_op jit(solution)/shard_map/ppermute | solution.py:43
  161.0 6.8 %collective-permute-start.17 = (bf16[16,4,128]{2,1,0:T(4,128)(2,1)S(1)}, bf16[16,4,128]{2,1,0:T(4,128)(2,1)S(1)}, u32[]{:S(2)}, u32[]{:S(2)}) collective-permute-start(bf16[16,4,128]{2,1,0:T(4,128)(2,1)S(1)} %add_convert_fusion.6), channel_id=1, source_target_pairs={{0,1},{1,0},{2,9},{3,8},{4,17},{5,16},{6,25},{7,24},{8,3},{9,2},{1... | collective-permute-start | bytes 49160 | tf_op jit(solution)/shard_map/ppermute | solution.py:43
  164.2 7.9 %collective-permute-start.13 = (bf16[32,4,128]{2,1,0:T(4,128)(2,1)S(1)}, bf16[32,4,128]{2,1,0:T(4,128)(2,1)S(1)}, u32[]{:S(2)}, u32[]{:S(2)}) collective-permute-start(bf16[32,4,128]{2,1,0:T(4,128)(2,1)S(1)} %add_convert_fusion.3), channel_id=1, source_target_pairs={{0,0},{1,1},{2,8},{3,9},{4,16},{5,17},{6,24},{7,25},{8,2},{9,3},{1... | collective-permute-start | bytes 98312 | tf_op jit(solution)/shard_map/ppermute | solution.py:43
  173.0 4.2 %copy-start.47 = (f32[128]{0:T(128)S(1)}, f32[128]{0:T(128)}, u32[]{:S(2)}) copy-start(f32[128]{0:T(128)} %copy-done.46) | copy-start | bytes 1540
  (22 other events, 28.0 us)

commit v2 on v0

v2 whole, which is shorter than its diff:
```python
import functools
import math

import jax
import jax.numpy as jnp
from jax import lax
from jax.experimental import pallas as pl
from jax.experimental.pallas import tpu as pltpu
from jax.sharding import PartitionSpec as P

loss_weight = 1.0 / 256.0
BOTH = ("gx", "gy")
LANES = 128
PITCH = 24
REACH = 3
CLASS_ROWS = 32
F32, BF16 = jnp.float32, jnp.bfloat16
VMEM_LIMIT = 48 * 1024 * 1024


def sigmoid(value):
    return 0.5 * jnp.tanh(0.5 * value) + 0.5


def silu_pair(value):
    sig = sigmoid(value)
    out = value * sig
    return out, sig + out - out * sig


def dot(a, b):
    return jnp.dot(a, b, preferred_element_type=F32)


def dot_nt(a, b):
    return lax.dot_general(a, b, (((1,), (1,)), ((), ())), preferred_element_type=F32)


def dot_tn(a, b):
    return lax.dot_general(a, b, (((0,), (0,)), ((), ())), preferred_element_type=F32)


def time_embedding(timestep, width):
    half = width // 2
    freqs = jnp.exp(-math.log(10000.0) * jnp.arange(half, dtype=jnp.float32) / half)
    angle = timestep.astype(jnp.float32)[0] * freqs
    return jnp.concatenate([jnp.cos(angle), jnp.sin(angle)])


class Grid:
    def __init__(self):
        self.nx, self.ny = lax.axis_size("gx"), lax.axis_size("gy")
        self.count = self.ny // self.nx
        self.ix, self.iy = lax.axis_index("gx"), lax.axis_index("gy")

    def move(self, array, target):
        pairs = []
        for i in range(self.nx):
            for j in range(self.ny):
                k, m = target(i, j)
                if 0 <= k < self.nx and 0 <= m < self.ny:
                    pairs.append((i * self.ny + j, k * self.ny + m))
        return lax.ppermute(array, BOTH, pairs)

    def turned(self, shift):
        count = self.count
        return lambda i, j: (j // count, count * i + (j % count + shift) % count)


def gradient_rows(width, hidden):
    sizes = (
        ("conv1", 9 * width),
        ("conv2", 9 * width),
        ("w1", width * hidden // LANES),
        ("w2", hidden * hidden // LANES),
        ("w3", CLASS_ROWS * hidden // LANES),
        ("time", 16),
    )
    at, total = {}, 0
    for name, rows in sizes:
        at[name] = total
        total += rows
    return at, total


def main_kernel(
    classes,
    place,
    xy,
    above,
    below,
    before,
    after,
    labels,
    xz_same,
    xz_second,
    xz_above,
    xz_below,
    yz_cols,
    temb,
    conv1,
    conv2,
    back,
    w1,
    w2,
    w3,
    packed,
    dxz_out,
    dyz_out,
    xs,
    hs,
    acts,
    xyds,
    dx,
    patch,
    xzs,
    dw1,
    dw2,
    dw3,
    dyz,
):
    nrows, ncols, width = xy.shape
    depth = labels.shape[2]
    hidden = w1.shape[1]
    share = xz_same.shape[1]
    at, _ = gradient_rows(width, hidden)
    side = place[0]
    open_up, open_down, open_left, open_right = (place[1] > 0, place[2] > 0, place[3] > 0, place[4] > 0)

    mid_r, mid_c = slice(REACH, REACH + nrows), slice(REACH, REACH + ncols)
    xs[...] = jnp.zeros_like(xs)
    xs[mid_r, mid_c] = xy[...].astype(F32)
    xs[0:REACH, mid_c] = above[0:REACH].astype(F32)
    xs[REACH + nrows : 2 * REACH + nrows, mid_c] = below[0:REACH].astype(F32)
    xs[:, 0:REACH] = before[...].astype(F32)[:, 0:REACH]
    xs[:, REACH + ncols : 2 * REACH + ncols] = after[...].astype(F32)[:, 0:REACH]

    def gather(source, row, col, rows, cols):
        count = rows * cols
        for a in range(3):
            for b in range(3):
                piece = source[row + a : row + a + rows, col + b : col + b + cols, :]
                tap = (3 * a + b) * width
                patch[0:count, tap : tap + width] = piece.reshape(count, width).astype(BF16)
        return count

    n1 = gather(xs, 0, 0, nrows + 4, PITCH)
    h1 = dot(patch[0:n1], conv1[...]) + temb[...]
    h1 = h1.reshape(nrows + 4, PITCH, width)
    hs[...] = h1
    row = lax.broadcasted_iota(jnp.int32, h1.shape, 0)
    col = lax.broadcasted_iota(jnp.int32, h1.shape, 1)
    low_r = jnp.where(open_up, 0, 2)
    high_r = jnp.where(open_down, nrows + 4, nrows + 2)
    low_c = jnp.where(open_left, 0, 2)
    high_c = jnp.where(open_right, ncols + 4, ncols + 2)
    inside = (row >= low_r) & (row < high_r) & (col >= low_c) & (col < high_c)
    a1 = jnp.where(inside, h1 * sigmoid(h1), 0.0)
    acts[...] = jnp.zeros_like(acts)
    acts[:, 0:PITCH] = a1.astype(BF16).astype(F32)
    n2 = gather(acts, 0, 0, nrows + 2, PITCH)
    xyd = dot(patch[0:n2], conv2[...])
    xyds[...] = xyd.astype(BF16).astype(F32).reshape(nrows + 2, PITCH, width)

    xzs[:, pl.ds(pl.multiple_of(side * share, share), share), :] = xz_same[...].astype(F32)
    xzs[:, pl.ds(pl.multiple_of((1 - side) * share, share), share), :] = xz_second[...].astype(F32)

    def decode(feat, label):
        u1 = dot(feat, w1[...])
        g1, s1 = silu_pair(u1)
        g1 = g1.astype(BF16)
        u2 = dot(g1, w2[...])
        g2, s2 = silu_pair(u2)
        g2 = g2.astype(BF16)
        logits = dot(g2, w3[...])
        lane = lax.broadcasted_iota(jnp.int32, logits.shape, 1)
        logits = jnp.where(lane < classes, logits, -jnp.inf)
        power = jnp.exp(logits - jnp.max(logits, axis=1, keepdims=True))
        prob = power / jnp.sum(power, axis=1, keepdims=True)
        onehot = jnp.where(lane == label, 1.0, 0.0)
        dlogits = (loss_weight * (prob - onehot)).astype(BF16)
        du2 = (dot_nt(dlogits, w3[...]) * s2).astype(BF16)
        du1 = (dot_nt(du2, w2[...]) * s1).astype(BF16)
        return g1, g2, dlogits, du2, du1, dot_nt(du1, w1[...])

    dw1[...] = jnp.zeros_like(dw1)
    dw2[...] = jnp.zeros_like(dw2)
    dw3[...] = jnp.zeros_like(dw3)
    dyz[...] = jnp.zeros_like(dyz)
    dx[...] = jnp.zeros_like(dx)
    chunk = 16
    size = chunk * ncols

    def step(index, carry):
        r0 = pl.multiple_of(index * chunk, chunk)
        tile = xyds[pl.ds(r0 + 1, chunk), 1 : ncols + 1, :]
        lab = labels[pl.ds(r0, chunk)].reshape(size, depth)
        feats, labs = [], []
        for k in range(depth):
            xz_k = xzs[k, pl.ds(r0, chunk), :]
            feat = tile + xz_k[:, None, :] + yz_cols[k].astype(F32)[None]
            feats.append(feat.reshape(size, width).astype(BF16))
            labs.append(jnp.broadcast_to(lab[:, k : k + 1], (size, LANES)))
        feat = jnp.concatenate(feats, axis=0)
        g1, g2, dlogits, du2, du1, dfeat = decode(feat, jnp.concatenate(labs, axis=0))
        dw3[...] += dot_tn(dlogits, g2)
        dw2[...] += dot_tn(g1, du2)
        dw1[...] += dot_tn(feat, du1)
        total = jnp.zeros((chunk, ncols, width), F32)
        for k in range(depth):
            piece = dfeat[k * size : (k + 1) * size].reshape(chunk, ncols, width)
            total = total + piece
            dxz_out[k, pl.ds(r0, chunk), :] = jnp.sum(piece, axis=1).astype(BF16)
            dyz[k] += jnp.sum(piece, axis=0)
        dx[pl.ds(r0 + 1, chunk), 1 : ncols + 1, :] = total.astype(BF16).astype(F32)
        return carry

    lax.fori_loop(0, nrows // chunk, step, 0)
    dyz_out[...] = dyz[...].astype(BF16)

    lab_before = before[2 : nrows + 4, 3, :].astype(F32).astype(jnp.int32)
    lab_after = after[2 : nrows + 4, 3, :].astype(F32).astype(jnp.int32)
    lab_up = above[3].astype(F32).astype(jnp.int32)
    lab_down = below[3].astype(F32).astype(jnp.int32)
    tail = jnp.zeros((PITCH - ncols - 2, LANES), jnp.int32)
    lab_rim = jnp.concatenate(
        [
            lab_before[0:1],
            lab_up,
            lab_after[0:1],
            tail,
            lab_before[nrows + 1 : nrows + 2],
            lab_down,
            lab_after[nrows + 1 : nrows + 2],
            tail,
            lab_before[1 : nrows + 1],
            lab_after[1 : nrows + 1],
        ],
        axis=0,
    )
    rim_at = (0, 1, nrows + 2 * REACH - 2, nrows + 2 * REACH - 1)
    feats, labs = [], []
    zero_tail = jnp.zeros((PITCH - ncols - 2, width), F32)
    for k in range(depth):
        yz_before = before[rim_at[k], 3:4, :].astype(F32)
        yz_after = after[rim_at[k], 3:4, :].astype(F32)
        yz_row = jnp.concatenate([yz_before, yz_cols[k].astype(F32), yz_after, zero_tail], axis=0)
        feats.append(xyds[0] + xz_above[k].astype(F32) + yz_row)
        feats.append(xyds[nrows + 1] + xz_below[k].astype(F32) + yz_row)
        feats.append(xyds[1 : nrows + 1, 0, :] + xzs[k] + yz_before)
        feats.append(xyds[1 : nrows + 1, ncols + 1, :] + xzs[k] + yz_after)
        labs.append(jnp.broadcast_to(lab_rim[:, k : k + 1], (2 * PITCH + 2 * nrows, LANES)))
    rim = decode(jnp.concatenate(feats, axis=0).astype(BF16), jnp.concatenate(labs, axis=0))[-1]
    span = 2 * PITCH + 2 * nrows
    rim_sum = rim[0:span]
    for k in range(1, depth):
        rim_sum = rim_sum + rim[k * span : (k + 1) * span]
    rim_sum = rim_sum.astype(BF16).astype(F32)
    rcol = lax.broadcasted_iota(jnp.int32, (PITCH, width), 0)
    keep = (rcol >= jnp.where(open_left, 0, 1)) & (rcol < jnp.where(open_right, ncols + 2, ncols + 1))
    dx[0] = jnp.where(keep & open_up, rim_sum[0:PITCH], 0.0)
    dx[nrows + 1] = jnp.where(keep & open_down, rim_sum[PITCH : 2 * PITCH], 0.0)
    west = rim_sum[2 * PITCH : 2 * PITCH + nrows]
    east = rim_sum[2 * PITCH + nrows : span]
    dx[1 : nrows + 1, 0, :] = jnp.where(open_left, west, 0.0)
    dx[1 : nrows + 1, ncols + 1, :] = jnp.where(open_right, east, 0.0)

    def weight_gradient(start, dout):
        grad = dot_tn(dout, patch[0 : nrows * ncols])
        for tap in range(9):
            block = grad[:, tap * width : (tap + 1) * width].T
            packed[start + tap * width : start + (tap + 1) * width, :] = block.astype(BF16)

    n3 = gather(acts, 1, 1, nrows, ncols)
    dxyd = dx[1 : nrows + 1, 1 : ncols + 1, :].reshape(n3, width).astype(BF16)
    weight_gradient(at["conv2"], dxyd)
    gather(dx, 0, 0, nrows, ncols)
    da1 = dot(patch[0:n3], back[...])
    _, slope = silu_pair(hs[2 : nrows + 2, 2 : ncols + 2, :].reshape(n3, width))
    dh1 = (da1 * slope).astype(BF16)
    gather(xs, 2, 2, nrows, ncols)
    weight_gradient(at["conv1"], dh1)

    parts = ((at["w1"], dw1, width), (at["w2"], dw2, hidden), (at["w3"], dw3, CLASS_ROWS))
    for start, ref, rows in parts:
        for half in range(hidden // LANES):
            packed[start + half * rows : start + (half + 1) * rows, :] = ref[
                0:rows, half * LANES : (half + 1) * LANES
            ].astype(BF16)
    time_row = jnp.sum(dh1.astype(F32), axis=0, keepdims=True)
    packed[at["time"] : at["time"] + 16, :] = jnp.broadcast_to(time_row, (16, LANES)).astype(BF16)
    used = at["time"] + 16
    if packed.shape[0] > used:
        packed[used:, :] = jnp.zeros((packed.shape[0] - used, LANES), BF16)


def last_kernel(hidden, classes, place, half, partner, emb, g1, g2, gt, gw1, gw2, gw3, whole):
    rows = half.shape[0]
    width = emb.shape[0]
    at, _ = gradient_rows(width, hidden)
    core = place[0]
    whole[pl.ds(pl.multiple_of(core * rows, rows), rows), :] = half[...]
    whole[pl.ds(pl.multiple_of((1 - core) * rows, rows), rows), :] = partner[...]
    g1[...] = whole[at["conv1"] : at["conv1"] + 9 * width, :].astype(F32).reshape(9, width, LANES)
    g2[...] = whole[at["conv2"] : at["conv2"] + 9 * width, :].astype(F32).reshape(9, width, LANES)
    gt[...] = emb[...] * whole[at["time"] : at["time"] + 16, :].astype(F32)[0:1]
    for half_index in range(hidden // LANES):
        lanes = slice(half_index * LANES, (half_index + 1) * LANES)
        for start, ref, size in ((at["w1"], gw1, width), (at["w2"], gw2, hidden)):
            begin = start + half_index * size
            ref[:, lanes] = whole[begin : begin + size, :].astype(F32)
        begin = at["w3"] + half_index * CLASS_ROWS
        block = whole[begin : begin + CLASS_ROWS, :].astype(F32)
        block = jnp.concatenate([block, jnp.zeros((LANES - CLASS_ROWS, LANES), F32)], axis=0).T
        gw3[lanes, :] = block[:, 0:classes]


def local(
    xy_noisy,
    xz_plane,
    yz_plane,
    labels,
    timestep,
    conv1_weight,
    conv2_weight,
    time_weight,
    w1,
    w2,
    w3,
):
    grid = Grid()
    nrows, ncols, width = xy_noisy.shape
    depth = labels.shape[2]
    hidden, classes = w3.shape
    count = grid.count
    side = grid.iy % count
    emb = time_embedding(timestep, width)
    temb = jnp.dot(emb, time_weight.astype(F32), precision=lax.Precision.HIGHEST)
    flat_one = conv1_weight.reshape(9 * width, width)
    flat_two = conv2_weight.reshape(9 * width, width)
    back_flat = jnp.transpose(conv2_weight[::-1, ::-1], (0, 1, 3, 2)).reshape(9 * width, width)
    w3_wide = jnp.pad(w3, ((0, 0), (0, LANES - classes)))

    up = lambda i, j: (i + 1, j)
    down = lambda i, j: (i - 1, j)
    left = lambda i, j: (i, j - 1)
    right = lambda i, j: (i, j + 1)

    def lab(part):
        return jnp.pad(part.astype(BF16), ((0, 0), (0, 0), (0, LANES - depth)))

    above = grid.move(jnp.concatenate([xy_noisy[nrows - REACH :], lab(labels[nrows - 1 :])]), up)
    below = grid.move(jnp.concatenate([xy_noisy[:REACH], lab(labels[:1])]), down)

    slab_count = xz_plane.shape[1] // depth
    start = timestep[0] % slab_count * depth
    xz_local = jnp.transpose(lax.dynamic_slice_in_dim(xz_plane, start, depth, 1), (1, 0, 2))
    yz_local = jnp.transpose(lax.dynamic_slice_in_dim(yz_plane, start, depth, 1), (1, 0, 2))
    share = xz_local.shape[1]
    yz_half = lax.dynamic_slice_in_dim(yz_local, side * ncols, ncols, 1)
    first = grid.move(jnp.concatenate([yz_half, xz_local], axis=1), grid.turned(0))
    xz_second = grid.move(xz_local, grid.turned(1))
    yz_cols, xz_same = first[:, :ncols], first[:, ncols:]
    edge = jnp.where(side == 0, xz_local[:, :1], xz_local[:, share - 1 :])
    rim_a = grid.move(
        edge,
        lambda i, j: (j // count - 1, count * i + 1) if j % count == 0 else (j // count + 1, count * i),
    )
    rim_b = grid.move(
        edge,
        lambda i, j: (j // count - 1, count * i) if j % count == 0 else (j // count + 1, count * i + 1),
    )
    xz_above = jnp.where(side == 0, rim_a, rim_b)
    xz_below = jnp.where(side == 0, rim_b, rim_a)

    def column(at, where):
        cols = jnp.concatenate(
            [above[:REACH, where], xy_noisy[:, where], below[:REACH, where]], axis=0
        )
        yz = yz_cols[:, at : at + 1]
        extra = jnp.concatenate(
            [yz[:2], above[3:, at : at + 1], lab(labels[:, at : at + 1]), below[3:, at : at + 1], yz[2:]],
            axis=0,
        )
        return jnp.concatenate([cols, extra], axis=1)

    before = grid.move(column(ncols - 1, slice(ncols - REACH, ncols)), right)
    after = grid.move(column(0, slice(0, REACH)), left)

    flags = jnp.stack(
        [side, grid.ix, grid.nx - 1 - grid.ix, grid.iy, grid.ny - 1 - grid.iy]
    ).astype(jnp.int32)
    chips = grid.nx * grid.ny // 2
    _, rows = gradient_rows(width, hidden)
    each = -(-rows // (2 * chips * 8)) * 8
    vmem = pl.BlockSpec(memory_space=pltpu.VMEM)
    smem = pl.BlockSpec(memory_space=pltpu.SMEM)
    packed, dxz, dyz = pl.pallas_call(
        functools.partial(main_kernel, classes),
        out_shape=(
            jax.ShapeDtypeStruct((2 * chips * each, LANES), BF16),
            jax.ShapeDtypeStruct((depth, nrows, width), BF16),
            jax.ShapeDtypeStruct((depth, ncols, width), BF16),
        ),
        in_specs=[smem] + [vmem] * 18,
        out_specs=(vmem, vmem, vmem),
        scratch_shapes=[
            pltpu.VMEM((nrows + 6, 32, width), F32),
            pltpu.VMEM((nrows + 4, PITCH, width), F32),
            pltpu.VMEM((nrows + 4, 32, width), F32),
            pltpu.VMEM((nrows + 2, PITCH, width), F32),
            pltpu.VMEM((nrows + 2, PITCH, width), F32),
            pltpu.VMEM(((nrows + 4) * PITCH, 9 * width), BF16),
            pltpu.VMEM((depth, nrows, width), F32),
            pltpu.VMEM((width, hidden), F32),
            pltpu.VMEM((hidden, hidden), F32),
            pltpu.VMEM((LANES, hidden), F32),
            pltpu.VMEM((depth, ncols, width), F32),
        ],
        compiler_params=pltpu.CompilerParams(vmem_limit_bytes=VMEM_LIMIT),
        name="tile",
    )(
        flags,
        xy_noisy,
        above,
        below,
        before,
        after,
        labels,
        xz_same,
        xz_second,
        xz_above,
        xz_below,
        yz_cols,
        temb.reshape(1, width),
        flat_one,
        flat_two,
        back_flat,
        w1,
        w2,
        w3_wide,
    )

    def both(own, got):
        return (own.astype(F32) + got.astype(F32)).astype(BF16)

    low, high = dxz[:, :share], dxz[:, share:]
    keep = jnp.where(side == 0, low, high)
    give = jnp.where(side == 0, high, low)
    xz_sum = both(keep, grid.move(give, lambda i, j: (i, j ^ 1)))
    bit = 2
    while bit < grid.ny:
        xz_sum = both(xz_sum, grid.move(xz_sum, lambda i, j, bit=bit: (i, j ^ bit)))
        bit *= 2
    grad_xz = jnp.transpose(grid.move(xz_sum, grid.turned(0)), (1, 0, 2)).astype(F32)
    yz_sum = dyz
    bit = 1
    while bit < grid.nx:
        yz_sum = both(yz_sum, grid.move(yz_sum, lambda i, j, bit=bit: (i ^ bit, j)))
        bit *= 2
    yz_same = grid.move(yz_sum, grid.turned(0))
    yz_other = grid.move(yz_sum, grid.turned(1))
    grad_yz = jnp.where(
        side == 0,
        jnp.concatenate([yz_same, yz_other], axis=1),
        jnp.concatenate([yz_other, yz_same], axis=1),
    )
    grad_yz = jnp.transpose(grad_yz, (1, 0, 2)).astype(F32)

    core = grid.ix % 2
    packed = packed.reshape(2, chips, each, LANES)
    own = lax.dynamic_index_in_dim(packed, core, 0, keepdims=False)
    other = lax.dynamic_index_in_dim(packed, 1 - core, 0, keepdims=False)
    own = both(own, grid.move(other, lambda i, j: (i ^ 1, j)))
    groups = [
        [i * grid.ny + j for i in range(c, grid.nx, 2) for j in range(grid.ny)] for c in range(2)
    ]
    pieces = lax.all_to_all(own, BOTH, 0, 0, axis_index_groups=groups)
    total = jnp.sum(pieces.astype(F32), axis=0).astype(BF16)
    spread = jnp.broadcast_to(total[None], (chips, each, LANES))
    half = lax.all_to_all(spread, BOTH, 0, 0, axis_index_groups=groups)
    partner = grid.move(half, lambda i, j: (i ^ 1, j))
    g1, g2, gt, gw1, gw2, gw3 = pl.pallas_call(
        functools.partial(last_kernel, hidden, classes),
        out_shape=(
            jax.ShapeDtypeStruct((9, width, width), F32),
            jax.ShapeDtypeStruct((9, width, width), F32),
            jax.ShapeDtypeStruct((width, width), F32),
            jax.ShapeDtypeStruct((width, hidden), F32),
            jax.ShapeDtypeStruct((hidden, hidden), F32),
            jax.ShapeDtypeStruct((hidden, classes), F32),
        ),
        in_specs=[smem, vmem, vmem, vmem],
        out_specs=(vmem,) * 6,
        scratch_shapes=[pltpu.VMEM((2 * chips * each, LANES), BF16)],
        compiler_params=pltpu.CompilerParams(vmem_limit_bytes=VMEM_LIMIT),
        name="spread",
    )(
        core.reshape(1).astype(jnp.int32),
        half.reshape(chips * each, LANES),
        partner.reshape(chips * each, LANES),
        emb.reshape(width, 1),
    )
    shape = (3, 3, width, width)
    return (g1.reshape(shape), g2.reshape(shape), gt, gw1, gw2, gw3, grad_xz, grad_yz)


def solution(mesh):
    placed = (
        P("gx", "gy", None),
        P("gy", None, None),
        P("gx", None, None),
        P("gx", "gy", None),
        P(),
        P(),
        P(),
        P(),
        P(),
        P(),
        P(),
    )
    return jax.shard_map(
        local,
        mesh=mesh,
        in_specs=placed,
        out_specs=(P(), P(), P(), P(), P(), P(), P("gy", None, None), P("gx", None, None)),
        check_vma=False,
    )
```

time: 366 us -> 112 us (0.31)
  the two profiles are of different devices: /device:TPU:0 before, /device:TPU:3 now
where the time goes in v2:
time: 112 us; the launch traced here: 111 us
  starting transfers between devices  56.9 us (51%)
  waiting for transfers between devices  25.4 us (23%)
  Pallas kernels  18 us (16%)
  local copies, waits for them, and re-layouts  7.39 us (7%)
  between operations  1.82 us (2%)
  other arithmetic  1.38 us (1%)
    ppermute x18, starting transfers between devices, move(): return lax.ppermute(array, BOTH, pairs)  47.3 us
    pallas_call x1, Pallas kernels, local(): pl.pallas_call(functools.partial(main_kernel, classes), out_shape=(jax.Sh...  16.8 us
    ppermute x18, waiting for transfers between devices, move(): return lax.ppermute(array, BOTH, pairs)  16.7 us
    all_to_all x1, waiting for transfers between devices, local(): pieces = lax.all_to_all(own, BOTH, 0, 0, axis_index_groups=groups)  8.75 us
    unnamed x29, local copies, waits for them, and re-layouts  5.03 us
    all_to_all x1, starting transfers between devices, local(): pieces = lax.all_to_all(own, BOTH, 0, 0, axis_index_groups=groups)  4.98 us
    all_to_all x1, starting transfers between devices, local(): half = lax.all_to_all(spread, BOTH, 0, 0, axis_index_groups=groups)  4.67 us
  transfers between devices with their start and end apart: 20, of which 7 were waited for; matrix products, arithmetic and copies ran while one was open for 4% of the time, Pallas kernels for 0%

profile of v2, /device:TPU:3, one launch (start us, length us, event | category | flops | bytes accessed | tf_op | source)
XLA Modules:
  0.0 111.1 jit_solution(3918917067258679902)
XLA Ops:
  1.4 0.3 copy-done
  1.8 4.9 %collective-permute-start.5 = (bf16[4,32,128]{2,1,0:T(8,128)(2,1)S(1)}, bf16[4,32,128]{2,1,0:T(8,128)(2,1)S(1)}, u32[]{:S(2)}, u32[]{:S(2)}) collective-permute-start(bf16[4,32,128]{2,1,0:T(8,128)(2,1)S(1)} %bitcast.49), channel_id=1, source_target_pairs={{0,1},{1,0},{2,9},{3,8},{4,17},{5,16},{6,25},{7,24},{8,3},{9,2},{1... | collective-permute-start | bytes 98312 | tf_op jit(solution)/shard_map/ppermute | solution.py:63
  6.6 0.7 collective-permute-start.7
  7.3 1.3 %collective-permute-start.6 = (bf16[4,1,128]{2,1,0:T(2,128)(2,1)S(1)}, bf16[4,1,128]{2,1,0:T(2,128)(2,1)S(1)}, u32[]{:S(2)}, u32[]{:S(2)}) collective-permute-start(bf16[4,1,128]{2,1,0:T(2,128)(2,1)S(1)} %broadcast_select_fusion.3), channel_id=1, source_target_pairs={{1,8},{2,1},{3,16},{4,9},{5,24},{6,17},{9,10},{10,3},{11,18},{12,1... | collective-permute-start | bytes 3080 | tf_op jit(solution)/shard_map/ppermute | solution.py:63
  8.6 0.3 copy.19.labels
  9.0 0.9 copy-done.2
  9.9 1.4 %collective-permute-start = (bf16[4,16,128]{2,1,0:T(8,128)(2,1)S(1)}, bf16[4,16,128]{2,1,0:T(8,128)(2,1)S(1)}, u32[]{:S(2)}, u32[]{:S(2)}) collective-permute-start(bf16[4,16,128]{2,1,0:T(8,128)(2,1)S(1)} %fusion.3), channel_id=1, source_target_pairs={{0,8},{1,9},{2,10},{3,11},{4,12},{5,13},{6,14},{7,15},{8,16},{9,17... | collective-permute-start | bytes 49160 | tf_op jit(solution)/shard_map/ppermute | solution.py:63
  11.4 3.0 %collective-permute-start.1 = (bf16[4,16,128]{2,1,0:T(8,128)(2,1)S(1)}, bf16[4,16,128]{2,1,0:T(8,128)(2,1)S(1)}, u32[]{:S(2)}, u32[]{:S(2)}) collective-permute-start(bf16[4,16,128]{2,1,0:T(8,128)(2,1)S(1)} %fusion.4), channel_id=1, source_target_pairs={{8,0},{9,1},{10,2},{11,3},{12,4},{13,5},{14,6},{15,7},{16,8},{17,9... | collective-permute-start | bytes 49160 | tf_op jit(solution)/shard_map/ppermute | solution.py:63
  14.5 0.9 constant_dynamic-slice_fusion.1
  15.6 0.6 copy-done.7
  16.3 0.1 fusion.13.temb
  16.4 0.2 copy.22
  16.6 0.5 copy-done.8
  17.1 0.1 copy.23
  17.3 0.1 stack.23.place
  17.4 6.8 %collective-permute-start.2 = (bf16[4,48,128]{2,1,0:T(8,128)(2,1)S(1)}, bf16[4,48,128]{2,1,0:T(8,128)(2,1)S(1)}, u32[]{:S(2)}, u32[]{:S(2)}) collective-permute-start(bf16[4,48,128]{2,1,0:T(8,128)(2,1)S(1)} %pad_maximum_fusion.2), channel_id=1, source_target_pairs={{0,0},{1,1},{2,8},{3,9},{4,16},{5,17},{6,24},{7,25},{8,2},{9,3},{1... | collective-permute-start | bytes 147464 | tf_op jit(solution)/shard_map/ppermute | solution.py:63
  24.2 1.9 %collective-permute-done.2 = bf16[4,48,128]{2,1,0:T(8,128)(2,1)S(1)} collective-permute-done((bf16[4,48,128]{2,1,0:T(8,128)(2,1)S(1)}, bf16[4,48,128]{2,1,0:T(8,128)(2,1)S(1)}, u32[]{:S(2)}, u32[]{:S(2)}) %collective-permute-start.2) | collective-permute-done | bytes 49184 | tf_op jit(solution)/shard_map/ppermute | solution.py:63
  26.1 0.1 pad_dynamic-update-slice_fusion
  26.3 0.1 pad_maximum_fusion
  26.4 6.3 %collective-permute-start.3 = (bf16[70,4,128]{2,1,0:T(4,128)(2,1)S(1)}, bf16[70,4,128]{2,1,0:T(4,128)(2,1)S(1)}, u32[]{:S(2)}, u32[]{:S(2)}) collective-permute-start(bf16[70,4,128]{2,1,0:T(4,128)(2,1)S(1)} %pad_maximum_fusion), channel_id=1, source_target_pairs={{0,1},{1,2},{2,3},{3,4},{4,5},{5,6},{6,7},{8,9},{9,10},{10,11},{11... | collective-permute-start | bytes 215048 | tf_op jit(solution)/shard_map/ppermute | solution.py:63
  32.7 0.1 pad_maximum_fusion.1
  32.8 1.4 %collective-permute-start.4 = (bf16[70,4,128]{2,1,0:T(4,128)(2,1)S(1)}, bf16[70,4,128]{2,1,0:T(4,128)(2,1)S(1)}, u32[]{:S(2)}, u32[]{:S(2)}) collective-permute-start(bf16[70,4,128]{2,1,0:T(4,128)(2,1)S(1)} %pad_maximum_fusion.1), channel_id=1, source_target_pairs={{1,0},{2,1},{3,2},{4,3},{5,4},{6,5},{7,6},{9,8},{10,9},{11,10},{12... | collective-permute-start | bytes 215048 | tf_op jit(solution)/shard_map/ppermute | solution.py:63
  34.3 0.2 collective-permute-done.3.before
  34.5 3.9 %collective-permute-done.4.after = bf16[70,4,128]{2,1,0:T(4,128)(2,1)S(1)} collective-permute-done((bf16[70,4,128]{2,1,0:T(4,128)(2,1)S(1)}, bf16[70,4,128]{2,1,0:T(4,128)(2,1)S(1)}, u32[]{:S(2)}, u32[]{:S(2)}) %collective-permute-start.4) | collective-permute-done | bytes 71712 | tf_op jit(solution)/shard_map/ppermute | solution.py:63
  38.5 16.8 %tile.1 = (bf16[3328,128]{1,0:T(8,128)(2,1)S(1)}, bf16[4,64,128]{2,1,0:T(8,128)(2,1)S(1)}, bf16[4,16,128]{2,1,0:T(8,128)(2,1)S(1)}) custom-call(s32[5]{0:T(128)S(1)} %stack.23.place, bf16[64,16,128]{2,1,0:T(8,128)(2,1)S(1)} %copy-done.2, bf16[4,16,128]{2,1,0:T(8,128)(2,1)S(1)} %collective-permute-done.above, ...), custom_call_target="tpu_custom_call" | custom-call | tf_op jit(solution)/shard_map/tile/pallas_call | solution.py:398
  55.3 1.1 collective-permute-start.8
  56.3 1.4 %collective-permute-done.8 = bf16[16,104,128]{2,1,0:T(8,128)(2,1)S(1)} collective-permute-done((bf16[16,104,128]{2,1,0:T(8,128)(2,1)S(1)}, bf16[16,104,128]{2,1,0:T(8,128)(2,1)S(1)}, u32[]{:S(2)}, u32[]{:S(2)}) %collective-permute-start.8) | collective-permute-done | bytes 426016 | tf_op jit(solution)/shard_map/ppermute | solution.py:63
  57.7 0.9 fusion
  58.6 5.0 %all-to-all-start = ((bf16[16,104,128]{2,1,0:T(8,128)(2,1)}), bf16[16,104,128]{2,1,0:T(8,128)(2,1)S(1)}, u32[]{:S(2)}, u32[]{:S(2)}) async-start(bf16[16,104,128]{2,1,0:T(8,128)(2,1)} %fusion), calls=%async_computation | async-start | bytes 851968 | tf_op jit(solution)/shard_map/all_to_all | solution.py:478
  63.6 1.2 %collective-permute-start.10 = (bf16[4,32,128]{2,1,0:T(8,128)(2,1)S(1)}, bf16[4,32,128]{2,1,0:T(8,128)(2,1)S(1)}, u32[]{:S(2)}, u32[]{:S(2)}) collective-permute-start(bf16[4,32,128]{2,1,0:T(8,128)(2,1)S(1)} %broadcast_select_fusion), channel_id=1, source_target_pairs={{0,1},{1,0},{2,3},{3,2},{4,5},{5,4},{6,7},{7,6},{8,9},{9,8},{10,11... | collective-permute-start | bytes 98312 | tf_op jit(solution)/shard_map/ppermute | solution.py:63
  64.8 0.1 copy.25.emb
  64.9 1.3 %collective-permute-start.14 = (bf16[4,16,128]{2,1,0:T(8,128)(2,1)S(1)}, bf16[4,16,128]{2,1,0:T(8,128)(2,1)S(1)}, u32[]{:S(2)}, u32[]{:S(2)}) collective-permute-start(bf16[4,16,128]{2,1,0:T(8,128)(2,1)S(1)} %get-tuple-element.25), channel_id=1, source_target_pairs={{0,8},{1,9},{2,10},{3,11},{4,12},{5,13},{6,14},{7,15},{8,0},{9,1},... | collective-permute-start | bytes 49160 | tf_op jit(solution)/shard_map/ppermute | solution.py:63
  66.2 8.7 %all-to-all-done = bf16[16,104,128]{2,1,0:T(8,128)(2,1)S(1)} async-done(((bf16[16,104,128]{2,1,0:T(8,128)(2,1)}), bf16[16,104,128]{2,1,0:T(8,128)(2,1)S(1)}, u32[]{:S(2)}, u32[]{:S(2)}) %all-to-all-start) | async-done | bytes 426016 | tf_op jit(solution)/shard_map/all_to_all | solution.py:478
  75.0 0.8 broadcast_in_dim.2
  75.8 4.7 %all-to-all-start.1 = ((bf16[16,104,128]{2,1,0:T(8,128)(2,1)}), bf16[16,104,128]{2,1,0:T(8,128)(2,1)S(1)}, u32[]{:S(2)}, u32[]{:S(2)}) async-start(bf16[16,104,128]{2,1,0:T(8,128)(2,1)} %broadcast_in_dim.2), calls=%async_computation.1 | async-start | bytes 851968 | tf_op jit(solution)/shard_map/all_to_all | solution.py:481
  80.5 1.2 %collective-permute-start.11 = (bf16[4,32,128]{2,1,0:T(8,128)(2,1)S(1)}, bf16[4,32,128]{2,1,0:T(8,128)(2,1)S(1)}, u32[]{:S(2)}, u32[]{:S(2)}) collective-permute-start(bf16[4,32,128]{2,1,0:T(8,128)(2,1)S(1)} %add_convert_fusion.2), channel_id=1, source_target_pairs={{0,2},{1,3},{2,0},{3,1},{4,6},{5,7},{6,4},{7,5},{8,10},{9,11},{10,... | collective-permute-start | bytes 98312 | tf_op jit(solution)/shard_map/ppermute | solution.py:63
  81.8 0.3 collective-permute-start.15
  82.2 4.5 %collective-permute-done.11 = bf16[4,32,128]{2,1,0:T(8,128)(2,1)S(1)} collective-permute-done((bf16[4,32,128]{2,1,0:T(8,128)(2,1)S(1)}, bf16[4,32,128]{2,1,0:T(8,128)(2,1)S(1)}, u32[]{:S(2)}, u32[]{:S(2)}) %collective-permute-start.11) | collective-permute-done | bytes 32800 | tf_op jit(solution)/shard_map/ppermute | solution.py:63
  86.6 4.0 %collective-permute-start.12 = (bf16[4,32,128]{2,1,0:T(8,128)(2,1)S(1)}, bf16[4,32,128]{2,1,0:T(8,128)(2,1)S(1)}, u32[]{:S(2)}, u32[]{:S(2)}) collective-permute-start(bf16[4,32,128]{2,1,0:T(8,128)(2,1)S(1)} %add_convert_fusion.1), channel_id=1, source_target_pairs={{0,4},{1,5},{2,6},{3,7},{4,0},{5,1},{6,2},{7,3},{8,12},{9,13},{10,... | collective-permute-start | bytes 98312 | tf_op jit(solution)/shard_map/ppermute | solution.py:63
  90.7 4.0 %collective-permute-start.17 = (bf16[4,16,128]{2,1,0:T(8,128)(2,1)S(1)}, bf16[4,16,128]{2,1,0:T(8,128)(2,1)S(1)}, u32[]{:S(2)}, u32[]{:S(2)}) collective-permute-start(bf16[4,16,128]{2,1,0:T(8,128)(2,1)S(1)} %add_convert_fusion.3), channel_id=1, source_target_pairs={{0,1},{1,0},{2,9},{3,8},{4,17},{5,16},{6,25},{7,24},{8,3},{9,2},{1... | collective-permute-start | bytes 49160 | tf_op jit(solution)/shard_map/ppermute | solution.py:63
  94.7 3.3 %collective-permute-start.16 = (bf16[4,16,128]{2,1,0:T(8,128)(2,1)S(1)}, bf16[4,16,128]{2,1,0:T(8,128)(2,1)S(1)}, u32[]{:S(2)}, u32[]{:S(2)}) collective-permute-start(bf16[4,16,128]{2,1,0:T(8,128)(2,1)S(1)} %add_convert_fusion.3), channel_id=1, source_target_pairs={{0,0},{1,1},{2,8},{3,9},{4,16},{5,17},{6,24},{7,25},{8,2},{9,3},{1... | collective-permute-start | bytes 49160 | tf_op jit(solution)/shard_map/ppermute | solution.py:63
  98.0 2.5 %collective-permute-start.9 = (bf16[16,104,128]{2,1,0:T(8,128)(2,1)S(1)}, bf16[16,104,128]{2,1,0:T(8,128)(2,1)S(1)}, u32[]{:S(2)}, u32[]{:S(2)}) collective-permute-start(bf16[16,104,128]{2,1,0:T(8,128)(2,1)S(1)} %all-to-all-done.1), channel_id=1, source_target_pairs={{0,8},{1,9},{2,10},{3,11},{4,12},{5,13},{6,14},{7,15},{8,0},{9,1},... | collective-permute-start | bytes 1277960 | tf_op jit(solution)/shard_map/ppermute | solution.py:63
  100.5 2.5 %collective-permute-start.13 = (bf16[4,32,128]{2,1,0:T(8,128)(2,1)S(1)}, bf16[4,32,128]{2,1,0:T(8,128)(2,1)S(1)}, u32[]{:S(2)}, u32[]{:S(2)}) collective-permute-start(bf16[4,32,128]{2,1,0:T(8,128)(2,1)S(1)} %add_convert_fusion), channel_id=1, source_target_pairs={{0,0},{1,1},{2,8},{3,9},{4,16},{5,17},{6,24},{7,25},{8,2},{9,3},{1... | collective-permute-start | bytes 98312 | tf_op jit(solution)/shard_map/ppermute | solution.py:63
  103.1 0.7 copy.28
  103.8 4.7 %collective-permute-done.13 = bf16[4,32,128]{2,1,0:T(8,128)(2,1)S(1)} collective-permute-done((bf16[4,32,128]{2,1,0:T(8,128)(2,1)S(1)}, bf16[4,32,128]{2,1,0:T(8,128)(2,1)S(1)}, u32[]{:S(2)}, u32[]{:S(2)}) %collective-permute-start.13) | collective-permute-done | bytes 32800 | tf_op jit(solution)/shard_map/ppermute | solution.py:63
  108.5 0.7 copy.27
  109.1 1.3 %spread.1 = (f32[9,128,128]{2,1,0:T(8,128)}, f32[9,128,128]{2,1,0:T(8,128)}, f32[128,128]{1,0:T(8,128)}, f32[128,256]{1,0:T(8,128)}, f32[256,256]{1,0:T(8,128)}, /*index=5*/f32[256,20]{1,0:T(8,128)S(1)}) custom-call(s32[1]{0:T(128)} %bitcast.place, bf16[1664,128]{1,0:T(8,128)(2,1)S(1)} %bitcast.42, bf16[1664,128]{1,0:T(8,128)(2,1)S(1)} %bitcast.47, ...), custom_call_target="tpu_custom_call" | custom-call | tf_op jit(solution)/shard_map/spread/pallas_call | solution.py:483
  110.4 0.7 copy.26
  (62 shorter events, 0.7 us)
Async XLA Ops:
  0.6 1.1 copy-start
  1.7 6.9 %copy-start.6 = (s32[64,16,4]{0,2,1:T(4,128)S(1)}, s32[64,16,4]{0,2,1:T(4,128)}, u32[]{:S(2)}) copy-start(s32[64,16,4]{0,2,1:T(4,128)} %param.14) | copy-start | bytes 49156
  1.8 32.5 %collective-permute-start.5 = (bf16[4,32,128]{2,1,0:T(8,128)(2,1)S(1)}, bf16[4,32,128]{2,1,0:T(8,128)(2,1)S(1)}, u32[]{:S(2)}, u32[]{:S(2)}) collective-permute-start(bf16[4,32,128]{2,1,0:T(8,128)(2,1)S(1)} %bitcast.49), channel_id=1, source_target_pairs={{0,1},{1,0},{2,9},{3,8},{4,17},{5,16},{6,25},{7,24},{8,3},{9,2},{1... | collective-permute-start | bytes 98312 | tf_op jit(solution)/shard_map/ppermute | solution.py:63
  6.6 27.6 %collective-permute-start.7 = (bf16[4,1,128]{2,1,0:T(2,128)(2,1)S(1)}, bf16[4,1,128]{2,1,0:T(2,128)(2,1)S(1)}, u32[]{:S(2)}, u32[]{:S(2)}) collective-permute-start(bf16[4,1,128]{2,1,0:T(2,128)(2,1)S(1)} %broadcast_select_fusion.3), channel_id=1, source_target_pairs={{1,9},{2,0},{3,17},{4,8},{5,25},{6,16},{9,11},{10,2},{11,19},{12,1... | collective-permute-start | bytes 3080 | tf_op jit(solution)/shard_map/ppermute | solution.py:63
  7.3 26.9 %collective-permute-start.6 = (bf16[4,1,128]{2,1,0:T(2,128)(2,1)S(1)}, bf16[4,1,128]{2,1,0:T(2,128)(2,1)S(1)}, u32[]{:S(2)}, u32[]{:S(2)}) collective-permute-start(bf16[4,1,128]{2,1,0:T(2,128)(2,1)S(1)} %broadcast_select_fusion.3), channel_id=1, source_target_pairs={{1,8},{2,1},{3,16},{4,9},{5,24},{6,17},{9,10},{10,3},{11,18},{12,1... | collective-permute-start | bytes 3080 | tf_op jit(solution)/shard_map/ppermute | solution.py:63
  8.9 1.0 copy-start.2
  9.9 5.6 %copy-start.1 = (bf16[3,3,128,128]{3,2,1,0:T(8,128)(2,1)S(1)}, bf16[3,3,128,128]{3,2,1,0:T(8,128)(2,1)}, u32[]{:S(2)}) copy-start(bf16[3,3,128,128]{3,2,1,0:T(8,128)(2,1)} %param.17) | copy-start | bytes 884740
  9.9 14.3 %collective-permute-start = (bf16[4,16,128]{2,1,0:T(8,128)(2,1)S(1)}, bf16[4,16,128]{2,1,0:T(8,128)(2,1)S(1)}, u32[]{:S(2)}, u32[]{:S(2)}) collective-permute-start(bf16[4,16,128]{2,1,0:T(8,128)(2,1)S(1)} %fusion.3), channel_id=1, source_target_pairs={{0,8},{1,9},{2,10},{3,11},{4,12},{5,13},{6,14},{7,15},{8,16},{9,17... | collective-permute-start | bytes 49160 | tf_op jit(solution)/shard_map/ppermute | solution.py:63
  11.4 6.0 %collective-permute-start.1 = (bf16[4,16,128]{2,1,0:T(8,128)(2,1)S(1)}, bf16[4,16,128]{2,1,0:T(8,128)(2,1)S(1)}, u32[]{:S(2)}, u32[]{:S(2)}) collective-permute-start(bf16[4,16,128]{2,1,0:T(8,128)(2,1)S(1)} %fusion.4), channel_id=1, source_target_pairs={{8,0},{9,1},{10,2},{11,3},{12,4},{13,5},{14,6},{15,7},{16,8},{17,9... | collective-permute-start | bytes 49160 | tf_op jit(solution)/shard_map/ppermute | solution.py:63
  15.5 0.8 copy-start.7
  16.4 0.7 copy-start.8
  17.4 8.7 %collective-permute-start.2 = (bf16[4,48,128]{2,1,0:T(8,128)(2,1)S(1)}, bf16[4,48,128]{2,1,0:T(8,128)(2,1)S(1)}, u32[]{:S(2)}, u32[]{:S(2)}) collective-permute-start(bf16[4,48,128]{2,1,0:T(8,128)(2,1)S(1)} %pad_maximum_fusion.2), channel_id=1, source_target_pairs={{0,0},{1,1},{2,8},{3,9},{4,16},{5,17},{6,24},{7,25},{8,2},{9,3},{1... | collective-permute-start | bytes 147464 | tf_op jit(solution)/shard_map/ppermute | solution.py:63
  26.1 12.3 %copy-start.3 = (bf16[3,3,128,128]{3,2,1,0:T(8,128)(2,1)S(1)}, bf16[3,3,128,128]{3,2,1,0:T(8,128)(2,1)}, u32[]{:S(2)}) copy-start(bf16[3,3,128,128]{3,2,1,0:T(8,128)(2,1)} %param.16) | copy-start | bytes 884740
  26.4 8.2 %collective-permute-start.3 = (bf16[70,4,128]{2,1,0:T(4,128)(2,1)S(1)}, bf16[70,4,128]{2,1,0:T(4,128)(2,1)S(1)}, u32[]{:S(2)}, u32[]{:S(2)}) collective-permute-start(bf16[70,4,128]{2,1,0:T(4,128)(2,1)S(1)} %pad_maximum_fusion), channel_id=1, source_target_pairs={{0,1},{1,2},{2,3},{3,4},{4,5},{5,6},{6,7},{8,9},{9,10},{10,11},{11... | collective-permute-start | bytes 215048 | tf_op jit(solution)/shard_map/ppermute | solution.py:63
  32.6 5.8 %copy-start.4 = (bf16[256,256]{1,0:T(8,128)(2,1)S(1)}, bf16[256,256]{1,0:T(8,128)(2,1)}, u32[]{:S(2)}) copy-start(bf16[256,256]{1,0:T(8,128)(2,1)} %w2.1) | copy-start | bytes 393220
  32.7 5.7 %copy-start.5 = (bf16[128,256]{1,0:T(8,128)(2,1)S(1)}, bf16[128,256]{1,0:T(8,128)(2,1)}, u32[]{:S(2)}) copy-start(bf16[128,256]{1,0:T(8,128)(2,1)} %w1.1) | copy-start | bytes 196612
  32.8 5.7 %collective-permute-start.4 = (bf16[70,4,128]{2,1,0:T(4,128)(2,1)S(1)}, bf16[70,4,128]{2,1,0:T(4,128)(2,1)S(1)}, u32[]{:S(2)}, u32[]{:S(2)}) collective-permute-start(bf16[70,4,128]{2,1,0:T(4,128)(2,1)S(1)} %pad_maximum_fusion.1), channel_id=1, source_target_pairs={{1,0},{2,1},{3,2},{4,3},{5,4},{6,5},{7,6},{9,8},{10,9},{11,10},{12... | collective-permute-start | bytes 215048 | tf_op jit(solution)/shard_map/ppermute | solution.py:63
  55.3 2.4 %collective-permute-start.8 = (bf16[16,104,128]{2,1,0:T(8,128)(2,1)S(1)}, bf16[16,104,128]{2,1,0:T(8,128)(2,1)S(1)}, u32[]{:S(2)}, u32[]{:S(2)}) collective-permute-start(bf16[16,104,128]{2,1,0:T(8,128)(2,1)S(1)} %dynamic-slice_bitcast_fusion), channel_id=1, source_target_pairs={{0,8},{1,9},{2,10},{3,11},{4,12},{5,13},{6,14},{7,15},{8,0},{9,1},... | collective-permute-start | bytes 1277960 | tf_op jit(solution)/shard_map/ppermute | solution.py:63
  58.6 16.4 %all-to-all-start = ((bf16[16,104,128]{2,1,0:T(8,128)(2,1)}), bf16[16,104,128]{2,1,0:T(8,128)(2,1)S(1)}, u32[]{:S(2)}, u32[]{:S(2)}) async-start(bf16[16,104,128]{2,1,0:T(8,128)(2,1)} %fusion), calls=%async_computation | async-start | bytes 851968 | tf_op jit(solution)/shard_map/all_to_all | solution.py:478
  63.6 16.9 %collective-permute-start.10 = (bf16[4,32,128]{2,1,0:T(8,128)(2,1)S(1)}, bf16[4,32,128]{2,1,0:T(8,128)(2,1)S(1)}, u32[]{:S(2)}, u32[]{:S(2)}) collective-permute-start(bf16[4,32,128]{2,1,0:T(8,128)(2,1)S(1)} %broadcast_select_fusion), channel_id=1, source_target_pairs={{0,1},{1,0},{2,3},{3,2},{4,5},{5,4},{6,7},{7,6},{8,9},{9,8},{10,11... | collective-permute-start | bytes 98312 | tf_op jit(solution)/shard_map/ppermute | solution.py:63
  64.9 16.9 %collective-permute-start.14 = (bf16[4,16,128]{2,1,0:T(8,128)(2,1)S(1)}, bf16[4,16,128]{2,1,0:T(8,128)(2,1)S(1)}, u32[]{:S(2)}, u32[]{:S(2)}) collective-permute-start(bf16[4,16,128]{2,1,0:T(8,128)(2,1)S(1)} %get-tuple-element.25), channel_id=1, source_target_pairs={{0,8},{1,9},{2,10},{3,11},{4,12},{5,13},{6,14},{7,15},{8,0},{9,1},... | collective-permute-start | bytes 49160 | tf_op jit(solution)/shard_map/ppermute | solution.py:63
  75.8 22.2 %all-to-all-start.1 = ((bf16[16,104,128]{2,1,0:T(8,128)(2,1)}), bf16[16,104,128]{2,1,0:T(8,128)(2,1)S(1)}, u32[]{:S(2)}, u32[]{:S(2)}) async-start(bf16[16,104,128]{2,1,0:T(8,128)(2,1)} %broadcast_in_dim.2), calls=%async_computation.1 | async-start | bytes 851968 | tf_op jit(solution)/shard_map/all_to_all | solution.py:481
  80.5 6.1 %collective-permute-start.11 = (bf16[4,32,128]{2,1,0:T(8,128)(2,1)S(1)}, bf16[4,32,128]{2,1,0:T(8,128)(2,1)S(1)}, u32[]{:S(2)}, u32[]{:S(2)}) collective-permute-start(bf16[4,32,128]{2,1,0:T(8,128)(2,1)S(1)} %add_convert_fusion.2), channel_id=1, source_target_pairs={{0,2},{1,3},{2,0},{3,1},{4,6},{5,7},{6,4},{7,5},{8,10},{9,11},{10,... | collective-permute-start | bytes 98312 | tf_op jit(solution)/shard_map/ppermute | solution.py:63
  81.8 8.9 %collective-permute-start.15 = (bf16[4,16,128]{2,1,0:T(8,128)(2,1)S(1)}, bf16[4,16,128]{2,1,0:T(8,128)(2,1)S(1)}, u32[]{:S(2)}, u32[]{:S(2)}) collective-permute-start(bf16[4,16,128]{2,1,0:T(8,128)(2,1)S(1)} %add_convert_fusion.4), channel_id=1, source_target_pairs={{0,16},{1,17},{2,18},{3,19},{4,20},{5,21},{6,22},{7,23},{8,24},{9,... | collective-permute-start | bytes 49160 | tf_op jit(solution)/shard_map/ppermute | solution.py:63
  86.6 13.9 %collective-permute-start.12 = (bf16[4,32,128]{2,1,0:T(8,128)(2,1)S(1)}, bf16[4,32,128]{2,1,0:T(8,128)(2,1)S(1)}, u32[]{:S(2)}, u32[]{:S(2)}) collective-permute-start(bf16[4,32,128]{2,1,0:T(8,128)(2,1)S(1)} %add_convert_fusion.1), channel_id=1, source_target_pairs={{0,4},{1,5},{2,6},{3,7},{4,0},{5,1},{6,2},{7,3},{8,12},{9,13},{10,... | collective-permute-start | bytes 98312 | tf_op jit(solution)/shard_map/ppermute | solution.py:63
  90.7 12.4 %collective-permute-start.17 = (bf16[4,16,128]{2,1,0:T(8,128)(2,1)S(1)}, bf16[4,16,128]{2,1,0:T(8,128)(2,1)S(1)}, u32[]{:S(2)}, u32[]{:S(2)}) collective-permute-start(bf16[4,16,128]{2,1,0:T(8,128)(2,1)S(1)} %add_convert_fusion.3), channel_id=1, source_target_pairs={{0,1},{1,0},{2,9},{3,8},{4,17},{5,16},{6,25},{7,24},{8,3},{9,2},{1... | collective-permute-start | bytes 49160 | tf_op jit(solution)/shard_map/ppermute | solution.py:63
  94.7 8.4 %collective-permute-start.16 = (bf16[4,16,128]{2,1,0:T(8,128)(2,1)S(1)}, bf16[4,16,128]{2,1,0:T(8,128)(2,1)S(1)}, u32[]{:S(2)}, u32[]{:S(2)}) collective-permute-start(bf16[4,16,128]{2,1,0:T(8,128)(2,1)S(1)} %add_convert_fusion.3), channel_id=1, source_target_pairs={{0,0},{1,1},{2,8},{3,9},{4,16},{5,17},{6,24},{7,25},{8,2},{9,3},{1... | collective-permute-start | bytes 49160 | tf_op jit(solution)/shard_map/ppermute | solution.py:63
  98.0 11.1 %collective-permute-start.9 = (bf16[16,104,128]{2,1,0:T(8,128)(2,1)S(1)}, bf16[16,104,128]{2,1,0:T(8,128)(2,1)S(1)}, u32[]{:S(2)}, u32[]{:S(2)}) collective-permute-start(bf16[16,104,128]{2,1,0:T(8,128)(2,1)S(1)} %all-to-all-done.1), channel_id=1, source_target_pairs={{0,8},{1,9},{2,10},{3,11},{4,12},{5,13},{6,14},{7,15},{8,0},{9,1},... | collective-permute-start | bytes 1277960 | tf_op jit(solution)/shard_map/ppermute | solution.py:63
  100.5 7.9 %collective-permute-start.13 = (bf16[4,32,128]{2,1,0:T(8,128)(2,1)S(1)}, bf16[4,32,128]{2,1,0:T(8,128)(2,1)S(1)}, u32[]{:S(2)}, u32[]{:S(2)}) collective-permute-start(bf16[4,32,128]{2,1,0:T(8,128)(2,1)S(1)} %add_convert_fusion), channel_id=1, source_target_pairs={{0,0},{1,1},{2,8},{3,9},{4,16},{5,17},{6,24},{7,25},{8,2},{9,3},{1... | collective-permute-start | bytes 98312 | tf_op jit(solution)/shard_map/ppermute | solution.py:63

commit v3 on v2

v3 whole, which is shorter than its diff:
```python
import functools
import math

import jax
import jax.numpy as jnp
from jax import lax
from jax.experimental import pallas as pl
from jax.experimental.pallas import tpu as pltpu
from jax.sharding import PartitionSpec as P

loss_weight = 1.0 / 256.0
BOTH = ("gx", "gy")
LANES = 128
PITCH = 24
REACH = 3
CLASS_ROWS = 32
F32, BF16 = jnp.float32, jnp.bfloat16
VMEM_LIMIT = 48 * 1024 * 1024


def sigmoid(value):
    return 0.5 * jnp.tanh(0.5 * value) + 0.5


def silu_pair(value):
    sig = sigmoid(value)
    out = value * sig
    return out, sig + out - out * sig


def dot(a, b):
    return jnp.dot(a, b, preferred_element_type=F32)


def dot_nt(a, b):
    return lax.dot_general(a, b, (((1,), (1,)), ((), ())), preferred_element_type=F32)


def dot_tn(a, b):
    return lax.dot_general(a, b, (((0,), (0,)), ((), ())), preferred_element_type=F32)


def time_embedding(timestep, width):
    half = width // 2
    freqs = jnp.exp(-math.log(10000.0) * jnp.arange(half, dtype=jnp.float32) / half)
    angle = timestep.astype(jnp.float32)[0] * freqs
    return jnp.concatenate([jnp.cos(angle), jnp.sin(angle)])


class Grid:
    def __init__(self):
        self.nx, self.ny = lax.axis_size("gx"), lax.axis_size("gy")
        self.count = self.ny // self.nx
        self.ix, self.iy = lax.axis_index("gx"), lax.axis_index("gy")

    def move(self, array, target):
        pairs = []
        for i in range(self.nx):
            for j in range(self.ny):
                k, m = target(i, j)
                if 0 <= k < self.nx and 0 <= m < self.ny:
                    pairs.append((i * self.ny + j, k * self.ny + m))
        return lax.ppermute(array, BOTH, pairs)

    def turned(self, shift):
        count = self.count
        return lambda i, j: (j // count, count * i + (j % count + shift) % count)


class Shares:
    def __init__(self, chips, nrows, ncols, depth, width, hidden):
        sizes = (("conv1", 9 * width), ("conv2", 9 * width), ("w1", width * hidden // LANES), ("w2", hidden * hidden // LANES))
        self.at, total = {}, 0
        for name, rows in sizes:
            self.at[name] = total
            total += rows
        self.chips = chips
        self.each = -(-total // (2 * chips * 8)) * 8
        self.xz_rows = nrows * depth // chips
        self.yz_rows = max(1, ncols * depth // 2 // chips)
        self.yz_shares = ncols * depth // 2 // self.yz_rows
        self.xz = self.each
        self.small = self.xz + -(-self.xz_rows // 8) * 8
        self.yz = self.small + 2
        self.rows = -(-(self.yz + 4 * self.yz_rows) // 16) * 16

    def split(self, start, rows):
        done = 0
        while done < rows:
            share, row = divmod(start + done, self.each)
            step = min(rows - done, self.each - row)
            yield share // self.chips, share % self.chips, row, done, step
            done += step


def main_kernel(
    classes,
    shares,
    place,
    xy,
    above,
    below,
    before,
    after,
    labels,
    first,
    rim_row,
    temb,
    conv1,
    conv2,
    back,
    w1,
    w2,
    w3,
    own_out,
    other_out,
    xs,
    hs,
    acts,
    xyds,
    dx,
    patch,
    xzs,
    yzs,
    dw1,
    dw2,
    dw3,
    dxz,
    dyz,
    flat,
    packed,
):
    nrows, ncols, width = xy.shape
    depth = labels.shape[2]
    hidden = w1.shape[1]
    share = nrows // 2
    side, core = place[0], place[5]
    open_up, open_down, open_left, open_right = (place[1] > 0, place[2] > 0, place[3] > 0, place[4] > 0)
    tall = nrows + 2 * REACH

    mid_r, mid_c = slice(REACH, REACH + nrows), slice(REACH, REACH + ncols)
    xs[...] = jnp.zeros_like(xs)
    xs[mid_r, mid_c] = xy[...].astype(F32)
    xs[0:REACH, mid_c] = above[0:REACH].astype(F32)
    xs[REACH + nrows : 2 * REACH + nrows, mid_c] = below[0:REACH].astype(F32)
    xs[:, 0:REACH] = before[0:tall].astype(F32)[:, 0:REACH]
    xs[:, REACH + ncols : 2 * REACH + ncols] = after[0:tall].astype(F32)[:, 0:REACH]

    def gather(source, row, col, rows, cols):
        count = rows * cols
        for a in range(3):
            for b in range(3):
                piece = source[row + a : row + a + rows, col + b : col + b + cols, :]
                tap = (3 * a + b) * width
                patch[0:count, tap : tap + width] = piece.reshape(count, width).astype(BF16)
        return count

    n1 = gather(xs, 0, 0, nrows + 4, PITCH)
    h1 = dot(patch[0:n1], conv1[...]) + temb[...]
    h1 = h1.reshape(nrows + 4, PITCH, width)
    hs[...] = h1
    row = lax.broadcasted_iota(jnp.int32, h1.shape, 0)
    col = lax.broadcasted_iota(jnp.int32, h1.shape, 1)
    low_r = jnp.where(open_up, 0, 2)
    high_r = jnp.where(open_down, nrows + 4, nrows + 2)
    low_c = jnp.where(open_left, 0, 2)
    high_c = jnp.where(open_right, ncols + 4, ncols + 2)
    inside = (row >= low_r) & (row < high_r) & (col >= low_c) & (col < high_c)
    a1 = jnp.where(inside, h1 * sigmoid(h1), 0.0)
    acts[...] = jnp.zeros_like(acts)
    acts[:, 0:PITCH] = a1.astype(BF16).astype(F32)
    n2 = gather(acts, 0, 0, nrows + 2, PITCH)
    xyd = dot(patch[0:n2], conv2[...])
    xyds[...] = xyd.astype(BF16).astype(F32).reshape(nrows + 2, PITCH, width)

    rows_before = before[tall : tall + share + 1].astype(F32)
    rows_after = after[tall : tall + share + 1].astype(F32)
    mine = first[...].astype(F32)
    rim_mine = rim_row[...].astype(F32)
    same_at = pl.ds(pl.multiple_of(side * share, share), share)
    second_at = pl.ds(pl.multiple_of((1 - side) * share, share), share)
    xz_above, xz_below = [], []
    for k in range(depth):
        second = jnp.where(side == 0, rows_after[:, k, :], rows_before[:, k, :])
        yzs[k] = mine[0:ncols, k, :]
        xzs[k, same_at, :] = mine[ncols:, k, :]
        xzs[k, second_at, :] = second[0:share]
        rim_same, rim_second = rim_mine[:, k, :], second[share:]
        xz_above.append(jnp.where(side == 0, rim_same, rim_second))
        xz_below.append(jnp.where(side == 0, rim_second, rim_same))

    def decode(feat, label):
        u1 = dot(feat, w1[...])
        g1, s1 = silu_pair(u1)
        g1 = g1.astype(BF16)
        u2 = dot(g1, w2[...])
        g2, s2 = silu_pair(u2)
        g2 = g2.astype(BF16)
        logits = dot(g2, w3[...])
        lane = lax.broadcasted_iota(jnp.int32, logits.shape, 1)
        logits = jnp.where(lane < classes, logits, -jnp.inf)
        power = jnp.exp(logits - jnp.max(logits, axis=1, keepdims=True))
        prob = power / jnp.sum(power, axis=1, keepdims=True)
        onehot = jnp.where(lane == label, 1.0, 0.0)
        dlogits = (loss_weight * (prob - onehot)).astype(BF16)
        du2 = (dot_nt(dlogits, w3[...]) * s2).astype(BF16)
        du1 = (dot_nt(du2, w2[...]) * s1).astype(BF16)
        return g1, g2, dlogits, du2, du1, dot_nt(du1, w1[...])

    dw1[...] = jnp.zeros_like(dw1)
    dw2[...] = jnp.zeros_like(dw2)
    dw3[...] = jnp.zeros_like(dw3)
    dyz[...] = jnp.zeros_like(dyz)
    dx[...] = jnp.zeros_like(dx)
    chunk = 16
    size = chunk * ncols

    def step(index, carry):
        r0 = pl.multiple_of(index * chunk, chunk)
        tile = xyds[pl.ds(r0 + 1, chunk), 1 : ncols + 1, :]
        lab = labels[pl.ds(r0, chunk)].reshape(size, depth)
        feats, labs = [], []
        for k in range(depth):
            xz_k = xzs[k, pl.ds(r0, chunk), :]
            feat = tile + xz_k[:, None, :] + yzs[k][None]
            feats.append(feat.reshape(size, width).astype(BF16))
            labs.append(jnp.broadcast_to(lab[:, k : k + 1], (size, LANES)))
        feat = jnp.concatenate(feats, axis=0)
        g1, g2, dlogits, du2, du1, dfeat = decode(feat, jnp.concatenate(labs, axis=0))
        dw3[...] += dot_tn(dlogits, g2)
        dw2[...] += dot_tn(g1, du2)
        dw1[...] += dot_tn(feat, du1)
        total = jnp.zeros((chunk, ncols, width), F32)
        for k in range(depth):
            piece = dfeat[k * size : (k + 1) * size].reshape(chunk, ncols, width)
            total = total + piece
            dxz[k, pl.ds(r0, chunk), :] = jnp.sum(piece, axis=1)
            dyz[k] += jnp.sum(piece, axis=0)
        dx[pl.ds(r0 + 1, chunk), 1 : ncols + 1, :] = total.astype(BF16).astype(F32)
        return carry

    lax.fori_loop(0, nrows // chunk, step, 0)

    lab_before = before[2 : nrows + 4, 3, :].astype(F32).astype(jnp.int32)
    lab_after = after[2 : nrows + 4, 3, :].astype(F32).astype(jnp.int32)
    lab_up = above[3].astype(F32).astype(jnp.int32)
    lab_down = below[3].astype(F32).astype(jnp.int32)
    tail = jnp.zeros((PITCH - ncols - 2, LANES), jnp.int32)
    lab_rim = jnp.concatenate(
        [
            lab_before[0:1],
            lab_up,
            lab_after[0:1],
            tail,
            lab_before[nrows + 1 : nrows + 2],
            lab_down,
            lab_after[nrows + 1 : nrows + 2],
            tail,
            lab_before[1 : nrows + 1],
            lab_after[1 : nrows + 1],
        ],
        axis=0,
    )
    rim_at = (0, 1, nrows + 2 * REACH - 2, nrows + 2 * REACH - 1)
    feats, labs = [], []
    zero_tail = jnp.zeros((PITCH - ncols - 2, width), F32)
    for k in range(depth):
        yz_before = before[rim_at[k], 3:4, :].astype(F32)
        yz_after = after[rim_at[k], 3:4, :].astype(F32)
        yz_row = jnp.concatenate([yz_before, yzs[k], yz_after, zero_tail], axis=0)
        feats.append(xyds[0] + xz_above[k] + yz_row)
        feats.append(xyds[nrows + 1] + xz_below[k] + yz_row)
        feats.append(xyds[1 : nrows + 1, 0, :] + xzs[k] + yz_before)
        feats.append(xyds[1 : nrows + 1, ncols + 1, :] + xzs[k] + yz_after)
        labs.append(jnp.broadcast_to(lab_rim[:, k : k + 1], (2 * PITCH + 2 * nrows, LANES)))
    rim = decode(jnp.concatenate(feats, axis=0).astype(BF16), jnp.concatenate(labs, axis=0))[-1]
    span = 2 * PITCH + 2 * nrows
    rim_sum = rim[0:span]
    for k in range(1, depth):
        rim_sum = rim_sum + rim[k * span : (k + 1) * span]
    rim_sum = rim_sum.astype(BF16).astype(F32)
    rcol = lax.broadcasted_iota(jnp.int32, (PITCH, width), 0)
    keep = (rcol >= jnp.where(open_left, 0, 1)) & (rcol < jnp.where(open_right, ncols + 2, ncols + 1))
    dx[0] = jnp.where(keep & open_up, rim_sum[0:PITCH], 0.0)
    dx[nrows + 1] = jnp.where(keep & open_down, rim_sum[PITCH : 2 * PITCH], 0.0)
    west = rim_sum[2 * PITCH : 2 * PITCH + nrows]
    east = rim_sum[2 * PITCH + nrows : span]
    dx[1 : nrows + 1, 0, :] = jnp.where(open_left, west, 0.0)
    dx[1 : nrows + 1, ncols + 1, :] = jnp.where(open_right, east, 0.0)

    def put(start, block):
        for half, index, row, offset, rows in shares.split(start, block.shape[0]):
            packed[half, index, row : row + rows, :] = block[offset : offset + rows]

    def weight_gradient(start, dout):
        grad = dot_tn(dout, patch[0 : nrows * ncols])
        for tap in range(9):
            put(start + tap * width, grad[:, tap * width : (tap + 1) * width].T)

    packed[...] = jnp.zeros_like(packed)

    n3 = gather(acts, 1, 1, nrows, ncols)
    dxyd = dx[1 : nrows + 1, 1 : ncols + 1, :].reshape(n3, width).astype(BF16)
    weight_gradient(shares.at["conv2"], dxyd)
    gather(dx, 0, 0, nrows, ncols)
    da1 = dot(patch[0:n3], back[...])
    _, slope = silu_pair(hs[2 : nrows + 2, 2 : ncols + 2, :].reshape(n3, width))
    dh1 = (da1 * slope).astype(BF16)
    gather(xs, 2, 2, nrows, ncols)
    weight_gradient(shares.at["conv1"], dh1)

    for name, ref in (("w1", dw1), ("w2", dw2)):
        rows = ref.shape[0]
        for half in range(hidden // LANES):
            put(shares.at[name] + half * rows, ref[:, half * LANES : (half + 1) * LANES])
    for q in range(classes):
        where = packed.at[q // shares.chips, q % shares.chips]
        for half in range(hidden // LANES):
            row = shares.small + half
            where[row : row + 1, :] = dw3[q : q + 1, half * LANES : (half + 1) * LANES]
    time_row = jnp.sum(dh1.astype(F32), axis=0, keepdims=True)
    packed[classes // shares.chips, classes % shares.chips, shares.small : shares.small + 1, :] = time_row
    for k in range(depth):
        flat[pl.ds(k, ncols, stride=depth), :] = dyz[k]
    for half in range(2):
        for index in range(shares.yz_shares):
            begin = half * ncols * depth // 2 + index * shares.yz_rows
            packed[half, index, shares.yz : shares.yz + shares.yz_rows, :] = flat[begin : begin + shares.yz_rows]
    for k in range(depth):
        flat[pl.ds(k, nrows, stride=depth), :] = dxz[k]
    for index in range(shares.chips):
        begin = index * shares.xz_rows
        packed[core, index, shares.xz : shares.xz + shares.xz_rows, :] = flat[begin : begin + shares.xz_rows]
    own_out[...] = packed[core].astype(BF16)
    other_out[...] = packed[1 - core].astype(BF16)


def sum_kernel(shares, ny, pieces, out):
    chips = pieces.shape[0]
    nx = chips // ny
    cut, at_yz, yz_rows = shares.xz, shares.yz, shares.yz_rows
    total = pieces[0].astype(F32)
    for index in range(1, chips):
        total = total + pieces[index].astype(F32)
    common = total.astype(BF16)
    by_row, by_col = [], []
    for i in range(nx):
        part = pieces[i * ny, cut : shares.small].astype(F32)
        for j in range(1, ny):
            part = part + pieces[i * ny + j, cut : shares.small].astype(F32)
        by_row.append(part.astype(BF16))
    for j in range(ny):
        part = pieces[j, shares.small :].astype(F32)
        for i in range(1, nx):
            part = part + pieces[i * ny + j, shares.small :].astype(F32)
        by_col.append(part[at_yz - shares.small : at_yz - shares.small + yz_rows])
    pad = shares.rows - at_yz - 4 * yz_rows
    for i in range(nx):
        tail = [total[shares.small : at_yz]] + by_col[4 * i : 4 * i + 4]
        if pad:
            tail.append(jnp.zeros((pad, LANES), F32))
        tail = jnp.concatenate(tail, axis=0).astype(BF16)
        for j in range(ny):
            out[i * ny + j, 0:cut, :] = common[0:cut]
            out[i * ny + j, cut : shares.small, :] = by_row[j // 4]
            out[i * ny + j, shares.small :, :] = tail


def last_kernel(shares, classes, place, half, partner, emb, g1, g2, gt, gw1, gw2, gw3, gxz, gyz, whole, w3_rows):
    width, hidden = emb.shape[0], gw2.shape[0]
    core, row_core, row_side = place[0], place[1], place[2]
    whole[pl.ds(core, 1)] = half[...].astype(F32)[None]
    whole[pl.ds(1 - core, 1)] = partner[...].astype(F32)[None]

    def take(start, ref, lead, lanes):
        for side, index, row, offset, rows in shares.split(start, width if lead is not None else ref.shape[0]):
            block = whole[side, index, row : row + rows, :]
            if lead is not None:
                ref[lead, offset : offset + rows, :] = block
            else:
                ref[offset : offset + rows, lanes] = block

    for name, ref in (("conv1", g1), ("conv2", g2)):
        for tap in range(9):
            take(shares.at[name] + tap * width, ref, tap, None)
    for name, ref in (("w1", gw1), ("w2", gw2)):
        for part in range(hidden // LANES):
            take(shares.at[name] + part * ref.shape[0], ref, None, slice(part * LANES, (part + 1) * LANES))
    small = slice(shares.small, shares.small + 1)
    gt[...] = emb[...] * whole[classes // shares.chips, classes % shares.chips, small, :]
    for part in range(hidden // LANES):
        small = slice(shares.small + part, shares.small + part + 1)
        w3_rows[...] = jnp.zeros_like(w3_rows)
        for q in range(classes):
            w3_rows[q : q + 1, :] = whole[q // shares.chips, q % shares.chips, small, :]
        gw3[part * LANES : (part + 1) * LANES, :] = w3_rows[...].T[:, 0:classes]
    count = gxz.shape[0]
    begin = pl.multiple_of(row_side * count, count)
    gxz[...] = whole[row_core, pl.ds(begin, count), shares.xz : shares.xz + shares.xz_rows, :]
    size, per = shares.yz_rows, shares.yz_rows * shares.yz_shares
    for r in range(2):
        for side in range(2):
            for index in range(shares.yz_shares):
                even = whole[side, index, shares.yz + r * size : shares.yz + (r + 1) * size, :]
                odd = whole[side, index, shares.yz + (2 + r) * size : shares.yz + (3 + r) * size, :]
                to = (2 * r + side) * per + index * size
                gyz[to : to + size, :] = jnp.where(core == 0, even, odd)


def local(
    xy_noisy,
    xz_plane,
    yz_plane,
    labels,
    timestep,
    conv1_weight,
    conv2_weight,
    time_weight,
    w1,
    w2,
    w3,
):
    grid = Grid()
    nrows, ncols, width = xy_noisy.shape
    depth = labels.shape[2]
    hidden, classes = w3.shape
    count = grid.count
    side = grid.iy % count
    emb = time_embedding(timestep, width)
    temb = jnp.dot(emb, time_weight.astype(F32), precision=lax.Precision.HIGHEST)
    flat_one = conv1_weight.reshape(9 * width, width)
    flat_two = conv2_weight.reshape(9 * width, width)
    back_flat = jnp.transpose(conv2_weight[::-1, ::-1], (0, 1, 3, 2)).reshape(9 * width, width)
    w3_wide = jnp.pad(w3, ((0, 0), (0, LANES - classes)))

    up = lambda i, j: (i + 1, j)
    down = lambda i, j: (i - 1, j)
    left = lambda i, j: (i, j - 1)
    right = lambda i, j: (i, j + 1)

    def lab(part):
        return jnp.pad(part.astype(BF16), ((0, 0), (0, 0), (0, LANES - depth)))

    above = grid.move(jnp.concatenate([xy_noisy[nrows - REACH :], lab(labels[nrows - 1 :])]), up)
    below = grid.move(jnp.concatenate([xy_noisy[:REACH], lab(labels[:1])]), down)

    slab_count = xz_plane.shape[1] // depth
    start = timestep[0] % slab_count * depth
    xz_local = lax.dynamic_slice_in_dim(xz_plane, start, depth, 1)
    share = xz_local.shape[0]
    yz_half = lax.dynamic_slice(yz_plane, (side * ncols, start, 0), (ncols, depth, width))
    first = grid.move(jnp.concatenate([yz_half, xz_local], axis=0), grid.turned(0))
    rim_row = grid.move(
        jnp.where(side == 0, xz_local[:1], xz_local[share - 1 :]),
        lambda i, j: (j // count - 1, count * i + 1) if j % count == 0 else (j // count + 1, count * i),
    )

    def column(at, where):
        cols = jnp.concatenate(
            [above[:REACH, where], xy_noisy[:, where], below[:REACH, where]], axis=0
        )
        yz = first[at].reshape(depth, 1, width)
        extra = jnp.concatenate(
            [yz[:2], above[3:, at : at + 1], lab(labels[:, at : at + 1]), below[3:, at : at + 1], yz[2:]],
            axis=0,
        )
        return jnp.concatenate([jnp.concatenate([cols, extra], axis=1), first[ncols:], rim_row], axis=0)

    before = grid.move(column(ncols - 1, slice(ncols - REACH, ncols)), right)
    after = grid.move(column(0, slice(0, REACH)), left)

    core = grid.ix % 2
    flags = jnp.stack(
        [side, grid.ix, grid.nx - 1 - grid.ix, grid.iy, grid.ny - 1 - grid.iy, core]
    ).astype(jnp.int32)
    chips = grid.nx * grid.ny // 2
    shares = Shares(chips, nrows, ncols, depth, width, hidden)
    vmem = pl.BlockSpec(memory_space=pltpu.VMEM)
    smem = pl.BlockSpec(memory_space=pltpu.SMEM)
    params = pltpu.CompilerParams(vmem_limit_bytes=VMEM_LIMIT)
    buffer = jax.ShapeDtypeStruct((chips, shares.rows, LANES), BF16)
    own, other = pl.pallas_call(
        functools.partial(main_kernel, classes, shares),
        out_shape=(buffer, buffer),
        in_specs=[smem] + [vmem] * 15,
        out_specs=(vmem, vmem),
        scratch_shapes=[
            pltpu.VMEM((nrows + 6, 32, width), F32),
            pltpu.VMEM((nrows + 4, PITCH, width), F32),
            pltpu.VMEM((nrows + 4, 32, width), F32),
            pltpu.VMEM((nrows + 2, PITCH, width), F32),
            pltpu.VMEM((nrows + 2, PITCH, width), F32),
            pltpu.VMEM(((nrows + 4) * PITCH, 9 * width), BF16),
            pltpu.VMEM((depth, nrows, width), F32),
            pltpu.VMEM((depth, ncols, width), F32),
            pltpu.VMEM((width, hidden), F32),
            pltpu.VMEM((hidden, hidden), F32),
            pltpu.VMEM((LANES, hidden), F32),
            pltpu.VMEM((depth, nrows, width), F32),
            pltpu.VMEM((depth, ncols, width), F32),
            pltpu.VMEM((nrows * depth, width), F32),
            pltpu.VMEM((2, chips, shares.rows, LANES), F32),
        ],
        compiler_params=params,
        name="tile",
    )(
        flags,
        xy_noisy,
        above,
        below,
        before,
        after,
        labels,
        first,
        rim_row,
        temb.reshape(1, width),
        flat_one,
        flat_two,
        back_flat,
        w1,
        w2,
        w3_wide,
    )

    swap = lambda i, j: (i ^ 1, j)
    own = (own.astype(F32) + grid.move(other, swap).astype(F32)).astype(BF16)
    groups = [
        [i * grid.ny + j for i in range(c, grid.nx, 2) for j in range(grid.ny)] for c in range(2)
    ]
    pieces = lax.all_to_all(own, BOTH, 0, 0, axis_index_groups=groups)
    sums = pl.pallas_call(
        functools.partial(sum_kernel, shares, grid.ny),
        out_shape=buffer,
        in_specs=[vmem],
        out_specs=vmem,
        compiler_params=params,
        name="sums",
    )(pieces)
    half = lax.all_to_all(sums, BOTH, 0, 0, axis_index_groups=groups)
    partner = grid.move(half, swap)
    row_of = grid.iy // count
    g1, g2, gt, gw1, gw2, gw3, gxz, gyz = pl.pallas_call(
        functools.partial(last_kernel, shares, classes),
        out_shape=(
            jax.ShapeDtypeStruct((9, width, width), F32),
            jax.ShapeDtypeStruct((9, width, width), F32),
            jax.ShapeDtypeStruct((width, width), F32),
            jax.ShapeDtypeStruct((width, hidden), F32),
            jax.ShapeDtypeStruct((hidden, hidden), F32),
            jax.ShapeDtypeStruct((hidden, classes), F32),
            jax.ShapeDtypeStruct((chips // 2, shares.xz_rows, width), F32),
            jax.ShapeDtypeStruct((2 * ncols * depth, width), F32),
        ),
        in_specs=[smem, vmem, vmem, vmem],
        out_specs=(vmem,) * 8,
        scratch_shapes=[
            pltpu.VMEM((2, chips, shares.rows, LANES), F32),
            pltpu.VMEM((LANES, LANES), F32),
        ],
        compiler_params=params,
        name="spread",
    )(
        jnp.stack([core, row_of % 2, side]).astype(jnp.int32),
        half,
        partner,
        emb.reshape(width, 1),
    )
    shape = (3, 3, width, width)
    return (
        g1.reshape(shape),
        g2.reshape(shape),
        gt,
        gw1,
        gw2,
        gw3,
        gxz.reshape(share, depth, width),
        gyz.reshape(2 * ncols, depth, width),
    )


def solution(mesh):
    placed = (
        P("gx", "gy", None),
        P("gy", None, None),
        P("gx", None, None),
        P("gx", "gy", None),
        P(),
        P(),
        P(),
        P(),
        P(),
        P(),
        P(),
    )
    return jax.shard_map(
        local,
        mesh=mesh,
        in_specs=placed,
        out_specs=(P(), P(), P(), P(), P(), P(), P("gy", None, None), P("gx", None, None)),
        check_vma=False,
    )
```

time: 112 us -> 93 us (0.83)
  the two profiles are of different devices: /device:TPU:3 before, /device:TPU:0 now
where the time goes in v3:
time: 93 us; the launch traced here: 92.4 us
  blocking collectives  40.1 us (43%)
  Pallas kernels  19 us (20%)
  starting transfers between devices  18.6 us (20%)
  waiting for transfers between devices  7.41 us (8%)
  local copies, waits for them, and re-layouts  4.19 us (5%)
  between operations  1.74 us (2%)
  other arithmetic  1.32 us (1%)
    all_to_all x1, blocking collectives, local(): pieces = lax.all_to_all(own, BOTH, 0, 0, axis_index_groups=groups)  22.3 us
    ppermute x8, starting transfers between devices, move(): return lax.ppermute(array, BOTH, pairs)  18.6 us
    all_to_all x1, blocking collectives, local(): half = lax.all_to_all(sums, BOTH, 0, 0, axis_index_groups=groups)  17.8 us
    pallas_call x1, Pallas kernels, local(): pl.pallas_call(functools.partial(main_kernel, classes, shares), out_shape...  16.9 us
    ppermute x8, waiting for transfers between devices, move(): return lax.ppermute(array, BOTH, pairs)  7.41 us
    unnamed x27, local copies, waits for them, and re-layouts  2.67 us
    pallas_call x1, Pallas kernels, local(): pl.pallas_call(functools.partial(last_kernel, shares, classes), out_shape...  1.93 us
  transfers between devices with their start and end apart: 8, of which 5 were waited for; matrix products, arithmetic and copies ran while one was open for 3% of the time, Pallas kernels for 0%

profile of v3, /device:TPU:0, one launch (start us, length us, event | category | flops | bytes accessed | tf_op | source)
XLA Modules:
  0.0 92.4 jit_solution(3417156645947882139)
XLA Ops:
  0.6 0.0 copy-start
  1.4 0.7 dynamic-slice_select_fusion
  2.1 0.6 collective-permute-start.3
  2.8 0.9 constant_dynamic-slice_fusion
  3.7 0.0 copy-done
  3.7 0.0 copy-start.6
  3.8 0.7 collective-permute-start.2
  4.5 0.1 copy-done.6
  4.5 0.3 copy.19.labels
  4.9 8.9 %collective-permute-start = (bf16[4,16,128]{2,1,0:T(8,128)(2,1)S(1)}, bf16[4,16,128]{2,1,0:T(8,128)(2,1)S(1)}, u32[]{:S(2)}, u32[]{:S(2)}) collective-permute-start(bf16[4,16,128]{2,1,0:T(8,128)(2,1)S(1)} %fusion.2), channel_id=1, source_target_pairs={{0,8},{1,9},{2,10},{3,11},{4,12},{5,13},{6,14},{7,15},{8,16},{9,17... | collective-permute-start | bytes 49160 | tf_op jit(solution)/shard_map/ppermute | solution.py:63
  13.8 1.3 %collective-permute-start.1 = (bf16[4,16,128]{2,1,0:T(8,128)(2,1)S(1)}, bf16[4,16,128]{2,1,0:T(8,128)(2,1)S(1)}, u32[]{:S(2)}, u32[]{:S(2)}) collective-permute-start(bf16[4,16,128]{2,1,0:T(8,128)(2,1)S(1)} %fusion.3), channel_id=1, source_target_pairs={{8,0},{9,1},{10,2},{11,3},{12,4},{13,5},{14,6},{15,7},{16,8},{17,9... | collective-permute-start | bytes 49160 | tf_op jit(solution)/shard_map/ppermute | solution.py:63
  15.1 0.1 fusion.6
  15.2 0.0 copy-start.7
  15.2 0.1 fusion.7
  15.3 0.1 fusion.4
  15.3 0.1 maximum_bitcast_fusion
  15.4 0.6 copy-done.7
  15.9 0.1 fusion.12.temb
  16.1 0.7 copy-done.8
  16.8 0.1 copy.25
  16.9 0.0 collective-permute-done.above
  16.9 1.2 %collective-permute-done.1.below = bf16[4,16,128]{2,1,0:T(8,128)(2,1)S(1)} collective-permute-done((bf16[4,16,128]{2,1,0:T(8,128)(2,1)S(1)}, bf16[4,16,128]{2,1,0:T(8,128)(2,1)S(1)}, u32[]{:S(2)}, u32[]{:S(2)}) %collective-permute-start.1) | collective-permute-done | bytes 16416 | tf_op jit(solution)/shard_map/ppermute | solution.py:63
  18.2 0.0 collective-permute-done.2.first
  18.3 0.1 pad_dynamic-update-slice_fusion
  18.3 0.1 pad_dynamic-update-slice_fusion.1
  18.4 0.0 collective-permute-done.3.rim_row
  18.5 0.2 pad_maximum_fusion
  18.6 1.3 %collective-permute-start.5 = (bf16[103,4,128]{2,1,0:T(4,128)(2,1)S(1)}, bf16[103,4,128]{2,1,0:T(4,128)(2,1)S(1)}, u32[]{:S(2)}, u32[]{:S(2)}) collective-permute-start(bf16[103,4,128]{2,1,0:T(4,128)(2,1)S(1)} %get-tuple-element.48), channel_id=1, source_target_pairs={{1,0},{2,1},{3,2},{4,3},{5,4},{6,5},{7,6},{9,8},{10,9},{11,10},{12... | collective-permute-start | bytes 316424 | tf_op jit(solution)/shard_map/ppermute | solution.py:63
  19.9 4.6 %collective-permute-start.4 = (bf16[103,4,128]{2,1,0:T(4,128)(2,1)S(1)}, bf16[103,4,128]{2,1,0:T(4,128)(2,1)S(1)}, u32[]{:S(2)}, u32[]{:S(2)}) collective-permute-start(bf16[103,4,128]{2,1,0:T(4,128)(2,1)S(1)} %get-tuple-element.49), channel_id=1, source_target_pairs={{0,1},{1,2},{2,3},{3,4},{4,5},{5,6},{6,7},{8,9},{9,10},{10,11},{11... | collective-permute-start | bytes 316424 | tf_op jit(solution)/shard_map/ppermute | solution.py:63
  24.5 0.0 copy-start.3
  24.5 0.0 copy-start.5
  24.6 0.2 copy.24
  24.8 0.1 stack.37.place
  24.9 0.3 collective-permute-done.5.after
  25.2 2.6 %collective-permute-done.4.before = bf16[103,4,128]{2,1,0:T(4,128)(2,1)S(1)} collective-permute-done((bf16[103,4,128]{2,1,0:T(4,128)(2,1)S(1)}, bf16[103,4,128]{2,1,0:T(4,128)(2,1)S(1)}, u32[]{:S(2)}, u32[]{:S(2)}) %collective-permute-start.4) | collective-permute-done | bytes 105504 | tf_op jit(solution)/shard_map/ppermute | solution.py:63
  27.8 16.9 %tile.1 = (bf16[16,128,128]{2,1,0:T(8,128)(2,1)S(1)}, bf16[16,128,128]{2,1,0:T(8,128)(2,1)S(1)}) custom-call(s32[6]{0:T(128)S(1)} %stack.37.place, bf16[64,16,128]{2,1,0:T(8,128)(2,1)S(1)} %copy-done.2, bf16[4,16,128]{2,1,0:T(8,128)(2,1)S(1)} %collective-permute-done.above, bf16[4,16,128]{2,1,0:T(8,128)(2,1)S(1)} %collective-permute-done.1.below, ...), custom_call_target="tpu_custom_call" | custom-call | tf_op jit(solution)/shard_map/tile/pallas_call | solution.py:482
  44.8 1.2 %collective-permute-start.6 = (bf16[16,128,128]{2,1,0:T(8,128)(2,1)S(1)}, bf16[16,128,128]{2,1,0:T(8,128)(2,1)S(1)}, u32[]{:S(2)}, u32[]{:S(2)}) collective-permute-start(bf16[16,128,128]{2,1,0:T(8,128)(2,1)S(1)} %get-tuple-element.19), channel_id=1, source_target_pairs={{0,8},{1,9},{2,10},{3,11},{4,12},{5,13},{6,14},{7,15},{8,0},{9,1},... | collective-permute-start | bytes 1572872 | tf_op jit(solution)/shard_map/ppermute | solution.py:63
  46.0 1.5 %collective-permute-done.6 = bf16[16,128,128]{2,1,0:T(8,128)(2,1)S(1)} collective-permute-done((bf16[16,128,128]{2,1,0:T(8,128)(2,1)S(1)}, bf16[16,128,128]{2,1,0:T(8,128)(2,1)S(1)}, u32[]{:S(2)}, u32[]{:S(2)}) %collective-permute-start.6) | collective-permute-done | bytes 524320 | tf_op jit(solution)/shard_map/ppermute | solution.py:63
  47.5 0.1 add_convert_fusion
  47.7 22.3 %all_to_all.10.pieces = bf16[16,128,128]{2,1,0:T(8,128)(2,1)S(1)} all-to-all(bf16[16,128,128]{2,1,0:T(8,128)(2,1)S(1)} %add_convert_fusion), channel_id=1, replica_groups={{0,1,2,3,4,5,6,7,16,17,18,19,20,21,22,23},{8,9,10,11,12,13,14,15,24,25,..., dimensions={0} | all-to-all | bytes 1048576 | tf_op jit(solution)/shard_map/all_to_all | solution.py:530
  70.0 0.1 sums.1
  70.1 17.8 %all_to_all.11.half = bf16[16,128,128]{2,1,0:T(8,128)(2,1)S(1)} all-to-all(bf16[16,128,128]{2,1,0:T(8,128)(2,1)S(1)} %sums.1), channel_id=1, replica_groups={{0,1,2,3,4,5,6,7,16,17,18,19,20,21,22,23},{8,9,10,11,12,13,14,15,24,25,..., dimensions={0} | all-to-all | bytes 1048576 | tf_op jit(solution)/shard_map/all_to_all | solution.py:539
  87.9 0.0 collective-permute-start.7
  87.9 0.1 copy.27.emb
  88.0 0.1 pad_add_fusion.place
  88.1 1.7 %collective-permute-done.7.partner = bf16[16,128,128]{2,1,0:T(8,128)(2,1)S(1)} collective-permute-done((bf16[16,128,128]{2,1,0:T(8,128)(2,1)S(1)}, bf16[16,128,128]{2,1,0:T(8,128)(2,1)S(1)}, u32[]{:S(2)}, u32[]{:S(2)}) %collective-permute-start.7) | collective-permute-done | bytes 524320 | tf_op jit(solution)/shard_map/ppermute | solution.py:63
  89.8 1.9 %spread.1 = (f32[9,128,128]{2,1,0:T(8,128)}, f32[9,128,128]{2,1,0:T(8,128)}, f32[128,128]{1,0:T(8,128)}, f32[128,256]{1,0:T(8,128)}, f32[256,256]{1,0:T(8,128)},...) custom-call(s32[3]{0:T(128)S(1)} %pad_add_fusion.place, ...), custom_call_target="tpu_custom_call" | custom-call | tf_op jit(solution)/shard_map/spread/pallas_call | solution.py:542
  91.7 0.7 copy.28
  (27 shorter events, 0.3 us)
Async XLA Ops:
  0.6 3.0 %copy-start = (bf16[32,64,128]{2,1,0:T(8,128)(2,1)S(1)}, bf16[32,64,128]{2,1,0:T(8,128)(2,1)}, u32[]{:S(2)}) copy-start(bf16[32,64,128]{2,1,0:T(8,128)(2,1)} %param.13) | copy-start | bytes 1572868
  0.6 3.8 %copy-start.2 = (bf16[64,16,128]{2,1,0:T(8,128)(2,1)S(1)}, bf16[64,16,128]{2,1,0:T(8,128)(2,1)}, u32[]{:S(2)}) copy-start(bf16[64,16,128]{2,1,0:T(8,128)(2,1)} %xy.1) | copy-start | bytes 786436
  2.1 16.3 %collective-permute-start.3 = (bf16[1,4,128]{2,1,0:T(4,128)(2,1)S(1)}, bf16[1,4,128]{2,1,0:T(4,128)(2,1)S(1)}, u32[]{:S(2)}, u32[]{:S(2)}) collective-permute-start(bf16[1,4,128]{2,1,0:T(4,128)(2,1)S(1)} %dynamic-slice_select_fusion), channel_id=1, source_target_pairs={{1,8},{2,1},{3,16},{4,9},{5,24},{6,17},{9,10},{10,3},{11,18},{12,1... | collective-permute-start | bytes 3080 | tf_op jit(solution)/shard_map/ppermute | solution.py:63
  3.7 0.8 copy-start.6
  3.8 14.5 %collective-permute-start.2 = (bf16[48,4,128]{2,1,0:T(4,128)(2,1)S(1)}, bf16[48,4,128]{2,1,0:T(4,128)(2,1)S(1)}, u32[]{:S(2)}, u32[]{:S(2)}) collective-permute-start(bf16[48,4,128]{2,1,0:T(4,128)(2,1)S(1)} %pad_maximum_fusion.4), channel_id=1, source_target_pairs={{0,0},{1,1},{2,8},{3,9},{4,16},{5,17},{6,24},{7,25},{8,2},{9,3},{1... | collective-permute-start | bytes 147464 | tf_op jit(solution)/shard_map/ppermute | solution.py:63
  4.9 12.0 %collective-permute-start = (bf16[4,16,128]{2,1,0:T(8,128)(2,1)S(1)}, bf16[4,16,128]{2,1,0:T(8,128)(2,1)S(1)}, u32[]{:S(2)}, u32[]{:S(2)}) collective-permute-start(bf16[4,16,128]{2,1,0:T(8,128)(2,1)S(1)} %fusion.2), channel_id=1, source_target_pairs={{0,8},{1,9},{2,10},{3,11},{4,12},{5,13},{6,14},{7,15},{8,16},{9,17... | collective-permute-start | bytes 49160 | tf_op jit(solution)/shard_map/ppermute | solution.py:63
  13.8 4.4 %collective-permute-start.1 = (bf16[4,16,128]{2,1,0:T(8,128)(2,1)S(1)}, bf16[4,16,128]{2,1,0:T(8,128)(2,1)S(1)}, u32[]{:S(2)}, u32[]{:S(2)}) collective-permute-start(bf16[4,16,128]{2,1,0:T(8,128)(2,1)S(1)} %fusion.3), channel_id=1, source_target_pairs={{8,0},{9,1},{10,2},{11,3},{12,4},{13,5},{14,6},{15,7},{16,8},{17,9... | collective-permute-start | bytes 49160 | tf_op jit(solution)/shard_map/ppermute | solution.py:63
  15.2 0.8 copy-start.7
  16.1 0.7 copy-start.8
  18.4 6.1 %copy-start.1 = (bf16[3,3,128,128]{3,2,1,0:T(8,128)(2,1)S(1)}, bf16[3,3,128,128]{3,2,1,0:T(8,128)(2,1)}, u32[]{:S(2)}) copy-start(bf16[3,3,128,128]{3,2,1,0:T(8,128)(2,1)} %param.17) | copy-start | bytes 884740
  18.6 6.6 %collective-permute-start.5 = (bf16[103,4,128]{2,1,0:T(4,128)(2,1)S(1)}, bf16[103,4,128]{2,1,0:T(4,128)(2,1)S(1)}, u32[]{:S(2)}, u32[]{:S(2)}) collective-permute-start(bf16[103,4,128]{2,1,0:T(4,128)(2,1)S(1)} %get-tuple-element.48), channel_id=1, source_target_pairs={{1,0},{2,1},{3,2},{4,3},{5,4},{6,5},{7,6},{9,8},{10,9},{11,10},{12... | collective-permute-start | bytes 316424 | tf_op jit(solution)/shard_map/ppermute | solution.py:63
  19.9 7.9 %collective-permute-start.4 = (bf16[103,4,128]{2,1,0:T(4,128)(2,1)S(1)}, bf16[103,4,128]{2,1,0:T(4,128)(2,1)S(1)}, u32[]{:S(2)}, u32[]{:S(2)}) collective-permute-start(bf16[103,4,128]{2,1,0:T(4,128)(2,1)S(1)} %get-tuple-element.49), channel_id=1, source_target_pairs={{0,1},{1,2},{2,3},{3,4},{4,5},{5,6},{6,7},{8,9},{9,10},{10,11},{11... | collective-permute-start | bytes 316424 | tf_op jit(solution)/shard_map/ppermute | solution.py:63
  24.5 3.3 %copy-start.3 = (bf16[3,3,128,128]{3,2,1,0:T(8,128)(2,1)S(1)}, bf16[3,3,128,128]{3,2,1,0:T(8,128)(2,1)}, u32[]{:S(2)}) copy-start(bf16[3,3,128,128]{3,2,1,0:T(8,128)(2,1)} %param.16) | copy-start | bytes 884740
  24.5 3.3 %copy-start.5 = (bf16[128,256]{1,0:T(8,128)(2,1)S(1)}, bf16[128,256]{1,0:T(8,128)(2,1)}, u32[]{:S(2)}) copy-start(bf16[128,256]{1,0:T(8,128)(2,1)} %w1.1) | copy-start | bytes 196612
  24.8 3.0 %copy-start.4 = (bf16[256,256]{1,0:T(8,128)(2,1)S(1)}, bf16[256,256]{1,0:T(8,128)(2,1)}, u32[]{:S(2)}) copy-start(bf16[256,256]{1,0:T(8,128)(2,1)} %w2.1) | copy-start | bytes 393220
  44.8 2.8 %collective-permute-start.6 = (bf16[16,128,128]{2,1,0:T(8,128)(2,1)S(1)}, bf16[16,128,128]{2,1,0:T(8,128)(2,1)S(1)}, u32[]{:S(2)}, u32[]{:S(2)}) collective-permute-start(bf16[16,128,128]{2,1,0:T(8,128)(2,1)S(1)} %get-tuple-element.19), channel_id=1, source_target_pairs={{0,8},{1,9},{2,10},{3,11},{4,12},{5,13},{6,14},{7,15},{8,0},{9,1},... | collective-permute-start | bytes 1572872 | tf_op jit(solution)/shard_map/ppermute | solution.py:63
  87.9 1.9 %collective-permute-start.7 = (bf16[16,128,128]{2,1,0:T(8,128)(2,1)S(1)}, bf16[16,128,128]{2,1,0:T(8,128)(2,1)S(1)}, u32[]{:S(2)}, u32[]{:S(2)}) collective-permute-start(bf16[16,128,128]{2,1,0:T(8,128)(2,1)S(1)} %all_to_all.11.half), channel_id=1, source_target_pairs={{0,8},{1,9},{2,10},{3,11},{4,12},{5,13},{6,14},{7,15},{8,0},{9,1},... | collective-permute-start | bytes 1572872 | tf_op jit(solution)/shard_map/ppermute | solution.py:63

commit v4 on v3

--- a/solution.py
+++ b/solution.py
@@ -68,21 +68,28 @@
 
 
 class Shares:
-    def __init__(self, chips, nrows, ncols, depth, width, hidden):
+    def __init__(self, nx, ny, nrows, ncols, depth, width, hidden):
         sizes = (("conv1", 9 * width), ("conv2", 9 * width), ("w1", width * hidden // LANES), ("w2", hidden * hidden // LANES))
         self.at, total = {}, 0
         for name, rows in sizes:
             self.at[name] = total
             total += rows
-        self.chips = chips
+        self.chips = chips = nx * ny // 2
+        self.ranks, self.planes, self.layers = nx // 2, nx, ny // 2
         self.each = -(-total // (2 * chips * 8)) * 8
         self.xz_rows = nrows * depth // chips
         self.yz_rows = max(1, ncols * depth // 2 // chips)
         self.yz_shares = ncols * depth // 2 // self.yz_rows
+        self.xz_slot = -(-self.xz_rows // 8) * 8
+        even = lambda rows: -(-rows // 16) * 16
         self.xz = self.each
-        self.small = self.xz + -(-self.xz_rows // 8) * 8
+        self.small = self.xz + self.xz_slot
         self.yz = self.small + 2
-        self.rows = -(-(self.yz + 4 * self.yz_rows) // 16) * 16
+        self.rows = even(self.yz + self.yz_rows)
+        self.mid_small = self.xz + self.ranks * self.xz_slot
+        self.mid_yz = self.mid_small + 2
+        self.mid_rows = even(self.mid_yz + 2 * self.yz_rows)
+        self.end_rows = even(self.yz + ny * self.yz_rows)
 
     def split(self, start, rows):
         done = 0
@@ -331,46 +338,75 @@
     for index in range(shares.chips):
         begin = index * shares.xz_rows
         packed[core, index, shares.xz : shares.xz + shares.xz_rows, :] = flat[begin : begin + shares.xz_rows]
-    own_out[...] = packed[core].astype(BF16)
-    other_out[...] = packed[1 - core].astype(BF16)
-
-
-def sum_kernel(shares, ny, pieces, out):
-    chips = pieces.shape[0]
-    nx = chips // ny
-    cut, at_yz, yz_rows = shares.xz, shares.yz, shares.yz_rows
-    total = pieces[0].astype(F32)
-    for index in range(1, chips):
-        total = total + pieces[index].astype(F32)
-    common = total.astype(BF16)
-    by_row, by_col = [], []
-    for i in range(nx):
-        part = pieces[i * ny, cut : shares.small].astype(F32)
-        for j in range(1, ny):
-            part = part + pieces[i * ny + j, cut : shares.small].astype(F32)
-        by_row.append(part.astype(BF16))
-    for j in range(ny):
-        part = pieces[j, shares.small :].astype(F32)
-        for i in range(1, nx):
-            part = part + pieces[i * ny + j, shares.small :].astype(F32)
-        by_col.append(part[at_yz - shares.small : at_yz - shares.small + yz_rows])
-    pad = shares.rows - at_yz - 4 * yz_rows
-    for i in range(nx):
-        tail = [total[shares.small : at_yz]] + by_col[4 * i : 4 * i + 4]
-        if pad:
-            tail.append(jnp.zeros((pad, LANES), F32))
-        tail = jnp.concatenate(tail, axis=0).astype(BF16)
-        for j in range(ny):
-            out[i * ny + j, 0:cut, :] = common[0:cut]
-            out[i * ny + j, cut : shares.small, :] = by_row[j // 4]
-            out[i * ny + j, shares.small :, :] = tail
-
-
-def last_kernel(shares, classes, place, half, partner, emb, g1, g2, gt, gw1, gw2, gw3, gxz, gyz, whole, w3_rows):
+    plane, layer = place[6], place[7]
+    for k in range(shares.planes):
+        for t in range(shares.layers):
+            index = (plane ^ k) * shares.layers + (layer ^ t)
+            own_out[k, t] = packed[core, index].astype(BF16)
+            other_out[k, t] = packed[1 - core, index].astype(BF16)
+
+
+def core_kernel(own, other, *outs):
+    for k, out in enumerate(outs):
+        out[...] = (own[k].astype(F32) + other[k].astype(F32)).astype(BF16)
+
+
+def plane_kernel(shares, *refs):
+    blocks, outs = refs[: shares.planes], refs[shares.planes :]
+    size = shares.yz_rows
+    for t, out in enumerate(outs):
+        got = [block[t].astype(F32) for block in blocks]
+        total = sum(got[1:], got[0])
+        pieces = [total[: shares.each]]
+        for rank in range(shares.ranks):
+            pair = got[2 * rank] + got[2 * rank + 1]
+            pieces.append(pair[shares.xz : shares.small])
+        pieces.append(total[shares.small : shares.yz])
+        for column in range(2):
+            part = sum(got[column + 2 :: 2], got[column])
+            pieces.append(part[shares.yz : shares.yz + size])
+        rest = shares.mid_rows - shares.mid_yz - 2 * size
+        if rest:
+            pieces.append(jnp.zeros((rest, LANES), F32))
+        out[...] = jnp.concatenate(pieces, axis=0).astype(BF16)
+
+
+def layer_kernel(shares, place, *refs):
+    layers, size = shares.layers, shares.yz_rows
+    blocks, outs = refs[:layers], refs[layers : 2 * layers]
+    by_row, by_col, tail = refs[2 * layers :]
+    plane, layer = place[6], place[7]
+    rank, column = plane // 2, plane % 2
+    got = [block[...].astype(F32) for block in blocks]
+    total = sum(got[1:], got[0])
+    for r in range(shares.ranks):
+        begin = shares.xz + r * shares.xz_slot
+        by_row[rank ^ r] = total[begin : begin + shares.xz_slot]
+    for t in range(layers):
+        for c in range(2):
+            begin = shares.mid_yz + c * size
+            by_col[2 * (layer ^ t) + (column ^ c), 0:size, :] = got[t][begin : begin + size]
+    tail[...] = jnp.zeros_like(tail)
+    tail[0:2, :] = total[shares.mid_small : shares.mid_yz]
+    for j in range(2 * layers):
+        tail[2 + j * size : 2 + (j + 1) * size, :] = by_col[j, 0:size, :]
+    common = total[: shares.each].astype(BF16)
+    for t, out in enumerate(outs):
+        out[0 : shares.each, :] = common
+        out[shares.each :, :] = jnp.concatenate([by_row[(layer ^ t) // 2], tail[...]], axis=0).astype(BF16)
+
+
+def last_kernel(shares, classes, place, *refs):
+    halves, refs = refs[: 2 * shares.planes], refs[2 * shares.planes :]
+    emb, g1, g2, gt, gw1, gw2, gw3, gxz, gyz, whole, w3_rows = refs
     width, hidden = emb.shape[0], gw2.shape[0]
-    core, row_core, row_side = place[0], place[1], place[2]
-    whole[pl.ds(core, 1)] = half[...].astype(F32)[None]
-    whole[pl.ds(1 - core, 1)] = partner[...].astype(F32)[None]
+    core, plane, layer = place[5], place[6], place[7]
+    row_core, row_side, rank = place[8], place[0], place[9]
+    for k in range(shares.planes):
+        for t in range(shares.layers):
+            index = (plane ^ k) * shares.layers + (layer ^ t)
+            whole[core, index] = halves[k][t].astype(F32)
+            whole[1 - core, index] = halves[shares.planes + k][t].astype(F32)
 
     def take(start, ref, lead, lanes):
         for side, index, row, offset, rows in shares.split(start, width if lead is not None else ref.shape[0]):
@@ -401,10 +437,12 @@
     for r in range(2):
         for side in range(2):
             for index in range(shares.yz_shares):
-                even = whole[side, index, shares.yz + r * size : shares.yz + (r + 1) * size, :]
-                odd = whole[side, index, shares.yz + (2 + r) * size : shares.yz + (3 + r) * size, :]
                 to = (2 * r + side) * per + index * size
-                gyz[to : to + size, :] = jnp.where(core == 0, even, odd)
+                value = whole[side, index, shares.yz + r * size : shares.yz + (r + 1) * size, :]
+                for i in range(1, shares.planes):
+                    begin = shares.yz + (2 * i + r) * size
+                    value = jnp.where(rank == i, whole[side, index, begin : begin + size, :], value)
+                gyz[to : to + size, :] = value
 
 
 def local(
@@ -471,14 +509,25 @@
 
     core = grid.ix % 2
     flags = jnp.stack(
-        [side, grid.ix, grid.nx - 1 - grid.ix, grid.iy, grid.ny - 1 - grid.iy, core]
+        [
+            side,
+            grid.ix,
+            grid.nx - 1 - grid.ix,
+            grid.iy,
+            grid.ny - 1 - grid.iy,
+            core,
+            grid.ix // 2 * 2 + grid.iy % 2,
+            grid.iy // 2,
+            grid.iy // count % 2,
+            grid.ix,
+        ]
     ).astype(jnp.int32)
-    chips = grid.nx * grid.ny // 2
-    shares = Shares(chips, nrows, ncols, depth, width, hidden)
+    shares = Shares(grid.nx, grid.ny, nrows, ncols, depth, width, hidden)
+    planes, layers, chips = shares.planes, shares.layers, shares.chips
     vmem = pl.BlockSpec(memory_space=pltpu.VMEM)
     smem = pl.BlockSpec(memory_space=pltpu.SMEM)
     params = pltpu.CompilerParams(vmem_limit_bytes=VMEM_LIMIT)
-    buffer = jax.ShapeDtypeStruct((chips, shares.rows, LANES), BF16)
+    buffer = jax.ShapeDtypeStruct((planes, layers, shares.rows, LANES), BF16)
     own, other = pl.pallas_call(
         functools.partial(main_kernel, classes, shares),
         out_shape=(buffer, buffer),
@@ -523,22 +572,37 @@
     )
 
     swap = lambda i, j: (i ^ 1, j)
-    own = (own.astype(F32) + grid.move(other, swap).astype(F32)).astype(BF16)
-    groups = [
-        [i * grid.ny + j for i in range(c, grid.nx, 2) for j in range(grid.ny)] for c in range(2)
-    ]
-    pieces = lax.all_to_all(own, BOTH, 0, 0, axis_index_groups=groups)
-    sums = pl.pallas_call(
-        functools.partial(sum_kernel, shares, grid.ny),
-        out_shape=buffer,
-        in_specs=[vmem],
-        out_specs=vmem,
-        compiler_params=params,
-        name="sums",
-    )(pieces)
-    half = lax.all_to_all(sums, BOTH, 0, 0, axis_index_groups=groups)
-    partner = grid.move(half, swap)
-    row_of = grid.iy // count
+    in_plane = lambda k: lambda i, j: (i ^ (k // 2 * 2), j ^ (k % 2))
+    in_layer = lambda t: lambda i, j: (i, j ^ (2 * t))
+
+    def kernel(body, count_in, shape, count_out, name, scratch=(), scalars=False):
+        return pl.pallas_call(
+            body,
+            out_shape=(jax.ShapeDtypeStruct(shape, BF16),) * count_out,
+            in_specs=[smem] * scalars + [vmem] * count_in,
+            out_specs=(vmem,) * count_out,
+            scratch_shapes=list(scratch),
+            compiler_params=params,
+            name=name,
+        )
+
+    swapped = grid.move(other, swap)
+    blocks = kernel(core_kernel, 2, (layers, shares.rows, LANES), planes, "cores")(own, swapped)
+    blocks = [blocks[0]] + [grid.move(blocks[k], in_plane(k)) for k in range(1, planes)]
+    body = functools.partial(plane_kernel, shares)
+    blocks = kernel(body, planes, (shares.mid_rows, LANES), layers, "planes")(*blocks)
+    blocks = [blocks[0]] + [grid.move(blocks[t], in_layer(t)) for t in range(1, layers)]
+    scratch = (
+        pltpu.VMEM((shares.ranks, shares.xz_slot, LANES), F32),
+        pltpu.VMEM((grid.ny, 8, LANES), F32),
+        pltpu.VMEM((shares.end_rows - shares.small, LANES), F32),
+    )
+    body = functools.partial(layer_kernel, shares)
+    blocks = kernel(body, layers, (shares.end_rows, LANES), layers, "layers", scratch, True)(flags, *blocks)
+    blocks = [blocks[0]] + [grid.move(blocks[t], in_layer(t)) for t in range(1, layers)]
+    mine = jnp.stack(blocks)
+    halves = [mine] + [grid.move(mine, in_plane(k)) for k in range(1, planes)]
+    halves = halves + [grid.move(half, swap) for half in halves]
     g1, g2, gt, gw1, gw2, gw3, gxz, gyz = pl.pallas_call(
         functools.partial(last_kernel, shares, classes),
         out_shape=(
@@ -551,18 +615,17 @@
             jax.ShapeDtypeStruct((chips // 2, shares.xz_rows, width), F32),
             jax.ShapeDtypeStruct((2 * ncols * depth, width), F32),
         ),
-        in_specs=[smem, vmem, vmem, vmem],
+        in_specs=[smem] + [vmem] * (2 * planes + 1),
         out_specs=(vmem,) * 8,
         scratch_shapes=[
-            pltpu.VMEM((2, chips, shares.rows, LANES), F32),
+            pltpu.VMEM((2, chips, shares.end_rows, LANES), F32),
             pltpu.VMEM((LANES, LANES), F32),
         ],
         compiler_params=params,
         name="spread",
     )(
-        jnp.stack([core, row_of % 2, side]).astype(jnp.int32),
-        half,
-        partner,
+        flags,
+        *halves,
         emb.reshape(width, 1),
     )
     shape = (3, 3, width, width)

time: 93 us -> 88.5 us (0.952)
  blocking collectives: 40.1 us -> 0 us
  starting transfers between devices: 18.6 us -> 36.2 us
  waiting for transfers between devices: 7.41 us -> 24.9 us
    all_to_all x2 -> x0, blocking collectives: 40.1 us -> none  [the longest x1 22.3 us: local(): pieces = lax.all_to_all(own, BOTH, 0, 0, axis_index_groups=groups)]
    ppermute x8 -> x23, starting transfers between devices: 18.6 us -> 36.2 us  [move(): return lax.ppermute(array, BOTH, pairs)]
    ppermute x8 -> x23, waiting for transfers between devices: 7.41 us -> 24.9 us  [move(): return lax.ppermute(array, BOTH, pairs)]
  transfers between devices with their start and end apart: 8 -> 23, of which waited for: 5 -> 16; matrix products, arithmetic and copies ran while one was open for 3% -> 3% of each run, Pallas kernels for 0% -> 0%
where the time goes in v4:
time: 88.5 us; the launch traced here: 88.1 us
  starting transfers between devices  36.2 us (41%)
  waiting for transfers between devices  24.9 us (28%)
  Pallas kernels  19.7 us (22%)
  local copies, waits for them, and re-layouts  4.19 us (5%)
  between operations  1.78 us (2%)
  other arithmetic  1.12 us (1%)
    ppermute x23, starting transfers between devices, move(): return lax.ppermute(array, BOTH, pairs)  36.2 us
    ppermute x23, waiting for transfers between devices, move(): return lax.ppermute(array, BOTH, pairs)  24.9 us
    pallas_call x1, Pallas kernels, local(): pl.pallas_call(functools.partial(main_kernel, classes, shares), out_shape...  16.9 us
    unnamed x27, local copies, waits for them, and re-layouts  2.67 us
    pallas_call x1, Pallas kernels, local(): pl.pallas_call(functools.partial(last_kernel, shares, classes), out_shape...  1.95 us
  transfers between devices with their start and end apart: 23, of which 16 were waited for; matrix products, arithmetic and copies ran while one was open for 3% of the time, Pallas kernels for 0%

profile of v4, /device:TPU:0, one launch (start us, length us, event | category | flops | bytes accessed | tf_op | source)
XLA Modules:
  0.0 88.1 jit_solution(15891754128612656573)
XLA Ops:
  1.4 0.7 dynamic-slice_select_fusion
  2.1 0.6 collective-permute-start.3
  2.8 0.9 constant_dynamic-slice_fusion
  3.8 0.7 collective-permute-start.2
  4.5 0.3 copy.19.labels
  4.9 8.9 %collective-permute-start = (bf16[4,16,128]{2,1,0:T(8,128)(2,1)S(1)}, bf16[4,16,128]{2,1,0:T(8,128)(2,1)S(1)}, u32[]{:S(2)}, u32[]{:S(2)}) collective-permute-start(bf16[4,16,128]{2,1,0:T(8,128)(2,1)S(1)} %fusion.2), channel_id=1, source_target_pairs={{0,8},{1,9},{2,10},{3,11},{4,12},{5,13},{6,14},{7,15},{8,16},{9,17... | collective-permute-start | bytes 49160 | tf_op jit(solution)/shard_map/ppermute | solution.py:63
  13.8 1.3 %collective-permute-start.1 = (bf16[4,16,128]{2,1,0:T(8,128)(2,1)S(1)}, bf16[4,16,128]{2,1,0:T(8,128)(2,1)S(1)}, u32[]{:S(2)}, u32[]{:S(2)}) collective-permute-start(bf16[4,16,128]{2,1,0:T(8,128)(2,1)S(1)} %fusion.3), channel_id=1, source_target_pairs={{8,0},{9,1},{10,2},{11,3},{12,4},{13,5},{14,6},{15,7},{16,8},{17,9... | collective-permute-start | bytes 49160 | tf_op jit(solution)/shard_map/ppermute | solution.py:63
  15.4 0.6 copy-done.7
  15.9 0.1 fusion.12.temb
  16.1 0.7 copy-done.8
  16.8 0.1 copy.25
  16.9 1.2 %collective-permute-done.1.below = bf16[4,16,128]{2,1,0:T(8,128)(2,1)S(1)} collective-permute-done((bf16[4,16,128]{2,1,0:T(8,128)(2,1)S(1)}, bf16[4,16,128]{2,1,0:T(8,128)(2,1)S(1)}, u32[]{:S(2)}, u32[]{:S(2)}) %collective-permute-start.1) | collective-permute-done | bytes 16416 | tf_op jit(solution)/shard_map/ppermute | solution.py:63
  18.5 0.2 pad_maximum_fusion.1
  18.6 1.3 %collective-permute-start.5 = (bf16[103,4,128]{2,1,0:T(4,128)(2,1)S(1)}, bf16[103,4,128]{2,1,0:T(4,128)(2,1)S(1)}, u32[]{:S(2)}, u32[]{:S(2)}) collective-permute-start(bf16[103,4,128]{2,1,0:T(4,128)(2,1)S(1)} %get-tuple-element.72), channel_id=1, source_target_pairs={{1,0},{2,1},{3,2},{4,3},{5,4},{6,5},{7,6},{9,8},{10,9},{11,10},{12... | collective-permute-start | bytes 316424 | tf_op jit(solution)/shard_map/ppermute | solution.py:63
  19.9 4.6 %collective-permute-start.4 = (bf16[103,4,128]{2,1,0:T(4,128)(2,1)S(1)}, bf16[103,4,128]{2,1,0:T(4,128)(2,1)S(1)}, u32[]{:S(2)}, u32[]{:S(2)}) collective-permute-start(bf16[103,4,128]{2,1,0:T(4,128)(2,1)S(1)} %get-tuple-element.73), channel_id=1, source_target_pairs={{0,1},{1,2},{2,3},{3,4},{4,5},{5,6},{6,7},{8,9},{9,10},{10,11},{11... | collective-permute-start | bytes 316424 | tf_op jit(solution)/shard_map/ppermute | solution.py:63
  24.6 0.2 copy.24
  24.9 0.3 collective-permute-done.5.after
  25.2 2.6 %collective-permute-done.4.before = bf16[103,4,128]{2,1,0:T(4,128)(2,1)S(1)} collective-permute-done((bf16[103,4,128]{2,1,0:T(4,128)(2,1)S(1)}, bf16[103,4,128]{2,1,0:T(4,128)(2,1)S(1)}, u32[]{:S(2)}, u32[]{:S(2)}) %collective-permute-start.4) | collective-permute-done | bytes 105504 | tf_op jit(solution)/shard_map/ppermute | solution.py:63
  27.8 16.9 %tile.1 = (bf16[4,4,128,128]{3,2,1,0:T(8,128)(2,1)S(1)}, bf16[4,4,128,128]{3,2,1,0:T(8,128)(2,1)S(1)}) custom-call(s32[10]{0:T(128)S(1)} %stack.55.place, bf16[64,16,128]{2,1,0:T(8,128)(2,1)S(1)} %copy-done.2, bf16[4,16,128]{2,1,0:T(8,128)(2,1)S(1)} %collective-permute-done.above, bf16[4,16,128]{2,1,0:T(8,128)(2,1)S(1)} %collective-permute-done.1.below, ...), custom_call_target="tpu_custom_call" | custom-call | tf_op jit(solution)/shard_map/tile/pallas_call | solution.py:531
  44.8 1.2 %collective-permute-start.6 = (bf16[4,4,128,128]{3,2,1,0:T(8,128)(2,1)S(1)}, bf16[4,4,128,128]{3,2,1,0:T(8,128)(2,1)S(1)}, u32[]{:S(2)}, u32[]{:S(2)}) collective-permute-start(bf16[4,4,128,128]{3,2,1,0:T(8,128)(2,1)S(1)} %get-tuple-element.31), channel_id=1, source_target_pairs={{0,8},{1,9},{2,10},{3,11},{4,12},{5,13},{6,14},{7,15},{8,0},{9,1},... | collective-permute-start | bytes 1572872 | tf_op jit(solution)/shard_map/ppermute | solution.py:63
  46.0 1.5 %collective-permute-done.6.other = bf16[4,4,128,128]{3,2,1,0:T(8,128)(2,1)S(1)} collective-permute-done((bf16[4,4,128,128]{3,2,1,0:T(8,128)(2,1)S(1)}, bf16[4,4,128,128]{3,2,1,0:T(8,128)(2,1)S(1)}, u32[]{:S(2)}, u32[]{:S(2)}) %collective-permute-start.6) | collective-permute-done | bytes 524320 | tf_op jit(solution)/shard_map/ppermute | solution.py:63
  47.5 0.1 cores.1
  47.7 2.3 %collective-permute-start.7 = (bf16[4,128,128]{2,1,0:T(8,128)(2,1)S(1)}, bf16[4,128,128]{2,1,0:T(8,128)(2,1)S(1)}, u32[]{:S(2)}, u32[]{:S(2)}) collective-permute-start(bf16[4,128,128]{2,1,0:T(8,128)(2,1)S(1)} %get-tuple-element.33), channel_id=1, source_target_pairs={{0,1},{1,0},{2,3},{3,2},{4,5},{5,4},{6,7},{7,6},{8,9},{9,8},{10,11... | collective-permute-start | bytes 393224 | tf_op jit(solution)/shard_map/ppermute | solution.py:63
  49.9 2.4 %collective-permute-start.8 = (bf16[4,128,128]{2,1,0:T(8,128)(2,1)S(1)}, bf16[4,128,128]{2,1,0:T(8,128)(2,1)S(1)}, u32[]{:S(2)}, u32[]{:S(2)}) collective-permute-start(bf16[4,128,128]{2,1,0:T(8,128)(2,1)S(1)} %get-tuple-element.34), channel_id=1, source_target_pairs={{0,16},{1,17},{2,18},{3,19},{4,20},{5,21},{6,22},{7,23},{8,24},{9,... | collective-permute-start | bytes 393224 | tf_op jit(solution)/shard_map/ppermute | solution.py:63
  52.3 1.7 %collective-permute-done.7.refs_1_ = bf16[4,128,128]{2,1,0:T(8,128)(2,1)S(1)} collective-permute-done((bf16[4,128,128]{2,1,0:T(8,128)(2,1)S(1)}, bf16[4,128,128]{2,1,0:T(8,128)(2,1)S(1)}, u32[]{:S(2)}, u32[]{:S(2)}) %collective-permute-start.7) | collective-permute-done | bytes 131104 | tf_op jit(solution)/shard_map/ppermute | solution.py:63
  54.0 2.6 %collective-permute-done.8.refs_2_ = bf16[4,128,128]{2,1,0:T(8,128)(2,1)S(1)} collective-permute-done((bf16[4,128,128]{2,1,0:T(8,128)(2,1)S(1)}, bf16[4,128,128]{2,1,0:T(8,128)(2,1)S(1)}, u32[]{:S(2)}, u32[]{:S(2)}) %collective-permute-start.8) | collective-permute-done | bytes 131104 | tf_op jit(solution)/shard_map/ppermute | solution.py:63
  56.6 1.8 %collective-permute-done.9.refs_3_ = bf16[4,128,128]{2,1,0:T(8,128)(2,1)S(1)} collective-permute-done((bf16[4,128,128]{2,1,0:T(8,128)(2,1)S(1)}, bf16[4,128,128]{2,1,0:T(8,128)(2,1)S(1)}, u32[]{:S(2)}, u32[]{:S(2)}) %collective-permute-start.9) | collective-permute-done | bytes 131104 | tf_op jit(solution)/shard_map/ppermute | solution.py:63
  58.5 2.4 %collective-permute-start.10 = (bf16[144,128]{1,0:T(8,128)(2,1)S(1)}, bf16[144,128]{1,0:T(8,128)(2,1)S(1)}, u32[]{:S(2)}, u32[]{:S(2)}) collective-permute-start(bf16[144,128]{1,0:T(8,128)(2,1)S(1)} %get-tuple-element.37), channel_id=1, source_target_pairs={{0,2},{1,3},{2,0},{3,1},{4,6},{5,7},{6,4},{7,5},{8,10},{9,11},{10,... | collective-permute-start | bytes 110600 | tf_op jit(solution)/shard_map/ppermute | solution.py:63
  60.8 1.3 %collective-permute-start.11 = (bf16[144,128]{1,0:T(8,128)(2,1)S(1)}, bf16[144,128]{1,0:T(8,128)(2,1)S(1)}, u32[]{:S(2)}, u32[]{:S(2)}) collective-permute-start(bf16[144,128]{1,0:T(8,128)(2,1)S(1)} %get-tuple-element.38), channel_id=1, source_target_pairs={{0,4},{1,5},{2,6},{3,7},{4,0},{5,1},{6,2},{7,3},{8,12},{9,13},{10,... | collective-permute-start | bytes 110600 | tf_op jit(solution)/shard_map/ppermute | solution.py:63
  62.2 1.1 %collective-permute-start.12 = (bf16[144,128]{1,0:T(8,128)(2,1)S(1)}, bf16[144,128]{1,0:T(8,128)(2,1)S(1)}, u32[]{:S(2)}, u32[]{:S(2)}) collective-permute-start(bf16[144,128]{1,0:T(8,128)(2,1)S(1)} %get-tuple-element.39), channel_id=1, source_target_pairs={{0,6},{1,7},{2,4},{3,5},{4,2},{5,3},{6,0},{7,1},{8,14},{9,15},{10,... | collective-permute-start | bytes 110600 | tf_op jit(solution)/shard_map/ppermute | solution.py:63
  63.3 2.7 %collective-permute-done.11.refs_2_ = bf16[144,128]{1,0:T(8,128)(2,1)S(1)} collective-permute-done((bf16[144,128]{1,0:T(8,128)(2,1)S(1)}, bf16[144,128]{1,0:T(8,128)(2,1)S(1)}, u32[]{:S(2)}, u32[]{:S(2)}) %collective-permute-start.11) | collective-permute-done | bytes 36896 | tf_op jit(solution)/shard_map/ppermute | solution.py:63
  66.0 1.9 %collective-permute-done.12.refs_3_ = bf16[144,128]{1,0:T(8,128)(2,1)S(1)} collective-permute-done((bf16[144,128]{1,0:T(8,128)(2,1)S(1)}, bf16[144,128]{1,0:T(8,128)(2,1)S(1)}, u32[]{:S(2)}, u32[]{:S(2)}) %collective-permute-start.12) | collective-permute-done | bytes 36896 | tf_op jit(solution)/shard_map/ppermute | solution.py:63
  67.9 0.6 layers.1
  68.6 1.7 %collective-permute-start.14 = (bf16[144,128]{1,0:T(8,128)(2,1)S(1)}, bf16[144,128]{1,0:T(8,128)(2,1)S(1)}, u32[]{:S(2)}, u32[]{:S(2)}) collective-permute-start(bf16[144,128]{1,0:T(8,128)(2,1)S(1)} %get-tuple-element.42), channel_id=1, source_target_pairs={{0,4},{1,5},{2,6},{3,7},{4,0},{5,1},{6,2},{7,3},{8,12},{9,13},{10,... | collective-permute-start | bytes 110600 | tf_op jit(solution)/shard_map/ppermute | solution.py:63
  70.3 2.7 %collective-permute-start.15 = (bf16[144,128]{1,0:T(8,128)(2,1)S(1)}, bf16[144,128]{1,0:T(8,128)(2,1)S(1)}, u32[]{:S(2)}, u32[]{:S(2)}) collective-permute-start(bf16[144,128]{1,0:T(8,128)(2,1)S(1)} %get-tuple-element.43), channel_id=1, source_target_pairs={{0,6},{1,7},{2,4},{3,5},{4,2},{5,3},{6,0},{7,1},{8,14},{9,15},{10,... | collective-permute-start | bytes 110600 | tf_op jit(solution)/shard_map/ppermute | solution.py:63
  73.0 0.5 collective-permute-done.14
  73.5 2.5 %collective-permute-done.15 = bf16[144,128]{1,0:T(8,128)(2,1)S(1)} collective-permute-done((bf16[144,128]{1,0:T(8,128)(2,1)S(1)}, bf16[144,128]{1,0:T(8,128)(2,1)S(1)}, u32[]{:S(2)}, u32[]{:S(2)}) %collective-permute-start.15) | collective-permute-done | bytes 36896 | tf_op jit(solution)/shard_map/ppermute | solution.py:63
  76.0 2.6 %collective-permute-start.18 = (bf16[4,144,128]{2,1,0:T(8,128)(2,1)S(1)}, bf16[4,144,128]{2,1,0:T(8,128)(2,1)S(1)}, u32[]{:S(2)}, u32[]{:S(2)}) collective-permute-start(bf16[4,144,128]{2,1,0:T(8,128)(2,1)S(1)} %pad_maximum_fusion.refs_0_), channel_id=1, source_target_pairs={{0,17},{1,16},{2,19},{3,18},{4,21},{5,20},{6,23},{7,22},{8,25},{9,... | collective-permute-start | bytes 442376 | tf_op jit(solution)/shard_map/ppermute | solution.py:63
  78.6 0.3 collective-permute-start.17
  78.9 0.7 collective-permute-start.16
  79.6 2.5 %collective-permute-done.18.refs_3_ = bf16[4,144,128]{2,1,0:T(8,128)(2,1)S(1)} collective-permute-done((bf16[4,144,128]{2,1,0:T(8,128)(2,1)S(1)}, bf16[4,144,128]{2,1,0:T(8,128)(2,1)S(1)}, u32[]{:S(2)}, u32[]{:S(2)}) %collective-permute-start.18) | collective-permute-done | bytes 147488 | tf_op jit(solution)/shard_map/ppermute | solution.py:63
  82.2 1.6 %collective-permute-done.17.refs_2_ = bf16[4,144,128]{2,1,0:T(8,128)(2,1)S(1)} collective-permute-done((bf16[4,144,128]{2,1,0:T(8,128)(2,1)S(1)}, bf16[4,144,128]{2,1,0:T(8,128)(2,1)S(1)}, u32[]{:S(2)}, u32[]{:S(2)}) %collective-permute-start.17) | collective-permute-done | bytes 147488 | tf_op jit(solution)/shard_map/ppermute | solution.py:63
  83.8 0.3 collective-permute-done.16.refs_1_
  84.0 0.2 collective-permute-start.20
  84.4 0.7 collective-permute-done.21.refs_6_
  85.1 0.3 collective-permute-done.20.refs_5_
  85.4 2.0 %spread.1 = (f32[9,128,128]{2,1,0:T(8,128)}, f32[9,128,128]{2,1,0:T(8,128)}, f32[128,128]{1,0:T(8,128)}, f32[128,256]{1,0:T(8,128)}, f32[256,256]{1,0:T(8,128)},...) custom-call(s32[10]{0:T(128)S(1)} %stack.55.place, ...), custom_call_target="tpu_custom_call" | custom-call | tf_op jit(solution)/shard_map/spread/pallas_call | solution.py:606
  87.4 0.7 copy.28
  (56 shorter events, 1.1 us)
Async XLA Ops:
  0.6 3.0 %copy-start = (bf16[32,64,128]{2,1,0:T(8,128)(2,1)S(1)}, bf16[32,64,128]{2,1,0:T(8,128)(2,1)}, u32[]{:S(2)}) copy-start(bf16[32,64,128]{2,1,0:T(8,128)(2,1)} %param.13) | copy-start | bytes 1572868
  0.6 3.8 %copy-start.2 = (bf16[64,16,128]{2,1,0:T(8,128)(2,1)S(1)}, bf16[64,16,128]{2,1,0:T(8,128)(2,1)}, u32[]{:S(2)}) copy-start(bf16[64,16,128]{2,1,0:T(8,128)(2,1)} %xy.1) | copy-start | bytes 786436
  2.1 16.3 %collective-permute-start.3 = (bf16[1,4,128]{2,1,0:T(4,128)(2,1)S(1)}, bf16[1,4,128]{2,1,0:T(4,128)(2,1)S(1)}, u32[]{:S(2)}, u32[]{:S(2)}) collective-permute-start(bf16[1,4,128]{2,1,0:T(4,128)(2,1)S(1)} %dynamic-slice_select_fusion), channel_id=1, source_target_pairs={{1,8},{2,1},{3,16},{4,9},{5,24},{6,17},{9,10},{10,3},{11,18},{12,1... | collective-permute-start | bytes 3080 | tf_op jit(solution)/shard_map/ppermute | solution.py:63
  3.7 0.8 copy-start.6
  3.8 14.5 %collective-permute-start.2 = (bf16[48,4,128]{2,1,0:T(4,128)(2,1)S(1)}, bf16[48,4,128]{2,1,0:T(4,128)(2,1)S(1)}, u32[]{:S(2)}, u32[]{:S(2)}) collective-permute-start(bf16[48,4,128]{2,1,0:T(4,128)(2,1)S(1)} %pad_maximum_fusion.5), channel_id=1, source_target_pairs={{0,0},{1,1},{2,8},{3,9},{4,16},{5,17},{6,24},{7,25},{8,2},{9,3},{1... | collective-permute-start | bytes 147464 | tf_op jit(solution)/shard_map/ppermute | solution.py:63
  4.9 12.0 %collective-permute-start = (bf16[4,16,128]{2,1,0:T(8,128)(2,1)S(1)}, bf16[4,16,128]{2,1,0:T(8,128)(2,1)S(1)}, u32[]{:S(2)}, u32[]{:S(2)}) collective-permute-start(bf16[4,16,128]{2,1,0:T(8,128)(2,1)S(1)} %fusion.2), channel_id=1, source_target_pairs={{0,8},{1,9},{2,10},{3,11},{4,12},{5,13},{6,14},{7,15},{8,16},{9,17... | collective-permute-start | bytes 49160 | tf_op jit(solution)/shard_map/ppermute | solution.py:63
  13.8 4.4 %collective-permute-start.1 = (bf16[4,16,128]{2,1,0:T(8,128)(2,1)S(1)}, bf16[4,16,128]{2,1,0:T(8,128)(2,1)S(1)}, u32[]{:S(2)}, u32[]{:S(2)}) collective-permute-start(bf16[4,16,128]{2,1,0:T(8,128)(2,1)S(1)} %fusion.3), channel_id=1, source_target_pairs={{8,0},{9,1},{10,2},{11,3},{12,4},{13,5},{14,6},{15,7},{16,8},{17,9... | collective-permute-start | bytes 49160 | tf_op jit(solution)/shard_map/ppermute | solution.py:63
  15.2 0.8 copy-start.7
  16.1 0.7 copy-start.8
  18.4 6.1 %copy-start.1 = (bf16[3,3,128,128]{3,2,1,0:T(8,128)(2,1)S(1)}, bf16[3,3,128,128]{3,2,1,0:T(8,128)(2,1)}, u32[]{:S(2)}) copy-start(bf16[3,3,128,128]{3,2,1,0:T(8,128)(2,1)} %param.17) | copy-start | bytes 884740
  18.6 6.6 %collective-permute-start.5 = (bf16[103,4,128]{2,1,0:T(4,128)(2,1)S(1)}, bf16[103,4,128]{2,1,0:T(4,128)(2,1)S(1)}, u32[]{:S(2)}, u32[]{:S(2)}) collective-permute-start(bf16[103,4,128]{2,1,0:T(4,128)(2,1)S(1)} %get-tuple-element.72), channel_id=1, source_target_pairs={{1,0},{2,1},{3,2},{4,3},{5,4},{6,5},{7,6},{9,8},{10,9},{11,10},{12... | collective-permute-start | bytes 316424 | tf_op jit(solution)/shard_map/ppermute | solution.py:63
  19.9 7.9 %collective-permute-start.4 = (bf16[103,4,128]{2,1,0:T(4,128)(2,1)S(1)}, bf16[103,4,128]{2,1,0:T(4,128)(2,1)S(1)}, u32[]{:S(2)}, u32[]{:S(2)}) collective-permute-start(bf16[103,4,128]{2,1,0:T(4,128)(2,1)S(1)} %get-tuple-element.73), channel_id=1, source_target_pairs={{0,1},{1,2},{2,3},{3,4},{4,5},{5,6},{6,7},{8,9},{9,10},{10,11},{11... | collective-permute-start | bytes 316424 | tf_op jit(solution)/shard_map/ppermute | solution.py:63
  24.5 3.3 %copy-start.3 = (bf16[3,3,128,128]{3,2,1,0:T(8,128)(2,1)S(1)}, bf16[3,3,128,128]{3,2,1,0:T(8,128)(2,1)}, u32[]{:S(2)}) copy-start(bf16[3,3,128,128]{3,2,1,0:T(8,128)(2,1)} %param.16) | copy-start | bytes 884740
  24.5 3.3 %copy-start.5 = (bf16[128,256]{1,0:T(8,128)(2,1)S(1)}, bf16[128,256]{1,0:T(8,128)(2,1)}, u32[]{:S(2)}) copy-start(bf16[128,256]{1,0:T(8,128)(2,1)} %w1.1) | copy-start | bytes 196612
  24.8 3.0 %copy-start.4 = (bf16[256,256]{1,0:T(8,128)(2,1)S(1)}, bf16[256,256]{1,0:T(8,128)(2,1)}, u32[]{:S(2)}) copy-start(bf16[256,256]{1,0:T(8,128)(2,1)} %w2.1) | copy-start | bytes 393220
  44.8 2.8 %collective-permute-start.6 = (bf16[4,4,128,128]{3,2,1,0:T(8,128)(2,1)S(1)}, bf16[4,4,128,128]{3,2,1,0:T(8,128)(2,1)S(1)}, u32[]{:S(2)}, u32[]{:S(2)}) collective-permute-start(bf16[4,4,128,128]{3,2,1,0:T(8,128)(2,1)S(1)} %get-tuple-element.31), channel_id=1, source_target_pairs={{0,8},{1,9},{2,10},{3,11},{4,12},{5,13},{6,14},{7,15},{8,0},{9,1},... | collective-permute-start | bytes 1572872 | tf_op jit(solution)/shard_map/ppermute | solution.py:63
  47.7 6.3 %collective-permute-start.7 = (bf16[4,128,128]{2,1,0:T(8,128)(2,1)S(1)}, bf16[4,128,128]{2,1,0:T(8,128)(2,1)S(1)}, u32[]{:S(2)}, u32[]{:S(2)}) collective-permute-start(bf16[4,128,128]{2,1,0:T(8,128)(2,1)S(1)} %get-tuple-element.33), channel_id=1, source_target_pairs={{0,1},{1,0},{2,3},{3,2},{4,5},{5,4},{6,7},{7,6},{8,9},{9,8},{10,11... | collective-permute-start | bytes 393224 | tf_op jit(solution)/shard_map/ppermute | solution.py:63
  49.9 6.7 %collective-permute-start.8 = (bf16[4,128,128]{2,1,0:T(8,128)(2,1)S(1)}, bf16[4,128,128]{2,1,0:T(8,128)(2,1)S(1)}, u32[]{:S(2)}, u32[]{:S(2)}) collective-permute-start(bf16[4,128,128]{2,1,0:T(8,128)(2,1)S(1)} %get-tuple-element.34), channel_id=1, source_target_pairs={{0,16},{1,17},{2,18},{3,19},{4,20},{5,21},{6,22},{7,23},{8,24},{9,... | collective-permute-start | bytes 393224 | tf_op jit(solution)/shard_map/ppermute | solution.py:63
  52.3 6.1 %collective-permute-start.9 = (bf16[4,128,128]{2,1,0:T(8,128)(2,1)S(1)}, bf16[4,128,128]{2,1,0:T(8,128)(2,1)S(1)}, u32[]{:S(2)}, u32[]{:S(2)}) collective-permute-start(bf16[4,128,128]{2,1,0:T(8,128)(2,1)S(1)} %get-tuple-element.35), channel_id=1, source_target_pairs={{0,17},{1,16},{2,19},{3,18},{4,21},{5,20},{6,23},{7,22},{8,25},{9,... | collective-permute-start | bytes 393224 | tf_op jit(solution)/shard_map/ppermute | solution.py:63
  58.5 4.8 %collective-permute-start.10 = (bf16[144,128]{1,0:T(8,128)(2,1)S(1)}, bf16[144,128]{1,0:T(8,128)(2,1)S(1)}, u32[]{:S(2)}, u32[]{:S(2)}) collective-permute-start(bf16[144,128]{1,0:T(8,128)(2,1)S(1)} %get-tuple-element.37), channel_id=1, source_target_pairs={{0,2},{1,3},{2,0},{3,1},{4,6},{5,7},{6,4},{7,5},{8,10},{9,11},{10,... | collective-permute-start | bytes 110600 | tf_op jit(solution)/shard_map/ppermute | solution.py:63
  60.8 5.2 %collective-permute-start.11 = (bf16[144,128]{1,0:T(8,128)(2,1)S(1)}, bf16[144,128]{1,0:T(8,128)(2,1)S(1)}, u32[]{:S(2)}, u32[]{:S(2)}) collective-permute-start(bf16[144,128]{1,0:T(8,128)(2,1)S(1)} %get-tuple-element.38), channel_id=1, source_target_pairs={{0,4},{1,5},{2,6},{3,7},{4,0},{5,1},{6,2},{7,3},{8,12},{9,13},{10,... | collective-permute-start | bytes 110600 | tf_op jit(solution)/shard_map/ppermute | solution.py:63
  62.2 5.8 %collective-permute-start.12 = (bf16[144,128]{1,0:T(8,128)(2,1)S(1)}, bf16[144,128]{1,0:T(8,128)(2,1)S(1)}, u32[]{:S(2)}, u32[]{:S(2)}) collective-permute-start(bf16[144,128]{1,0:T(8,128)(2,1)S(1)} %get-tuple-element.39), channel_id=1, source_target_pairs={{0,6},{1,7},{2,4},{3,5},{4,2},{5,3},{6,0},{7,1},{8,14},{9,15},{10,... | collective-permute-start | bytes 110600 | tf_op jit(solution)/shard_map/ppermute | solution.py:63
  68.5 4.5 %collective-permute-start.13 = (bf16[144,128]{1,0:T(8,128)(2,1)S(1)}, bf16[144,128]{1,0:T(8,128)(2,1)S(1)}, u32[]{:S(2)}, u32[]{:S(2)}) collective-permute-start(bf16[144,128]{1,0:T(8,128)(2,1)S(1)} %get-tuple-element.41), channel_id=1, source_target_pairs={{0,2},{1,3},{2,0},{3,1},{4,6},{5,7},{6,4},{7,5},{8,10},{9,11},{10,... | collective-permute-start | bytes 110600 | tf_op jit(solution)/shard_map/ppermute | solution.py:63
  68.6 4.9 %collective-permute-start.14 = (bf16[144,128]{1,0:T(8,128)(2,1)S(1)}, bf16[144,128]{1,0:T(8,128)(2,1)S(1)}, u32[]{:S(2)}, u32[]{:S(2)}) collective-permute-start(bf16[144,128]{1,0:T(8,128)(2,1)S(1)} %get-tuple-element.42), channel_id=1, source_target_pairs={{0,4},{1,5},{2,6},{3,7},{4,0},{5,1},{6,2},{7,3},{8,12},{9,13},{10,... | collective-permute-start | bytes 110600 | tf_op jit(solution)/shard_map/ppermute | solution.py:63
  70.3 5.8 %collective-permute-start.15 = (bf16[144,128]{1,0:T(8,128)(2,1)S(1)}, bf16[144,128]{1,0:T(8,128)(2,1)S(1)}, u32[]{:S(2)}, u32[]{:S(2)}) collective-permute-start(bf16[144,128]{1,0:T(8,128)(2,1)S(1)} %get-tuple-element.43), channel_id=1, source_target_pairs={{0,6},{1,7},{2,4},{3,5},{4,2},{5,3},{6,0},{7,1},{8,14},{9,15},{10,... | collective-permute-start | bytes 110600 | tf_op jit(solution)/shard_map/ppermute | solution.py:63
  76.0 6.1 %collective-permute-start.18 = (bf16[4,144,128]{2,1,0:T(8,128)(2,1)S(1)}, bf16[4,144,128]{2,1,0:T(8,128)(2,1)S(1)}, u32[]{:S(2)}, u32[]{:S(2)}) collective-permute-start(bf16[4,144,128]{2,1,0:T(8,128)(2,1)S(1)} %pad_maximum_fusion.refs_0_), channel_id=1, source_target_pairs={{0,17},{1,16},{2,19},{3,18},{4,21},{5,20},{6,23},{7,22},{8,25},{9,... | collective-permute-start | bytes 442376 | tf_op jit(solution)/shard_map/ppermute | solution.py:63
  78.6 5.1 %collective-permute-start.17 = (bf16[4,144,128]{2,1,0:T(8,128)(2,1)S(1)}, bf16[4,144,128]{2,1,0:T(8,128)(2,1)S(1)}, u32[]{:S(2)}, u32[]{:S(2)}) collective-permute-start(bf16[4,144,128]{2,1,0:T(8,128)(2,1)S(1)} %pad_maximum_fusion.refs_0_), channel_id=1, source_target_pairs={{0,16},{1,17},{2,18},{3,19},{4,20},{5,21},{6,22},{7,23},{8,24},{9,... | collective-permute-start | bytes 442376 | tf_op jit(solution)/shard_map/ppermute | solution.py:63
  78.9 5.1 %collective-permute-start.16 = (bf16[4,144,128]{2,1,0:T(8,128)(2,1)S(1)}, bf16[4,144,128]{2,1,0:T(8,128)(2,1)S(1)}, u32[]{:S(2)}, u32[]{:S(2)}) collective-permute-start(bf16[4,144,128]{2,1,0:T(8,128)(2,1)S(1)} %pad_maximum_fusion.refs_0_), channel_id=1, source_target_pairs={{0,1},{1,0},{2,3},{3,2},{4,5},{5,4},{6,7},{7,6},{8,9},{9,8},{10,11... | collective-permute-start | bytes 442376 | tf_op jit(solution)/shard_map/ppermute | solution.py:63
  79.6 4.8 %collective-permute-start.19 = (bf16[4,144,128]{2,1,0:T(8,128)(2,1)S(1)}, bf16[4,144,128]{2,1,0:T(8,128)(2,1)S(1)}, u32[]{:S(2)}, u32[]{:S(2)}) collective-permute-start(bf16[4,144,128]{2,1,0:T(8,128)(2,1)S(1)} %pad_maximum_fusion.refs_0_), channel_id=1, source_target_pairs={{0,8},{1,9},{2,10},{3,11},{4,12},{5,13},{6,14},{7,15},{8,0},{9,1},... | collective-permute-start | bytes 442376 | tf_op jit(solution)/shard_map/ppermute | solution.py:63
  82.2 2.2 %collective-permute-start.22 = (bf16[4,144,128]{2,1,0:T(8,128)(2,1)S(1)}, bf16[4,144,128]{2,1,0:T(8,128)(2,1)S(1)}, u32[]{:S(2)}, u32[]{:S(2)}) collective-permute-start(bf16[4,144,128]{2,1,0:T(8,128)(2,1)S(1)} %collective-permute-done.18.refs_3_), channel_id=1, source_target_pairs={{0,8},{1,9},{2,10},{3,11},{4,12},{5,13},{6,14},{7,15},{8,0},{9,1},... | collective-permute-start | bytes 442376 | tf_op jit(solution)/shard_map/ppermute | solution.py:63
  83.8 1.4 %collective-permute-start.21 = (bf16[4,144,128]{2,1,0:T(8,128)(2,1)S(1)}, bf16[4,144,128]{2,1,0:T(8,128)(2,1)S(1)}, u32[]{:S(2)}, u32[]{:S(2)}) collective-permute-start(bf16[4,144,128]{2,1,0:T(8,128)(2,1)S(1)} %collective-permute-done.17.refs_2_), channel_id=1, source_target_pairs={{0,8},{1,9},{2,10},{3,11},{4,12},{5,13},{6,14},{7,15},{8,0},{9,1},... | collective-permute-start | bytes 442376 | tf_op jit(solution)/shard_map/ppermute | solution.py:63
  84.0 1.4 %collective-permute-start.20 = (bf16[4,144,128]{2,1,0:T(8,128)(2,1)S(1)}, bf16[4,144,128]{2,1,0:T(8,128)(2,1)S(1)}, u32[]{:S(2)}, u32[]{:S(2)}) collective-permute-start(bf16[4,144,128]{2,1,0:T(8,128)(2,1)S(1)} %collective-permute-done.16.refs_1_), channel_id=1, source_target_pairs={{0,8},{1,9},{2,10},{3,11},{4,12},{5,13},{6,14},{7,15},{8,0},{9,1},... | collective-permute-start | bytes 442376 | tf_op jit(solution)/shard_map/ppermute | solution.py:63

commit v5 on v4

--- a/solution.py
+++ b/solution.py
@@ -126,6 +126,8 @@
     acts,
     xyds,
     dx,
+    das,
+    paired,
     patch,
     xzs,
     yzs,
@@ -138,7 +140,7 @@
     packed,
 ):
     nrows, ncols, width = xy.shape
-    depth = labels.shape[2]
+    depth = labels.shape[1]
     hidden = w1.shape[1]
     share = nrows // 2
     side, core = place[0], place[5]
@@ -162,9 +164,24 @@
                 patch[0:count, tap : tap + width] = piece.reshape(count, width).astype(BF16)
         return count
 
-    n1 = gather(xs, 0, 0, nrows + 4, PITCH)
-    h1 = dot(patch[0:n1], conv1[...]) + temb[...]
-    h1 = h1.reshape(nrows + 4, PITCH, width)
+    def pair_rows(source, weight, out, rows, cols):
+        span, inner = 3 * width, rows // 2
+        count = inner * cols
+        paired[0 : 3 * span, 0:width] = weight[...]
+        paired[3 * span : 4 * span, 0:width] = jnp.zeros((span, width), BF16)
+        paired[0:span, width : 2 * width] = jnp.zeros((span, width), BF16)
+        paired[span : 4 * span, width : 2 * width] = weight[...]
+        for a in range(4):
+            for b in range(3):
+                piece = source[pl.ds(a, inner, stride=2), b : b + cols, :]
+                tap = (3 * a + b) * width
+                patch[0:count, tap : tap + width] = piece.reshape(count, width).astype(BF16)
+        both = dot(patch[0:count, 0 : 4 * span], paired[...])
+        out[pl.ds(0, inner, stride=2)] = both[:, 0:width].reshape(inner, cols, width)
+        out[pl.ds(1, inner, stride=2)] = both[:, width : 2 * width].reshape(inner, cols, width)
+
+    pair_rows(xs, conv1, hs, nrows + 4, PITCH)
+    h1 = hs[...] + temb[...][None]
     hs[...] = h1
     row = lax.broadcasted_iota(jnp.int32, h1.shape, 0)
     col = lax.broadcasted_iota(jnp.int32, h1.shape, 1)
@@ -176,9 +193,8 @@
     a1 = jnp.where(inside, h1 * sigmoid(h1), 0.0)
     acts[...] = jnp.zeros_like(acts)
     acts[:, 0:PITCH] = a1.astype(BF16).astype(F32)
-    n2 = gather(acts, 0, 0, nrows + 2, PITCH)
-    xyd = dot(patch[0:n2], conv2[...])
-    xyds[...] = xyd.astype(BF16).astype(F32).reshape(nrows + 2, PITCH, width)
+    pair_rows(acts, conv2, xyds, nrows + 2, PITCH)
+    xyds[...] = xyds[...].astype(BF16).astype(F32)
 
     rows_before = before[tall : tall + share + 1].astype(F32)
     rows_after = after[tall : tall + share + 1].astype(F32)
@@ -197,44 +213,53 @@
         xz_below.append(jnp.where(side == 0, rim_second, rim_same))
 
     def decode(feat, label):
+        pixels = feat.shape[0] // depth
         u1 = dot(feat, w1[...])
         g1, s1 = silu_pair(u1)
         g1 = g1.astype(BF16)
         u2 = dot(g1, w2[...])
         g2, s2 = silu_pair(u2)
         g2 = g2.astype(BF16)
-        logits = dot(g2, w3[...])
-        lane = lax.broadcasted_iota(jnp.int32, logits.shape, 1)
-        logits = jnp.where(lane < classes, logits, -jnp.inf)
-        power = jnp.exp(logits - jnp.max(logits, axis=1, keepdims=True))
-        prob = power / jnp.sum(power, axis=1, keepdims=True)
-        onehot = jnp.where(lane == label, 1.0, 0.0)
-        dlogits = (loss_weight * (prob - onehot)).astype(BF16)
-        du2 = (dot_nt(dlogits, w3[...]) * s2).astype(BF16)
+        logits = dot(g2[0:pixels], w3[0])
+        for k in range(1, depth):
+            logits = logits + dot(g2[k * pixels : (k + 1) * pixels], w3[k])
+        turned = logits.T
+        outs = []
+        for k in range(depth):
+            part = turned[k * CLASS_ROWS : (k + 1) * CLASS_ROWS]
+            lane = lax.broadcasted_iota(jnp.int32, part.shape, 0)
+            part = jnp.where(lane < classes, part, -jnp.inf)
+            power = jnp.exp(part - jnp.max(part, axis=0, keepdims=True))
+            prob = power / jnp.sum(power, axis=0, keepdims=True)
+            onehot = jnp.where(lane.astype(F32) == label[k : k + 1], 1.0, 0.0)
+            outs.append(loss_weight * (prob - onehot))
+        turned = jnp.concatenate(outs, axis=0)
+        dlogits = turned.T.astype(BF16)
+        dg2 = jnp.concatenate([dot_nt(dlogits, w3[k]) for k in range(depth)], axis=0)
+        du2 = (dg2 * s2).astype(BF16)
         du1 = (dot_nt(du2, w2[...]) * s1).astype(BF16)
-        return g1, g2, dlogits, du2, du1, dot_nt(du1, w1[...])
+        return g1, g2, turned.astype(BF16), du2, du1, dot_nt(du1, w1[...])
 
     dw1[...] = jnp.zeros_like(dw1)
     dw2[...] = jnp.zeros_like(dw2)
     dw3[...] = jnp.zeros_like(dw3)
     dyz[...] = jnp.zeros_like(dyz)
     dx[...] = jnp.zeros_like(dx)
-    chunk = 16
+    chunk = nrows // labels.shape[0]
     size = chunk * ncols
 
     def step(index, carry):
         r0 = pl.multiple_of(index * chunk, chunk)
         tile = xyds[pl.ds(r0 + 1, chunk), 1 : ncols + 1, :]
-        lab = labels[pl.ds(r0, chunk)].reshape(size, depth)
-        feats, labs = [], []
+        feats = []
         for k in range(depth):
             xz_k = xzs[k, pl.ds(r0, chunk), :]
             feat = tile + xz_k[:, None, :] + yzs[k][None]
             feats.append(feat.reshape(size, width).astype(BF16))
-            labs.append(jnp.broadcast_to(lab[:, k : k + 1], (size, LANES)))
         feat = jnp.concatenate(feats, axis=0)
-        g1, g2, dlogits, du2, du1, dfeat = decode(feat, jnp.concatenate(labs, axis=0))
-        dw3[...] += dot_tn(dlogits, g2)
+        g1, g2, dlogits, du2, du1, dfeat = decode(feat, labels[index])
+        for k in range(depth):
+            dw3[...] += dot(dlogits[k * CLASS_ROWS : (k + 1) * CLASS_ROWS], g2[k * size : (k + 1) * size])
         dw2[...] += dot_tn(g1, du2)
         dw1[...] += dot_tn(feat, du1)
         total = jnp.zeros((chunk, ncols, width), F32)
@@ -246,13 +271,15 @@
         dx[pl.ds(r0 + 1, chunk), 1 : ncols + 1, :] = total.astype(BF16).astype(F32)
         return carry
 
-    lax.fori_loop(0, nrows // chunk, step, 0)
-
-    lab_before = before[2 : nrows + 4, 3, :].astype(F32).astype(jnp.int32)
-    lab_after = after[2 : nrows + 4, 3, :].astype(F32).astype(jnp.int32)
-    lab_up = above[3].astype(F32).astype(jnp.int32)
-    lab_down = below[3].astype(F32).astype(jnp.int32)
-    tail = jnp.zeros((PITCH - ncols - 2, LANES), jnp.int32)
+    lax.fori_loop(0, nrows // chunk, step, 0, unroll=True)
+
+    lab_before = before[2 : nrows + 4, 3, :].astype(F32)
+    lab_after = after[2 : nrows + 4, 3, :].astype(F32)
+    lab_up = above[3].astype(F32)
+    lab_down = below[3].astype(F32)
+    tail = jnp.zeros((PITCH - ncols - 2, LANES), F32)
+    span = 2 * PITCH + 2 * nrows
+    fill = -span % LANES
     lab_rim = jnp.concatenate(
         [
             lab_before[0:1],
@@ -265,11 +292,12 @@
             tail,
             lab_before[1 : nrows + 1],
             lab_after[1 : nrows + 1],
+            jnp.zeros((fill, LANES), F32),
         ],
         axis=0,
     )
     rim_at = (0, 1, nrows + 2 * REACH - 2, nrows + 2 * REACH - 1)
-    feats, labs = [], []
+    feats = []
     zero_tail = jnp.zeros((PITCH - ncols - 2, width), F32)
     for k in range(depth):
         yz_before = before[rim_at[k], 3:4, :].astype(F32)
@@ -279,12 +307,12 @@
         feats.append(xyds[nrows + 1] + xz_below[k] + yz_row)
         feats.append(xyds[1 : nrows + 1, 0, :] + xzs[k] + yz_before)
         feats.append(xyds[1 : nrows + 1, ncols + 1, :] + xzs[k] + yz_after)
-        labs.append(jnp.broadcast_to(lab_rim[:, k : k + 1], (2 * PITCH + 2 * nrows, LANES)))
-    rim = decode(jnp.concatenate(feats, axis=0).astype(BF16), jnp.concatenate(labs, axis=0))[-1]
-    span = 2 * PITCH + 2 * nrows
+        feats.append(jnp.zeros((fill, width), F32))
+    rim = decode(jnp.concatenate(feats, axis=0).astype(BF16), lab_rim.T[0:8])[-1]
+    whole_span = span + fill
     rim_sum = rim[0:span]
     for k in range(1, depth):
-        rim_sum = rim_sum + rim[k * span : (k + 1) * span]
+        rim_sum = rim_sum + rim[k * whole_span : k * whole_span + span]
     rim_sum = rim_sum.astype(BF16).astype(F32)
     rcol = lax.broadcasted_iota(jnp.int32, (PITCH, width), 0)
     keep = (rcol >= jnp.where(open_left, 0, 1)) & (rcol < jnp.where(open_right, ncols + 2, ncols + 1))
@@ -309,8 +337,8 @@
     n3 = gather(acts, 1, 1, nrows, ncols)
     dxyd = dx[1 : nrows + 1, 1 : ncols + 1, :].reshape(n3, width).astype(BF16)
     weight_gradient(shares.at["conv2"], dxyd)
-    gather(dx, 0, 0, nrows, ncols)
-    da1 = dot(patch[0:n3], back[...])
+    pair_rows(dx, back, das, nrows, ncols)
+    da1 = das[...].reshape(n3, width)
     _, slope = silu_pair(hs[2 : nrows + 2, 2 : ncols + 2, :].reshape(n3, width))
     dh1 = (da1 * slope).astype(BF16)
     gather(xs, 2, 2, nrows, ncols)
@@ -469,7 +497,11 @@
     flat_one = conv1_weight.reshape(9 * width, width)
     flat_two = conv2_weight.reshape(9 * width, width)
     back_flat = jnp.transpose(conv2_weight[::-1, ::-1], (0, 1, 3, 2)).reshape(9 * width, width)
-    w3_wide = jnp.pad(w3, ((0, 0), (0, LANES - classes)))
+    w3_wide = jnp.stack(
+        [jnp.pad(w3, ((0, 0), (CLASS_ROWS * k, LANES - classes - CLASS_ROWS * k))) for k in range(depth)]
+    )
+    chunks = nrows // 16
+    labels_by_depth = labels.astype(F32).reshape(chunks, -1, depth).transpose(0, 2, 1)
 
     up = lambda i, j: (i + 1, j)
     down = lambda i, j: (i - 1, j)
@@ -539,12 +571,14 @@
             pltpu.VMEM((nrows + 4, 32, width), F32),
             pltpu.VMEM((nrows + 2, PITCH, width), F32),
             pltpu.VMEM((nrows + 2, PITCH, width), F32),
-            pltpu.VMEM(((nrows + 4) * PITCH, 9 * width), BF16),
+            pltpu.VMEM((nrows, ncols, width), F32),
+            pltpu.VMEM((12 * width, 2 * width), BF16),
+            pltpu.VMEM((nrows * ncols, 12 * width), BF16),
             pltpu.VMEM((depth, nrows, width), F32),
             pltpu.VMEM((depth, ncols, width), F32),
             pltpu.VMEM((width, hidden), F32),
             pltpu.VMEM((hidden, hidden), F32),
-            pltpu.VMEM((LANES, hidden), F32),
+            pltpu.VMEM((CLASS_ROWS, hidden), F32),
             pltpu.VMEM((depth, nrows, width), F32),
             pltpu.VMEM((depth, ncols, width), F32),
             pltpu.VMEM((nrows * depth, width), F32),
@@ -559,7 +593,7 @@
         below,
         before,
         after,
-        labels,
+        labels_by_depth,
         first,
         rim_row,
         temb.reshape(1, width),

time: 88.5 us -> 87.4 us (0.988)
  Pallas kernels: 19.7 us -> 17.5 us
  starting transfers between devices: 36.2 us -> 37.2 us
    pallas_call x1, Pallas kernels: 16.9 us -> 14.7 us  [local(): pl.pallas_call(functools.partial(main_kernel, classes, shares), out_shape...]
    ppermute x23, starting transfers between devices: 36.2 us -> 37.2 us  [move(): return lax.ppermute(array, BOTH, pairs)]
where the time goes in v5:
time: 87.4 us; the launch traced here: 86.9 us
  starting transfers between devices  37.2 us (43%)
  waiting for transfers between devices  24.5 us (28%)
  Pallas kernels  17.5 us (20%)
  local copies, waits for them, and re-layouts  4.48 us (5%)
  between operations  1.87 us (2%)
  other arithmetic  1.17 us (1%)
    ppermute x23, starting transfers between devices, move(): return lax.ppermute(array, BOTH, pairs)  37.2 us
    ppermute x23, waiting for transfers between devices, move(): return lax.ppermute(array, BOTH, pairs)  24.5 us
    pallas_call x1, Pallas kernels, local(): pl.pallas_call(functools.partial(main_kernel, classes, shares), out_shape...  14.7 us
    unnamed x27, local copies, waits for them, and re-layouts  2.62 us
    pallas_call x1, Pallas kernels, local(): pl.pallas_call(functools.partial(last_kernel, shares, classes), out_shape...  1.95 us
  transfers between devices with their start and end apart: 23, of which 16 were waited for; matrix products, arithmetic and copies ran while one was open for 3% of the time, Pallas kernels for 0%

profile of v5, /device:TPU:0, one launch (start us, length us, event | category | flops | bytes accessed | tf_op | source)
XLA Modules:
  0.0 86.9 jit_solution(3702228755440701981)
XLA Ops:
  1.4 0.7 dynamic-slice_select_fusion
  2.1 0.6 collective-permute-start.3
  2.8 0.9 constant_dynamic-slice_fusion
  3.8 0.7 collective-permute-start.2
  4.5 0.3 copy.31
  4.9 9.0 %collective-permute-start = (bf16[4,16,128]{2,1,0:T(8,128)(2,1)S(1)}, bf16[4,16,128]{2,1,0:T(8,128)(2,1)S(1)}, u32[]{:S(2)}, u32[]{:S(2)}) collective-permute-start(bf16[4,16,128]{2,1,0:T(8,128)(2,1)S(1)} %fusion.2), channel_id=1, source_target_pairs={{0,8},{1,9},{2,10},{3,11},{4,12},{5,13},{6,14},{7,15},{8,16},{9,17... | collective-permute-start | bytes 49160 | tf_op jit(solution)/shard_map/ppermute | solution.py:63
  14.0 1.3 %collective-permute-start.1 = (bf16[4,16,128]{2,1,0:T(8,128)(2,1)S(1)}, bf16[4,16,128]{2,1,0:T(8,128)(2,1)S(1)}, u32[]{:S(2)}, u32[]{:S(2)}) collective-permute-start(bf16[4,16,128]{2,1,0:T(8,128)(2,1)S(1)} %fusion.3), channel_id=1, source_target_pairs={{8,0},{9,1},{10,2},{11,3},{12,4},{13,5},{14,6},{15,7},{16,8},{17,9... | collective-permute-start | bytes 49160 | tf_op jit(solution)/shard_map/ppermute | solution.py:63
  15.5 0.6 copy-done.8
  16.0 0.1 copy.39
  16.3 0.6 copy-done.7
  17.1 0.1 pad_bitcast_fusion.3
  17.5 0.2 copy.38
  17.9 0.5 collective-permute-done.1.below
  18.6 0.2 pad_maximum_fusion.2
  18.8 1.4 %collective-permute-start.5 = (bf16[103,4,128]{2,1,0:T(4,128)(2,1)S(1)}, bf16[103,4,128]{2,1,0:T(4,128)(2,1)S(1)}, u32[]{:S(2)}, u32[]{:S(2)}) collective-permute-start(bf16[103,4,128]{2,1,0:T(4,128)(2,1)S(1)} %get-tuple-element.84), channel_id=1, source_target_pairs={{1,0},{2,1},{3,2},{4,3},{5,4},{6,5},{7,6},{9,8},{10,9},{11,10},{12... | collective-permute-start | bytes 316424 | tf_op jit(solution)/shard_map/ppermute | solution.py:63
  20.2 4.6 %collective-permute-start.4 = (bf16[103,4,128]{2,1,0:T(4,128)(2,1)S(1)}, bf16[103,4,128]{2,1,0:T(4,128)(2,1)S(1)}, u32[]{:S(2)}, u32[]{:S(2)}) collective-permute-start(bf16[103,4,128]{2,1,0:T(4,128)(2,1)S(1)} %get-tuple-element.85), channel_id=1, source_target_pairs={{0,1},{1,2},{2,3},{3,4},{4,5},{5,6},{6,7},{8,9},{9,10},{10,11},{11... | collective-permute-start | bytes 316424 | tf_op jit(solution)/shard_map/ppermute | solution.py:63
  24.8 0.7 collective-permute-done.5.after
  25.5 2.6 %collective-permute-done.4.before = bf16[103,4,128]{2,1,0:T(4,128)(2,1)S(1)} collective-permute-done((bf16[103,4,128]{2,1,0:T(4,128)(2,1)S(1)}, bf16[103,4,128]{2,1,0:T(4,128)(2,1)S(1)}, u32[]{:S(2)}, u32[]{:S(2)}) %collective-permute-start.4) | collective-permute-done | bytes 105504 | tf_op jit(solution)/shard_map/ppermute | solution.py:63
  28.1 14.7 %tile.1 = (bf16[4,4,128,128]{3,2,1,0:T(8,128)(2,1)S(1)}, bf16[4,4,128,128]{3,2,1,0:T(8,128)(2,1)S(1)}) custom-call(s32[10]{0:T(128)S(1)} %stack.70.place, bf16[64,16,128]{2,1,0:T(8,128)(2,1)S(1)} %copy-done.2, bf16[4,16,128]{2,1,0:T(8,128)(2,1)S(1)} %collective-permute-done.above, bf16[4,16,128]{2,1,0:T(8,128)(2,1)S(1)} %collective-permute-done.1.below, ...), custom_call_target="tpu_custom_call" | custom-call | tf_op jit(solution)/shard_map/tile/pallas_call | solution.py:563
  42.8 1.2 %collective-permute-start.6 = (bf16[4,4,128,128]{3,2,1,0:T(8,128)(2,1)S(1)}, bf16[4,4,128,128]{3,2,1,0:T(8,128)(2,1)S(1)}, u32[]{:S(2)}, u32[]{:S(2)}) collective-permute-start(bf16[4,4,128,128]{3,2,1,0:T(8,128)(2,1)S(1)} %get-tuple-element.31), channel_id=1, source_target_pairs={{0,8},{1,9},{2,10},{3,11},{4,12},{5,13},{6,14},{7,15},{8,0},{9,1},... | collective-permute-start | bytes 1572872 | tf_op jit(solution)/shard_map/ppermute | solution.py:63
  44.0 1.5 %collective-permute-done.6.other = bf16[4,4,128,128]{3,2,1,0:T(8,128)(2,1)S(1)} collective-permute-done((bf16[4,4,128,128]{3,2,1,0:T(8,128)(2,1)S(1)}, bf16[4,4,128,128]{3,2,1,0:T(8,128)(2,1)S(1)}, u32[]{:S(2)}, u32[]{:S(2)}) %collective-permute-start.6) | collective-permute-done | bytes 524320 | tf_op jit(solution)/shard_map/ppermute | solution.py:63
  45.6 0.1 cores.1
  45.7 2.3 %collective-permute-start.7 = (bf16[4,128,128]{2,1,0:T(8,128)(2,1)S(1)}, bf16[4,128,128]{2,1,0:T(8,128)(2,1)S(1)}, u32[]{:S(2)}, u32[]{:S(2)}) collective-permute-start(bf16[4,128,128]{2,1,0:T(8,128)(2,1)S(1)} %get-tuple-element.33), channel_id=1, source_target_pairs={{0,1},{1,0},{2,3},{3,2},{4,5},{5,4},{6,7},{7,6},{8,9},{9,8},{10,11... | collective-permute-start | bytes 393224 | tf_op jit(solution)/shard_map/ppermute | solution.py:63
  48.0 3.1 %collective-permute-start.8 = (bf16[4,128,128]{2,1,0:T(8,128)(2,1)S(1)}, bf16[4,128,128]{2,1,0:T(8,128)(2,1)S(1)}, u32[]{:S(2)}, u32[]{:S(2)}) collective-permute-start(bf16[4,128,128]{2,1,0:T(8,128)(2,1)S(1)} %get-tuple-element.34), channel_id=1, source_target_pairs={{0,16},{1,17},{2,18},{3,19},{4,20},{5,21},{6,22},{7,23},{8,24},{9,... | collective-permute-start | bytes 393224 | tf_op jit(solution)/shard_map/ppermute | solution.py:63
  51.1 0.9 %collective-permute-done.7.refs_1_ = bf16[4,128,128]{2,1,0:T(8,128)(2,1)S(1)} collective-permute-done((bf16[4,128,128]{2,1,0:T(8,128)(2,1)S(1)}, bf16[4,128,128]{2,1,0:T(8,128)(2,1)S(1)}, u32[]{:S(2)}, u32[]{:S(2)}) %collective-permute-start.7) | collective-permute-done | bytes 131104 | tf_op jit(solution)/shard_map/ppermute | solution.py:63
  52.0 3.4 %collective-permute-done.8.refs_2_ = bf16[4,128,128]{2,1,0:T(8,128)(2,1)S(1)} collective-permute-done((bf16[4,128,128]{2,1,0:T(8,128)(2,1)S(1)}, bf16[4,128,128]{2,1,0:T(8,128)(2,1)S(1)}, u32[]{:S(2)}, u32[]{:S(2)}) %collective-permute-start.8) | collective-permute-done | bytes 131104 | tf_op jit(solution)/shard_map/ppermute | solution.py:63
  55.4 1.8 %collective-permute-done.9.refs_3_ = bf16[4,128,128]{2,1,0:T(8,128)(2,1)S(1)} collective-permute-done((bf16[4,128,128]{2,1,0:T(8,128)(2,1)S(1)}, bf16[4,128,128]{2,1,0:T(8,128)(2,1)S(1)}, u32[]{:S(2)}, u32[]{:S(2)}) %collective-permute-start.9) | collective-permute-done | bytes 131104 | tf_op jit(solution)/shard_map/ppermute | solution.py:63
  57.3 2.4 %collective-permute-start.10 = (bf16[144,128]{1,0:T(8,128)(2,1)S(1)}, bf16[144,128]{1,0:T(8,128)(2,1)S(1)}, u32[]{:S(2)}, u32[]{:S(2)}) collective-permute-start(bf16[144,128]{1,0:T(8,128)(2,1)S(1)} %get-tuple-element.37), channel_id=1, source_target_pairs={{0,2},{1,3},{2,0},{3,1},{4,6},{5,7},{6,4},{7,5},{8,10},{9,11},{10,... | collective-permute-start | bytes 110600 | tf_op jit(solution)/shard_map/ppermute | solution.py:63
  59.7 1.4 %collective-permute-start.11 = (bf16[144,128]{1,0:T(8,128)(2,1)S(1)}, bf16[144,128]{1,0:T(8,128)(2,1)S(1)}, u32[]{:S(2)}, u32[]{:S(2)}) collective-permute-start(bf16[144,128]{1,0:T(8,128)(2,1)S(1)} %get-tuple-element.38), channel_id=1, source_target_pairs={{0,4},{1,5},{2,6},{3,7},{4,0},{5,1},{6,2},{7,3},{8,12},{9,13},{10,... | collective-permute-start | bytes 110600 | tf_op jit(solution)/shard_map/ppermute | solution.py:63
  61.1 1.0 %collective-permute-start.12 = (bf16[144,128]{1,0:T(8,128)(2,1)S(1)}, bf16[144,128]{1,0:T(8,128)(2,1)S(1)}, u32[]{:S(2)}, u32[]{:S(2)}) collective-permute-start(bf16[144,128]{1,0:T(8,128)(2,1)S(1)} %get-tuple-element.39), channel_id=1, source_target_pairs={{0,6},{1,7},{2,4},{3,5},{4,2},{5,3},{6,0},{7,1},{8,14},{9,15},{10,... | collective-permute-start | bytes 110600 | tf_op jit(solution)/shard_map/ppermute | solution.py:63
  62.1 2.7 %collective-permute-done.11.refs_2_ = bf16[144,128]{1,0:T(8,128)(2,1)S(1)} collective-permute-done((bf16[144,128]{1,0:T(8,128)(2,1)S(1)}, bf16[144,128]{1,0:T(8,128)(2,1)S(1)}, u32[]{:S(2)}, u32[]{:S(2)}) %collective-permute-start.11) | collective-permute-done | bytes 36896 | tf_op jit(solution)/shard_map/ppermute | solution.py:63
  64.8 2.0 %collective-permute-done.12.refs_3_ = bf16[144,128]{1,0:T(8,128)(2,1)S(1)} collective-permute-done((bf16[144,128]{1,0:T(8,128)(2,1)S(1)}, bf16[144,128]{1,0:T(8,128)(2,1)S(1)}, u32[]{:S(2)}, u32[]{:S(2)}) %collective-permute-start.12) | collective-permute-done | bytes 36896 | tf_op jit(solution)/shard_map/ppermute | solution.py:63
  66.9 0.6 layers.1
  67.5 1.6 %collective-permute-start.14 = (bf16[144,128]{1,0:T(8,128)(2,1)S(1)}, bf16[144,128]{1,0:T(8,128)(2,1)S(1)}, u32[]{:S(2)}, u32[]{:S(2)}) collective-permute-start(bf16[144,128]{1,0:T(8,128)(2,1)S(1)} %get-tuple-element.42), channel_id=1, source_target_pairs={{0,4},{1,5},{2,6},{3,7},{4,0},{5,1},{6,2},{7,3},{8,12},{9,13},{10,... | collective-permute-start | bytes 110600 | tf_op jit(solution)/shard_map/ppermute | solution.py:63
  69.1 2.8 %collective-permute-start.15 = (bf16[144,128]{1,0:T(8,128)(2,1)S(1)}, bf16[144,128]{1,0:T(8,128)(2,1)S(1)}, u32[]{:S(2)}, u32[]{:S(2)}) collective-permute-start(bf16[144,128]{1,0:T(8,128)(2,1)S(1)} %get-tuple-element.43), channel_id=1, source_target_pairs={{0,6},{1,7},{2,4},{3,5},{4,2},{5,3},{6,0},{7,1},{8,14},{9,15},{10,... | collective-permute-start | bytes 110600 | tf_op jit(solution)/shard_map/ppermute | solution.py:63
  71.9 0.5 collective-permute-done.14
  72.5 2.4 %collective-permute-done.15 = bf16[144,128]{1,0:T(8,128)(2,1)S(1)} collective-permute-done((bf16[144,128]{1,0:T(8,128)(2,1)S(1)}, bf16[144,128]{1,0:T(8,128)(2,1)S(1)}, u32[]{:S(2)}, u32[]{:S(2)}) %collective-permute-start.15) | collective-permute-done | bytes 36896 | tf_op jit(solution)/shard_map/ppermute | solution.py:63
  74.9 2.6 %collective-permute-start.18 = (bf16[4,144,128]{2,1,0:T(8,128)(2,1)S(1)}, bf16[4,144,128]{2,1,0:T(8,128)(2,1)S(1)}, u32[]{:S(2)}, u32[]{:S(2)}) collective-permute-start(bf16[4,144,128]{2,1,0:T(8,128)(2,1)S(1)} %pad_maximum_fusion.1.refs_0_), channel_id=1, source_target_pairs={{0,17},{1,16},{2,19},{3,18},{4,21},{5,20},{6,23},{7,22},{8,25},{9,... | collective-permute-start | bytes 442376 | tf_op jit(solution)/shard_map/ppermute | solution.py:63
  77.4 0.3 collective-permute-start.17
  77.7 0.7 collective-permute-start.16
  78.4 2.5 %collective-permute-done.18.refs_3_ = bf16[4,144,128]{2,1,0:T(8,128)(2,1)S(1)} collective-permute-done((bf16[4,144,128]{2,1,0:T(8,128)(2,1)S(1)}, bf16[4,144,128]{2,1,0:T(8,128)(2,1)S(1)}, u32[]{:S(2)}, u32[]{:S(2)}) %collective-permute-start.18) | collective-permute-done | bytes 147488 | tf_op jit(solution)/shard_map/ppermute | solution.py:63
  81.0 1.6 %collective-permute-done.17.refs_2_ = bf16[4,144,128]{2,1,0:T(8,128)(2,1)S(1)} collective-permute-done((bf16[4,144,128]{2,1,0:T(8,128)(2,1)S(1)}, bf16[4,144,128]{2,1,0:T(8,128)(2,1)S(1)}, u32[]{:S(2)}, u32[]{:S(2)}) %collective-permute-start.17) | collective-permute-done | bytes 147488 | tf_op jit(solution)/shard_map/ppermute | solution.py:63
  82.6 0.3 collective-permute-done.16.refs_1_
  82.9 0.2 collective-permute-start.20
  83.2 0.7 collective-permute-done.21.refs_6_
  84.0 0.3 collective-permute-done.20.refs_5_
  84.2 2.0 %spread.1 = (f32[9,128,128]{2,1,0:T(8,128)}, f32[9,128,128]{2,1,0:T(8,128)}, f32[128,128]{1,0:T(8,128)}, f32[128,256]{1,0:T(8,128)}, f32[256,256]{1,0:T(8,128)},...) custom-call(s32[10]{0:T(128)S(1)} %stack.70.place, ...), custom_call_target="tpu_custom_call" | custom-call | tf_op jit(solution)/shard_map/spread/pallas_call | solution.py:640
  86.2 0.7 copy.44
  (61 shorter events, 1.5 us)
Async XLA Ops:
  0.6 3.0 %copy-start = (bf16[32,64,128]{2,1,0:T(8,128)(2,1)S(1)}, bf16[32,64,128]{2,1,0:T(8,128)(2,1)}, u32[]{:S(2)}) copy-start(bf16[32,64,128]{2,1,0:T(8,128)(2,1)} %param.13) | copy-start | bytes 1572868
  0.6 3.8 %copy-start.2 = (bf16[64,16,128]{2,1,0:T(8,128)(2,1)S(1)}, bf16[64,16,128]{2,1,0:T(8,128)(2,1)}, u32[]{:S(2)}) copy-start(bf16[64,16,128]{2,1,0:T(8,128)(2,1)} %xy.1) | copy-start | bytes 786436
  2.1 16.5 %collective-permute-start.3 = (bf16[1,4,128]{2,1,0:T(4,128)(2,1)S(1)}, bf16[1,4,128]{2,1,0:T(4,128)(2,1)S(1)}, u32[]{:S(2)}, u32[]{:S(2)}) collective-permute-start(bf16[1,4,128]{2,1,0:T(4,128)(2,1)S(1)} %dynamic-slice_select_fusion), channel_id=1, source_target_pairs={{1,8},{2,1},{3,16},{4,9},{5,24},{6,17},{9,10},{10,3},{11,18},{12,1... | collective-permute-start | bytes 3080 | tf_op jit(solution)/shard_map/ppermute | solution.py:63
  3.7 0.8 copy-start.6
  3.8 14.6 %collective-permute-start.2 = (bf16[48,4,128]{2,1,0:T(4,128)(2,1)S(1)}, bf16[48,4,128]{2,1,0:T(4,128)(2,1)S(1)}, u32[]{:S(2)}, u32[]{:S(2)}) collective-permute-start(bf16[48,4,128]{2,1,0:T(4,128)(2,1)S(1)} %pad_maximum_fusion.6), channel_id=1, source_target_pairs={{0,0},{1,1},{2,8},{3,9},{4,16},{5,17},{6,24},{7,25},{8,2},{9,3},{1... | collective-permute-start | bytes 147464 | tf_op jit(solution)/shard_map/ppermute | solution.py:63
  4.9 11.3 %copy-start.1 = (bf16[3,3,128,128]{3,2,1,0:T(8,128)(2,1)S(1)}, bf16[3,3,128,128]{3,2,1,0:T(8,128)(2,1)}, u32[]{:S(2)}) copy-start(bf16[3,3,128,128]{3,2,1,0:T(8,128)(2,1)} %param.17) | copy-start | bytes 884740
  4.9 12.9 %collective-permute-start = (bf16[4,16,128]{2,1,0:T(8,128)(2,1)S(1)}, bf16[4,16,128]{2,1,0:T(8,128)(2,1)S(1)}, u32[]{:S(2)}, u32[]{:S(2)}) collective-permute-start(bf16[4,16,128]{2,1,0:T(8,128)(2,1)S(1)} %fusion.2), channel_id=1, source_target_pairs={{0,8},{1,9},{2,10},{3,11},{4,12},{5,13},{6,14},{7,15},{8,16},{9,17... | collective-permute-start | bytes 49160 | tf_op jit(solution)/shard_map/ppermute | solution.py:63
  14.0 4.4 %collective-permute-start.1 = (bf16[4,16,128]{2,1,0:T(8,128)(2,1)S(1)}, bf16[4,16,128]{2,1,0:T(8,128)(2,1)S(1)}, u32[]{:S(2)}, u32[]{:S(2)}) collective-permute-start(bf16[4,16,128]{2,1,0:T(8,128)(2,1)S(1)} %fusion.3), channel_id=1, source_target_pairs={{8,0},{9,1},{10,2},{11,3},{12,4},{13,5},{14,6},{15,7},{16,8},{17,9... | collective-permute-start | bytes 49160 | tf_op jit(solution)/shard_map/ppermute | solution.py:63
  15.3 0.7 copy-start.8
  16.2 0.8 copy-start.7
  18.8 9.3 %copy-start.3 = (bf16[3,3,128,128]{3,2,1,0:T(8,128)(2,1)S(1)}, bf16[3,3,128,128]{3,2,1,0:T(8,128)(2,1)}, u32[]{:S(2)}) copy-start(bf16[3,3,128,128]{3,2,1,0:T(8,128)(2,1)} %param.16) | copy-start | bytes 884740
  18.8 6.7 %collective-permute-start.5 = (bf16[103,4,128]{2,1,0:T(4,128)(2,1)S(1)}, bf16[103,4,128]{2,1,0:T(4,128)(2,1)S(1)}, u32[]{:S(2)}, u32[]{:S(2)}) collective-permute-start(bf16[103,4,128]{2,1,0:T(4,128)(2,1)S(1)} %get-tuple-element.84), channel_id=1, source_target_pairs={{1,0},{2,1},{3,2},{4,3},{5,4},{6,5},{7,6},{9,8},{10,9},{11,10},{12... | collective-permute-start | bytes 316424 | tf_op jit(solution)/shard_map/ppermute | solution.py:63
  20.2 7.9 %collective-permute-start.4 = (bf16[103,4,128]{2,1,0:T(4,128)(2,1)S(1)}, bf16[103,4,128]{2,1,0:T(4,128)(2,1)S(1)}, u32[]{:S(2)}, u32[]{:S(2)}) collective-permute-start(bf16[103,4,128]{2,1,0:T(4,128)(2,1)S(1)} %get-tuple-element.85), channel_id=1, source_target_pairs={{0,1},{1,2},{2,3},{3,4},{4,5},{5,6},{6,7},{8,9},{9,10},{10,11},{11... | collective-permute-start | bytes 316424 | tf_op jit(solution)/shard_map/ppermute | solution.py:63
  24.8 3.3 %copy-start.4 = (bf16[256,256]{1,0:T(8,128)(2,1)S(1)}, bf16[256,256]{1,0:T(8,128)(2,1)}, u32[]{:S(2)}) copy-start(bf16[256,256]{1,0:T(8,128)(2,1)} %w2.1) | copy-start | bytes 393220
  24.8 3.3 %copy-start.5 = (bf16[128,256]{1,0:T(8,128)(2,1)S(1)}, bf16[128,256]{1,0:T(8,128)(2,1)}, u32[]{:S(2)}) copy-start(bf16[128,256]{1,0:T(8,128)(2,1)} %w1.1) | copy-start | bytes 196612
  42.8 2.7 %collective-permute-start.6 = (bf16[4,4,128,128]{3,2,1,0:T(8,128)(2,1)S(1)}, bf16[4,4,128,128]{3,2,1,0:T(8,128)(2,1)S(1)}, u32[]{:S(2)}, u32[]{:S(2)}) collective-permute-start(bf16[4,4,128,128]{3,2,1,0:T(8,128)(2,1)S(1)} %get-tuple-element.31), channel_id=1, source_target_pairs={{0,8},{1,9},{2,10},{3,11},{4,12},{5,13},{6,14},{7,15},{8,0},{9,1},... | collective-permute-start | bytes 1572872 | tf_op jit(solution)/shard_map/ppermute | solution.py:63
  45.7 6.3 %collective-permute-start.7 = (bf16[4,128,128]{2,1,0:T(8,128)(2,1)S(1)}, bf16[4,128,128]{2,1,0:T(8,128)(2,1)S(1)}, u32[]{:S(2)}, u32[]{:S(2)}) collective-permute-start(bf16[4,128,128]{2,1,0:T(8,128)(2,1)S(1)} %get-tuple-element.33), channel_id=1, source_target_pairs={{0,1},{1,0},{2,3},{3,2},{4,5},{5,4},{6,7},{7,6},{8,9},{9,8},{10,11... | collective-permute-start | bytes 393224 | tf_op jit(solution)/shard_map/ppermute | solution.py:63
  48.0 7.4 %collective-permute-start.8 = (bf16[4,128,128]{2,1,0:T(8,128)(2,1)S(1)}, bf16[4,128,128]{2,1,0:T(8,128)(2,1)S(1)}, u32[]{:S(2)}, u32[]{:S(2)}) collective-permute-start(bf16[4,128,128]{2,1,0:T(8,128)(2,1)S(1)} %get-tuple-element.34), channel_id=1, source_target_pairs={{0,16},{1,17},{2,18},{3,19},{4,20},{5,21},{6,22},{7,23},{8,24},{9,... | collective-permute-start | bytes 393224 | tf_op jit(solution)/shard_map/ppermute | solution.py:63
  51.1 6.1 %collective-permute-start.9 = (bf16[4,128,128]{2,1,0:T(8,128)(2,1)S(1)}, bf16[4,128,128]{2,1,0:T(8,128)(2,1)S(1)}, u32[]{:S(2)}, u32[]{:S(2)}) collective-permute-start(bf16[4,128,128]{2,1,0:T(8,128)(2,1)S(1)} %get-tuple-element.35), channel_id=1, source_target_pairs={{0,17},{1,16},{2,19},{3,18},{4,21},{5,20},{6,23},{7,22},{8,25},{9,... | collective-permute-start | bytes 393224 | tf_op jit(solution)/shard_map/ppermute | solution.py:63
  57.3 4.8 %collective-permute-start.10 = (bf16[144,128]{1,0:T(8,128)(2,1)S(1)}, bf16[144,128]{1,0:T(8,128)(2,1)S(1)}, u32[]{:S(2)}, u32[]{:S(2)}) collective-permute-start(bf16[144,128]{1,0:T(8,128)(2,1)S(1)} %get-tuple-element.37), channel_id=1, source_target_pairs={{0,2},{1,3},{2,0},{3,1},{4,6},{5,7},{6,4},{7,5},{8,10},{9,11},{10,... | collective-permute-start | bytes 110600 | tf_op jit(solution)/shard_map/ppermute | solution.py:63
  59.7 5.2 %collective-permute-start.11 = (bf16[144,128]{1,0:T(8,128)(2,1)S(1)}, bf16[144,128]{1,0:T(8,128)(2,1)S(1)}, u32[]{:S(2)}, u32[]{:S(2)}) collective-permute-start(bf16[144,128]{1,0:T(8,128)(2,1)S(1)} %get-tuple-element.38), channel_id=1, source_target_pairs={{0,4},{1,5},{2,6},{3,7},{4,0},{5,1},{6,2},{7,3},{8,12},{9,13},{10,... | collective-permute-start | bytes 110600 | tf_op jit(solution)/shard_map/ppermute | solution.py:63
  61.1 5.8 %collective-permute-start.12 = (bf16[144,128]{1,0:T(8,128)(2,1)S(1)}, bf16[144,128]{1,0:T(8,128)(2,1)S(1)}, u32[]{:S(2)}, u32[]{:S(2)}) collective-permute-start(bf16[144,128]{1,0:T(8,128)(2,1)S(1)} %get-tuple-element.39), channel_id=1, source_target_pairs={{0,6},{1,7},{2,4},{3,5},{4,2},{5,3},{6,0},{7,1},{8,14},{9,15},{10,... | collective-permute-start | bytes 110600 | tf_op jit(solution)/shard_map/ppermute | solution.py:63
  67.4 4.5 %collective-permute-start.13 = (bf16[144,128]{1,0:T(8,128)(2,1)S(1)}, bf16[144,128]{1,0:T(8,128)(2,1)S(1)}, u32[]{:S(2)}, u32[]{:S(2)}) collective-permute-start(bf16[144,128]{1,0:T(8,128)(2,1)S(1)} %get-tuple-element.41), channel_id=1, source_target_pairs={{0,2},{1,3},{2,0},{3,1},{4,6},{5,7},{6,4},{7,5},{8,10},{9,11},{10,... | collective-permute-start | bytes 110600 | tf_op jit(solution)/shard_map/ppermute | solution.py:63
  67.5 4.9 %collective-permute-start.14 = (bf16[144,128]{1,0:T(8,128)(2,1)S(1)}, bf16[144,128]{1,0:T(8,128)(2,1)S(1)}, u32[]{:S(2)}, u32[]{:S(2)}) collective-permute-start(bf16[144,128]{1,0:T(8,128)(2,1)S(1)} %get-tuple-element.42), channel_id=1, source_target_pairs={{0,4},{1,5},{2,6},{3,7},{4,0},{5,1},{6,2},{7,3},{8,12},{9,13},{10,... | collective-permute-start | bytes 110600 | tf_op jit(solution)/shard_map/ppermute | solution.py:63
  69.1 5.8 %collective-permute-start.15 = (bf16[144,128]{1,0:T(8,128)(2,1)S(1)}, bf16[144,128]{1,0:T(8,128)(2,1)S(1)}, u32[]{:S(2)}, u32[]{:S(2)}) collective-permute-start(bf16[144,128]{1,0:T(8,128)(2,1)S(1)} %get-tuple-element.43), channel_id=1, source_target_pairs={{0,6},{1,7},{2,4},{3,5},{4,2},{5,3},{6,0},{7,1},{8,14},{9,15},{10,... | collective-permute-start | bytes 110600 | tf_op jit(solution)/shard_map/ppermute | solution.py:63
  74.9 6.1 %collective-permute-start.18 = (bf16[4,144,128]{2,1,0:T(8,128)(2,1)S(1)}, bf16[4,144,128]{2,1,0:T(8,128)(2,1)S(1)}, u32[]{:S(2)}, u32[]{:S(2)}) collective-permute-start(bf16[4,144,128]{2,1,0:T(8,128)(2,1)S(1)} %pad_maximum_fusion.1.refs_0_), channel_id=1, source_target_pairs={{0,17},{1,16},{2,19},{3,18},{4,21},{5,20},{6,23},{7,22},{8,25},{9,... | collective-permute-start | bytes 442376 | tf_op jit(solution)/shard_map/ppermute | solution.py:63
  77.4 5.1 %collective-permute-start.17 = (bf16[4,144,128]{2,1,0:T(8,128)(2,1)S(1)}, bf16[4,144,128]{2,1,0:T(8,128)(2,1)S(1)}, u32[]{:S(2)}, u32[]{:S(2)}) collective-permute-start(bf16[4,144,128]{2,1,0:T(8,128)(2,1)S(1)} %pad_maximum_fusion.1.refs_0_), channel_id=1, source_target_pairs={{0,16},{1,17},{2,18},{3,19},{4,20},{5,21},{6,22},{7,23},{8,24},{9,... | collective-permute-start | bytes 442376 | tf_op jit(solution)/shard_map/ppermute | solution.py:63
  77.7 5.1 %collective-permute-start.16 = (bf16[4,144,128]{2,1,0:T(8,128)(2,1)S(1)}, bf16[4,144,128]{2,1,0:T(8,128)(2,1)S(1)}, u32[]{:S(2)}, u32[]{:S(2)}) collective-permute-start(bf16[4,144,128]{2,1,0:T(8,128)(2,1)S(1)} %pad_maximum_fusion.1.refs_0_), channel_id=1, source_target_pairs={{0,1},{1,0},{2,3},{3,2},{4,5},{5,4},{6,7},{7,6},{8,9},{9,8},{10,11... | collective-permute-start | bytes 442376 | tf_op jit(solution)/shard_map/ppermute | solution.py:63
  78.4 4.8 %collective-permute-start.19 = (bf16[4,144,128]{2,1,0:T(8,128)(2,1)S(1)}, bf16[4,144,128]{2,1,0:T(8,128)(2,1)S(1)}, u32[]{:S(2)}, u32[]{:S(2)}) collective-permute-start(bf16[4,144,128]{2,1,0:T(8,128)(2,1)S(1)} %pad_maximum_fusion.1.refs_0_), channel_id=1, source_target_pairs={{0,8},{1,9},{2,10},{3,11},{4,12},{5,13},{6,14},{7,15},{8,0},{9,1},... | collective-permute-start | bytes 442376 | tf_op jit(solution)/shard_map/ppermute | solution.py:63
  81.0 2.2 %collective-permute-start.22 = (bf16[4,144,128]{2,1,0:T(8,128)(2,1)S(1)}, bf16[4,144,128]{2,1,0:T(8,128)(2,1)S(1)}, u32[]{:S(2)}, u32[]{:S(2)}) collective-permute-start(bf16[4,144,128]{2,1,0:T(8,128)(2,1)S(1)} %collective-permute-done.18.refs_3_), channel_id=1, source_target_pairs={{0,8},{1,9},{2,10},{3,11},{4,12},{5,13},{6,14},{7,15},{8,0},{9,1},... | collective-permute-start | bytes 442376 | tf_op jit(solution)/shard_map/ppermute | solution.py:63
  82.6 1.4 %collective-permute-start.21 = (bf16[4,144,128]{2,1,0:T(8,128)(2,1)S(1)}, bf16[4,144,128]{2,1,0:T(8,128)(2,1)S(1)}, u32[]{:S(2)}, u32[]{:S(2)}) collective-permute-start(bf16[4,144,128]{2,1,0:T(8,128)(2,1)S(1)} %collective-permute-done.17.refs_2_), channel_id=1, source_target_pairs={{0,8},{1,9},{2,10},{3,11},{4,12},{5,13},{6,14},{7,15},{8,0},{9,1},... | collective-permute-start | bytes 442376 | tf_op jit(solution)/shard_map/ppermute | solution.py:63
  82.9 1.4 %collective-permute-start.20 = (bf16[4,144,128]{2,1,0:T(8,128)(2,1)S(1)}, bf16[4,144,128]{2,1,0:T(8,128)(2,1)S(1)}, u32[]{:S(2)}, u32[]{:S(2)}) collective-permute-start(bf16[4,144,128]{2,1,0:T(8,128)(2,1)S(1)} %collective-permute-done.16.refs_1_), channel_id=1, source_target_pairs={{0,8},{1,9},{2,10},{3,11},{4,12},{5,13},{6,14},{7,15},{8,0},{9,1},... | collective-permute-start | bytes 442376 | tf_op jit(solution)/shard_map/ppermute | solution.py:63

commit v6 on v5

--- a/solution.py
+++ b/solution.py
@@ -111,7 +111,6 @@
     after,
     labels,
     first,
-    rim_row,
     temb,
     conv1,
     conv2,
@@ -199,7 +198,7 @@
     rows_before = before[tall : tall + share + 1].astype(F32)
     rows_after = after[tall : tall + share + 1].astype(F32)
     mine = first[...].astype(F32)
-    rim_mine = rim_row[...].astype(F32)
+    edge_above, edge_below = above[4].astype(F32), below[4].astype(F32)
     same_at = pl.ds(pl.multiple_of(side * share, share), share)
     second_at = pl.ds(pl.multiple_of((1 - side) * share, share), share)
     xz_above, xz_below = [], []
@@ -208,9 +207,8 @@
         yzs[k] = mine[0:ncols, k, :]
         xzs[k, same_at, :] = mine[ncols:, k, :]
         xzs[k, second_at, :] = second[0:share]
-        rim_same, rim_second = rim_mine[:, k, :], second[share:]
-        xz_above.append(jnp.where(side == 0, rim_same, rim_second))
-        xz_below.append(jnp.where(side == 0, rim_second, rim_same))
+        xz_above.append(jnp.where(side == 0, second[share:], edge_above[k : k + 1]))
+        xz_below.append(jnp.where(side == 0, edge_below[k : k + 1], second[share:]))
 
     def decode(feat, label):
         pixels = feat.shape[0] // depth
@@ -426,19 +424,21 @@
 
 def last_kernel(shares, classes, place, *refs):
     halves, refs = refs[: 2 * shares.planes], refs[2 * shares.planes :]
-    emb, g1, g2, gt, gw1, gw2, gw3, gxz, gyz, whole, w3_rows = refs
+    emb, g1, g2, gt, gw1, gw2, gw3, gxz, gyz, whole, rest = refs
+    each = shares.each
     width, hidden = emb.shape[0], gw2.shape[0]
     core, plane, layer = place[5], place[6], place[7]
     row_core, row_side, rank = place[8], place[0], place[9]
     for k in range(shares.planes):
         for t in range(shares.layers):
             index = (plane ^ k) * shares.layers + (layer ^ t)
-            whole[core, index] = halves[k][t].astype(F32)
-            whole[1 - core, index] = halves[shares.planes + k][t].astype(F32)
+            for half, block in ((core, halves[k]), (1 - core, halves[shares.planes + k])):
+                whole[half, index] = block[t, 0:each, :]
+                rest[half, index] = block[t, each:, :].astype(F32)
 
     def take(start, ref, lead, lanes):
         for side, index, row, offset, rows in shares.split(start, width if lead is not None else ref.shape[0]):
-            block = whole[side, index, row : row + rows, :]
+            block = whole[side, index, row : row + rows, :].astype(F32)
             if lead is not None:
                 ref[lead, offset : offset + rows, :] = block
             else:
@@ -450,26 +450,24 @@
     for name, ref in (("w1", gw1), ("w2", gw2)):
         for part in range(hidden // LANES):
             take(shares.at[name] + part * ref.shape[0], ref, None, slice(part * LANES, (part + 1) * LANES))
-    small = slice(shares.small, shares.small + 1)
-    gt[...] = emb[...] * whole[classes // shares.chips, classes % shares.chips, small, :]
-    for part in range(hidden // LANES):
-        small = slice(shares.small + part, shares.small + part + 1)
-        w3_rows[...] = jnp.zeros_like(w3_rows)
-        for q in range(classes):
-            w3_rows[q : q + 1, :] = whole[q // shares.chips, q % shares.chips, small, :]
-        gw3[part * LANES : (part + 1) * LANES, :] = w3_rows[...].T[:, 0:classes]
+    at_small, at_yz = shares.small - each, shares.yz - each
+    gt[...] = emb[...] * rest[classes // shares.chips, classes % shares.chips, at_small : at_small + 1, :]
+    for q in range(classes):
+        for part in range(hidden // LANES):
+            value = rest[q // shares.chips, q % shares.chips, at_small + part : at_small + part + 1, :]
+            gw3[q : q + 1, part * LANES : (part + 1) * LANES] = value
     count = gxz.shape[0]
     begin = pl.multiple_of(row_side * count, count)
-    gxz[...] = whole[row_core, pl.ds(begin, count), shares.xz : shares.xz + shares.xz_rows, :]
+    gxz[...] = rest[row_core, pl.ds(begin, count), 0 : shares.xz_rows, :]
     size, per = shares.yz_rows, shares.yz_rows * shares.yz_shares
     for r in range(2):
         for side in range(2):
             for index in range(shares.yz_shares):
                 to = (2 * r + side) * per + index * size
-                value = whole[side, index, shares.yz + r * size : shares.yz + (r + 1) * size, :]
+                value = rest[side, index, at_yz + r * size : at_yz + (r + 1) * size, :]
                 for i in range(1, shares.planes):
-                    begin = shares.yz + (2 * i + r) * size
-                    value = jnp.where(rank == i, whole[side, index, begin : begin + size, :], value)
+                    begin = at_yz + (2 * i + r) * size
+                    value = jnp.where(rank == i, rest[side, index, begin : begin + size, :], value)
                 gyz[to : to + size, :] = value
 
 
@@ -511,19 +509,20 @@
     def lab(part):
         return jnp.pad(part.astype(BF16), ((0, 0), (0, 0), (0, LANES - depth)))
 
-    above = grid.move(jnp.concatenate([xy_noisy[nrows - REACH :], lab(labels[nrows - 1 :])]), up)
-    below = grid.move(jnp.concatenate([xy_noisy[:REACH], lab(labels[:1])]), down)
-
     slab_count = xz_plane.shape[1] // depth
     start = timestep[0] % slab_count * depth
     xz_local = lax.dynamic_slice_in_dim(xz_plane, start, depth, 1)
     share = xz_local.shape[0]
     yz_half = lax.dynamic_slice(yz_plane, (side * ncols, start, 0), (ncols, depth, width))
     first = grid.move(jnp.concatenate([yz_half, xz_local], axis=0), grid.turned(0))
-    rim_row = grid.move(
-        jnp.where(side == 0, xz_local[:1], xz_local[share - 1 :]),
-        lambda i, j: (j // count - 1, count * i + 1) if j % count == 0 else (j // count + 1, count * i),
-    )
+
+    def row(features, labels_row, edge):
+        edge = jnp.pad(edge[None], ((0, 0), (0, ncols - depth), (0, 0)))
+        return jnp.concatenate([features, lab(labels_row), edge])
+
+    above = grid.move(row(xy_noisy[nrows - REACH :], labels[nrows - 1 :], first[ncols + share - 1]), up)
+    below = grid.move(row(xy_noisy[:REACH], labels[:1], first[ncols]), down)
+    edge_row = jnp.where(side == 0, below[4:, :depth], above[4:, :depth])
 
     def column(at, where):
         cols = jnp.concatenate(
@@ -531,10 +530,10 @@
         )
         yz = first[at].reshape(depth, 1, width)
         extra = jnp.concatenate(
-            [yz[:2], above[3:, at : at + 1], lab(labels[:, at : at + 1]), below[3:, at : at + 1], yz[2:]],
+            [yz[:2], above[3:4, at : at + 1], lab(labels[:, at : at + 1]), below[3:4, at : at + 1], yz[2:]],
             axis=0,
         )
-        return jnp.concatenate([jnp.concatenate([cols, extra], axis=1), first[ncols:], rim_row], axis=0)
+        return jnp.concatenate([jnp.concatenate([cols, extra], axis=1), first[ncols:], edge_row], axis=0)
 
     before = grid.move(column(ncols - 1, slice(ncols - REACH, ncols)), right)
     after = grid.move(column(0, slice(0, REACH)), left)
@@ -563,7 +562,7 @@
     own, other = pl.pallas_call(
         functools.partial(main_kernel, classes, shares),
         out_shape=(buffer, buffer),
-        in_specs=[smem] + [vmem] * 15,
+        in_specs=[smem] + [vmem] * 14,
         out_specs=(vmem, vmem),
         scratch_shapes=[
             pltpu.VMEM((nrows + 6, 32, width), F32),
@@ -595,7 +594,6 @@
         after,
         labels_by_depth,
         first,
-        rim_row,
         temb.reshape(1, width),
         flat_one,
         flat_two,
@@ -645,15 +643,15 @@
             jax.ShapeDtypeStruct((width, width), F32),
             jax.ShapeDtypeStruct((width, hidden), F32),
             jax.ShapeDtypeStruct((hidden, hidden), F32),
-            jax.ShapeDtypeStruct((hidden, classes), F32),
+            jax.ShapeDtypeStruct((classes, hidden), F32),
             jax.ShapeDtypeStruct((chips // 2, shares.xz_rows, width), F32),
             jax.ShapeDtypeStruct((2 * ncols * depth, width), F32),
         ),
         in_specs=[smem] + [vmem] * (2 * planes + 1),
         out_specs=(vmem,) * 8,
         scratch_shapes=[
-            pltpu.VMEM((2, chips, shares.end_rows, LANES), F32),
-            pltpu.VMEM((LANES, LANES), F32),
+            pltpu.VMEM((2, chips, shares.each, LANES), BF16),
+            pltpu.VMEM((2, chips, shares.end_rows - shares.each, LANES), F32),
         ],
         compiler_params=params,
         name="spread",
@@ -669,7 +667,7 @@
         gt,
         gw1,
         gw2,
-        gw3,
+        gw3.T,
         gxz.reshape(share, depth, width),
         gyz.reshape(2 * ncols, depth, width),
     )

time: 87.4 us -> 86.3 us (0.987)
  starting transfers between devices: 37.2 us -> 31.6 us
  waiting for transfers between devices: 24.5 us -> 29.7 us
    ppermute x23 -> x22, starting transfers between devices: 37.2 us -> 31.6 us  [move(): return lax.ppermute(array, BOTH, pairs)]
    ppermute x23 -> x22, waiting for transfers between devices: 24.5 us -> 29.7 us  [move(): return lax.ppermute(array, BOTH, pairs)]
    unnamed x27 -> x30, local copies, waits for them, and re-layouts: 2.62 us -> 2.9 us
  transfers between devices with their start and end apart: 23 -> 22, of which waited for: 16 -> 16; matrix products, arithmetic and copies ran while one was open for 3% -> 2% of each run, Pallas kernels for 0% -> 0%
where the time goes in v6:
time: 86.3 us; the launch traced here: 85.8 us
  starting transfers between devices  31.6 us (37%)
  waiting for transfers between devices  29.7 us (34%)
  Pallas kernels  17.3 us (20%)
  local copies, waits for them, and re-layouts  4.67 us (5%)
  between operations  1.88 us (2%)
    ppermute x22, starting transfers between devices, move(): return lax.ppermute(array, BOTH, pairs)  31.6 us
    ppermute x22, waiting for transfers between devices, move(): return lax.ppermute(array, BOTH, pairs)  29.7 us
    pallas_call x1, Pallas kernels, local(): pl.pallas_call(functools.partial(main_kernel, classes, shares), out_shape...  14.7 us
    unnamed x30, local copies, waits for them, and re-layouts  2.9 us
    pallas_call x1, Pallas kernels, local(): pl.pallas_call(functools.partial(last_kernel, shares, classes), out_shape...  1.86 us
  transfers between devices with their start and end apart: 22, of which 16 were waited for; matrix products, arithmetic and copies ran while one was open for 2% of the time, Pallas kernels for 0%

profile of v6, /device:TPU:0, one launch (start us, length us, event | category | flops | bytes accessed | tf_op | source)
XLA Modules:
  0.0 85.8 jit_solution(17665701083963174722)
XLA Ops:
  1.4 0.3 copy-done
  1.7 0.8 constant_dynamic-slice_fusion.1
  2.6 0.7 collective-permute-start
  3.3 0.7 copy-done.8
  4.0 0.3 copy.30
  4.5 0.6 copy-done.10
  5.1 0.1 copy.38
  5.4 0.7 copy-done.9
  6.1 0.1 fusion.18.temb
  6.2 0.1 pad_bitcast_fusion.3
  6.6 0.2 copy.37
  7.1 6.3 %collective-permute-start.1 = (bf16[5,16,128]{2,1,0:T(8,128)(2,1)S(1)}, bf16[5,16,128]{2,1,0:T(8,128)(2,1)S(1)}, u32[]{:S(2)}, u32[]{:S(2)}) collective-permute-start(bf16[5,16,128]{2,1,0:T(8,128)(2,1)S(1)} %fusion.6), channel_id=1, source_target_pairs={{0,8},{1,9},{2,10},{3,11},{4,12},{5,13},{6,14},{7,15},{8,16},{9,17... | collective-permute-start | bytes 61448 | tf_op jit(solution)/shard_map/ppermute | solution.py:63
  13.4 1.3 %collective-permute-start.2 = (bf16[5,16,128]{2,1,0:T(8,128)(2,1)S(1)}, bf16[5,16,128]{2,1,0:T(8,128)(2,1)S(1)}, u32[]{:S(2)}, u32[]{:S(2)}) collective-permute-start(bf16[5,16,128]{2,1,0:T(8,128)(2,1)S(1)} %fusion.8), channel_id=1, source_target_pairs={{8,0},{9,1},{10,2},{11,3},{12,4},{13,5},{14,6},{15,7},{16,8},{17,9... | collective-permute-start | bytes 61448 | tf_op jit(solution)/shard_map/ppermute | solution.py:63
  14.8 4.3 %collective-permute-done.2.below = bf16[5,16,128]{2,1,0:T(8,128)(2,1)S(1)} collective-permute-done((bf16[5,16,128]{2,1,0:T(8,128)(2,1)S(1)}, bf16[5,16,128]{2,1,0:T(8,128)(2,1)S(1)}, u32[]{:S(2)}, u32[]{:S(2)}) %collective-permute-start.2) | collective-permute-done | bytes 20512 | tf_op jit(solution)/shard_map/ppermute | solution.py:63
  19.1 0.2 pad_maximum_fusion.2
  19.3 1.4 %collective-permute-start.4 = (bf16[103,4,128]{2,1,0:T(4,128)(2,1)S(1)}, bf16[103,4,128]{2,1,0:T(4,128)(2,1)S(1)}, u32[]{:S(2)}, u32[]{:S(2)}) collective-permute-start(bf16[103,4,128]{2,1,0:T(4,128)(2,1)S(1)} %get-tuple-element.70), channel_id=1, source_target_pairs={{1,0},{2,1},{3,2},{4,3},{5,4},{6,5},{7,6},{9,8},{10,9},{11,10},{12... | collective-permute-start | bytes 316424 | tf_op jit(solution)/shard_map/ppermute | solution.py:63
  20.8 4.6 %collective-permute-start.3 = (bf16[103,4,128]{2,1,0:T(4,128)(2,1)S(1)}, bf16[103,4,128]{2,1,0:T(4,128)(2,1)S(1)}, u32[]{:S(2)}, u32[]{:S(2)}) collective-permute-start(bf16[103,4,128]{2,1,0:T(4,128)(2,1)S(1)} %get-tuple-element.71), channel_id=1, source_target_pairs={{0,1},{1,2},{2,3},{3,4},{4,5},{5,6},{6,7},{8,9},{9,10},{10,11},{11... | collective-permute-start | bytes 316424 | tf_op jit(solution)/shard_map/ppermute | solution.py:63
  25.4 0.6 collective-permute-done.4.after
  26.1 3.6 %collective-permute-done.3.before = bf16[103,4,128]{2,1,0:T(4,128)(2,1)S(1)} collective-permute-done((bf16[103,4,128]{2,1,0:T(4,128)(2,1)S(1)}, bf16[103,4,128]{2,1,0:T(4,128)(2,1)S(1)}, u32[]{:S(2)}, u32[]{:S(2)}) %collective-permute-start.3) | collective-permute-done | bytes 105504 | tf_op jit(solution)/shard_map/ppermute | solution.py:63
  29.7 14.7 %tile.1 = (bf16[4,4,128,128]{3,2,1,0:T(8,128)(2,1)S(1)}, bf16[4,4,128,128]{3,2,1,0:T(8,128)(2,1)S(1)}) custom-call(s32[10]{0:T(128)S(1)} %stack.70.place, bf16[64,16,128]{2,1,0:T(8,128)(2,1)S(1)} %copy-done.2, bf16[5,16,128]{2,1,0:T(8,128)(2,1)S(1)} %collective-permute-done.1.above, bf16[5,16,128]{2,1,0:T(8,128)(2,1)S(1)} %collective-permute-done.2.below, ...), custom_call_target="tpu_custom_call" | custom-call | tf_op jit(solution)/shard_map/tile/pallas_call | solution.py:562
  44.4 0.4 collective-permute-start.5
  44.8 1.6 %collective-permute-done.5.other = bf16[4,4,128,128]{3,2,1,0:T(8,128)(2,1)S(1)} collective-permute-done((bf16[4,4,128,128]{3,2,1,0:T(8,128)(2,1)S(1)}, bf16[4,4,128,128]{3,2,1,0:T(8,128)(2,1)S(1)}, u32[]{:S(2)}, u32[]{:S(2)}) %collective-permute-start.5) | collective-permute-done | bytes 524320 | tf_op jit(solution)/shard_map/ppermute | solution.py:63
  46.4 0.1 cores.1
  46.5 2.6 %collective-permute-start.6 = (bf16[4,128,128]{2,1,0:T(8,128)(2,1)S(1)}, bf16[4,128,128]{2,1,0:T(8,128)(2,1)S(1)}, u32[]{:S(2)}, u32[]{:S(2)}) collective-permute-start(bf16[4,128,128]{2,1,0:T(8,128)(2,1)S(1)} %get-tuple-element.33), channel_id=1, source_target_pairs={{0,1},{1,0},{2,3},{3,2},{4,5},{5,4},{6,7},{7,6},{8,9},{9,8},{10,11... | collective-permute-start | bytes 393224 | tf_op jit(solution)/shard_map/ppermute | solution.py:63
  49.0 0.3 collective-permute-start.7
  49.3 1.2 %collective-permute-start.8 = (bf16[4,128,128]{2,1,0:T(8,128)(2,1)S(1)}, bf16[4,128,128]{2,1,0:T(8,128)(2,1)S(1)}, u32[]{:S(2)}, u32[]{:S(2)}) collective-permute-start(bf16[4,128,128]{2,1,0:T(8,128)(2,1)S(1)} %get-tuple-element.35), channel_id=1, source_target_pairs={{0,17},{1,16},{2,19},{3,18},{4,21},{5,20},{6,23},{7,22},{8,25},{9,... | collective-permute-start | bytes 393224 | tf_op jit(solution)/shard_map/ppermute | solution.py:63
  50.6 2.3 %collective-permute-done.6.refs_1_ = bf16[4,128,128]{2,1,0:T(8,128)(2,1)S(1)} collective-permute-done((bf16[4,128,128]{2,1,0:T(8,128)(2,1)S(1)}, bf16[4,128,128]{2,1,0:T(8,128)(2,1)S(1)}, u32[]{:S(2)}, u32[]{:S(2)}) %collective-permute-start.6) | collective-permute-done | bytes 131104 | tf_op jit(solution)/shard_map/ppermute | solution.py:63
  52.8 2.6 %collective-permute-done.7.refs_2_ = bf16[4,128,128]{2,1,0:T(8,128)(2,1)S(1)} collective-permute-done((bf16[4,128,128]{2,1,0:T(8,128)(2,1)S(1)}, bf16[4,128,128]{2,1,0:T(8,128)(2,1)S(1)}, u32[]{:S(2)}, u32[]{:S(2)}) %collective-permute-start.7) | collective-permute-done | bytes 131104 | tf_op jit(solution)/shard_map/ppermute | solution.py:63
  55.4 1.5 %collective-permute-done.8.refs_3_ = bf16[4,128,128]{2,1,0:T(8,128)(2,1)S(1)} collective-permute-done((bf16[4,128,128]{2,1,0:T(8,128)(2,1)S(1)}, bf16[4,128,128]{2,1,0:T(8,128)(2,1)S(1)}, u32[]{:S(2)}, u32[]{:S(2)}) %collective-permute-start.8) | collective-permute-done | bytes 131104 | tf_op jit(solution)/shard_map/ppermute | solution.py:63
  57.0 2.4 %collective-permute-start.9 = (bf16[144,128]{1,0:T(8,128)(2,1)S(1)}, bf16[144,128]{1,0:T(8,128)(2,1)S(1)}, u32[]{:S(2)}, u32[]{:S(2)}) collective-permute-start(bf16[144,128]{1,0:T(8,128)(2,1)S(1)} %get-tuple-element.37), channel_id=1, source_target_pairs={{0,2},{1,3},{2,0},{3,1},{4,6},{5,7},{6,4},{7,5},{8,10},{9,11},{10,... | collective-permute-start | bytes 110600 | tf_op jit(solution)/shard_map/ppermute | solution.py:63
  59.4 2.4 %collective-permute-start.11 = (bf16[144,128]{1,0:T(8,128)(2,1)S(1)}, bf16[144,128]{1,0:T(8,128)(2,1)S(1)}, u32[]{:S(2)}, u32[]{:S(2)}) collective-permute-start(bf16[144,128]{1,0:T(8,128)(2,1)S(1)} %get-tuple-element.39), channel_id=1, source_target_pairs={{0,6},{1,7},{2,4},{3,5},{4,2},{5,3},{6,0},{7,1},{8,14},{9,15},{10,... | collective-permute-start | bytes 110600 | tf_op jit(solution)/shard_map/ppermute | solution.py:63
  61.8 2.4 %collective-permute-done.10.refs_2_ = bf16[144,128]{1,0:T(8,128)(2,1)S(1)} collective-permute-done((bf16[144,128]{1,0:T(8,128)(2,1)S(1)}, bf16[144,128]{1,0:T(8,128)(2,1)S(1)}, u32[]{:S(2)}, u32[]{:S(2)}) %collective-permute-start.10) | collective-permute-done | bytes 36896 | tf_op jit(solution)/shard_map/ppermute | solution.py:63
  64.2 0.9 %collective-permute-done.11.refs_3_ = bf16[144,128]{1,0:T(8,128)(2,1)S(1)} collective-permute-done((bf16[144,128]{1,0:T(8,128)(2,1)S(1)}, bf16[144,128]{1,0:T(8,128)(2,1)S(1)}, u32[]{:S(2)}, u32[]{:S(2)}) %collective-permute-start.11) | collective-permute-done | bytes 36896 | tf_op jit(solution)/shard_map/ppermute | solution.py:63
  65.1 0.6 layers.1
  65.7 0.1 collective-permute-start.12
  65.8 2.9 %collective-permute-start.13 = (bf16[144,128]{1,0:T(8,128)(2,1)S(1)}, bf16[144,128]{1,0:T(8,128)(2,1)S(1)}, u32[]{:S(2)}, u32[]{:S(2)}) collective-permute-start(bf16[144,128]{1,0:T(8,128)(2,1)S(1)} %get-tuple-element.42), channel_id=1, source_target_pairs={{0,4},{1,5},{2,6},{3,7},{4,0},{5,1},{6,2},{7,3},{8,12},{9,13},{10,... | collective-permute-start | bytes 110600 | tf_op jit(solution)/shard_map/ppermute | solution.py:63
  68.8 1.4 %collective-permute-start.14 = (bf16[144,128]{1,0:T(8,128)(2,1)S(1)}, bf16[144,128]{1,0:T(8,128)(2,1)S(1)}, u32[]{:S(2)}, u32[]{:S(2)}) collective-permute-start(bf16[144,128]{1,0:T(8,128)(2,1)S(1)} %get-tuple-element.43), channel_id=1, source_target_pairs={{0,6},{1,7},{2,4},{3,5},{4,2},{5,3},{6,0},{7,1},{8,14},{9,15},{10,... | collective-permute-start | bytes 110600 | tf_op jit(solution)/shard_map/ppermute | solution.py:63
  70.2 0.5 collective-permute-done.13
  70.7 3.8 %collective-permute-done.14 = bf16[144,128]{1,0:T(8,128)(2,1)S(1)} collective-permute-done((bf16[144,128]{1,0:T(8,128)(2,1)S(1)}, bf16[144,128]{1,0:T(8,128)(2,1)S(1)}, u32[]{:S(2)}, u32[]{:S(2)}) %collective-permute-start.14) | collective-permute-done | bytes 36896 | tf_op jit(solution)/shard_map/ppermute | solution.py:63
  74.6 1.3 %collective-permute-start.17 = (bf16[4,144,128]{2,1,0:T(8,128)(2,1)S(1)}, bf16[4,144,128]{2,1,0:T(8,128)(2,1)S(1)}, u32[]{:S(2)}, u32[]{:S(2)}) collective-permute-start(bf16[4,144,128]{2,1,0:T(8,128)(2,1)S(1)} %pad_maximum_fusion.1.refs_0_), channel_id=1, source_target_pairs={{0,17},{1,16},{2,19},{3,18},{4,21},{5,20},{6,23},{7,22},{8,25},{9,... | collective-permute-start | bytes 442376 | tf_op jit(solution)/shard_map/ppermute | solution.py:63
  75.9 1.5 %collective-permute-start.16 = (bf16[4,144,128]{2,1,0:T(8,128)(2,1)S(1)}, bf16[4,144,128]{2,1,0:T(8,128)(2,1)S(1)}, u32[]{:S(2)}, u32[]{:S(2)}) collective-permute-start(bf16[4,144,128]{2,1,0:T(8,128)(2,1)S(1)} %pad_maximum_fusion.1.refs_0_), channel_id=1, source_target_pairs={{0,16},{1,17},{2,18},{3,19},{4,20},{5,21},{6,22},{7,23},{8,24},{9,... | collective-permute-start | bytes 442376 | tf_op jit(solution)/shard_map/ppermute | solution.py:63
  77.4 0.7 collective-permute-start.15
  78.1 2.5 %collective-permute-done.17.refs_3_ = bf16[4,144,128]{2,1,0:T(8,128)(2,1)S(1)} collective-permute-done((bf16[4,144,128]{2,1,0:T(8,128)(2,1)S(1)}, bf16[4,144,128]{2,1,0:T(8,128)(2,1)S(1)}, u32[]{:S(2)}, u32[]{:S(2)}) %collective-permute-start.17) | collective-permute-done | bytes 147488 | tf_op jit(solution)/shard_map/ppermute | solution.py:63
  80.7 1.4 %collective-permute-done.16.refs_2_ = bf16[4,144,128]{2,1,0:T(8,128)(2,1)S(1)} collective-permute-done((bf16[4,144,128]{2,1,0:T(8,128)(2,1)S(1)}, bf16[4,144,128]{2,1,0:T(8,128)(2,1)S(1)}, u32[]{:S(2)}, u32[]{:S(2)}) %collective-permute-start.16) | collective-permute-done | bytes 147488 | tf_op jit(solution)/shard_map/ppermute | solution.py:63
  82.1 0.4 collective-permute-done.15.refs_1_
  82.7 0.7 collective-permute-done.20.refs_6_
  83.4 0.4 collective-permute-done.19.refs_5_
  83.9 1.9 %spread.1 = (f32[9,128,128]{2,1,0:T(8,128)}, f32[9,128,128]{2,1,0:T(8,128)}, f32[128,128]{1,0:T(8,128)}, f32[128,256]{1,0:T(8,128)}, f32[256,256]{1,0:T(8,128)},...) custom-call(s32[10]{0:T(128)S(1)} %stack.70.place, ...), custom_call_target="tpu_custom_call" | custom-call | tf_op jit(solution)/shard_map/spread/pallas_call | solution.py:638
  (64 shorter events, 1.3 us)
Async XLA Ops:
  0.6 1.1 %copy-start = (bf16[32,64,128]{2,1,0:T(8,128)(2,1)S(1)}, bf16[32,64,128]{2,1,0:T(8,128)(2,1)}, u32[]{:S(2)}) copy-start(bf16[32,64,128]{2,1,0:T(8,128)(2,1)} %param.12) | copy-start | bytes 1572868
  0.6 2.6 %copy-start.2 = (bf16[64,16,128]{2,1,0:T(8,128)(2,1)S(1)}, bf16[64,16,128]{2,1,0:T(8,128)(2,1)}, u32[]{:S(2)}) copy-start(bf16[64,16,128]{2,1,0:T(8,128)(2,1)} %xy.1) | copy-start | bytes 786436
  2.6 4.4 %collective-permute-start = (bf16[48,4,128]{2,1,0:T(4,128)(2,1)S(1)}, bf16[48,4,128]{2,1,0:T(4,128)(2,1)S(1)}, u32[]{:S(2)}, u32[]{:S(2)}) collective-permute-start(bf16[48,4,128]{2,1,0:T(4,128)(2,1)S(1)} %pad_maximum_fusion.6), channel_id=1, source_target_pairs={{0,0},{1,1},{2,8},{3,9},{4,16},{5,17},{6,24},{7,25},{8,2},{9,3},{1... | collective-permute-start | bytes 147464 | tf_op jit(solution)/shard_map/ppermute | solution.py:63
  3.2 0.8 copy-start.8
  4.3 1.0 %copy-start.1 = (bf16[3,3,128,128]{3,2,1,0:T(8,128)(2,1)S(1)}, bf16[3,3,128,128]{3,2,1,0:T(8,128)(2,1)}, u32[]{:S(2)}) copy-start(bf16[3,3,128,128]{3,2,1,0:T(8,128)(2,1)} %param.17) | copy-start | bytes 884740
  4.4 0.7 copy-start.10
  5.3 0.8 copy-start.9
  7.0 7.7 %copy-start.4 = (bf16[48,4,128]{2,1,0:T(4,128)(2,1)}, bf16[48,4,128]{2,1,0:T(4,128)(2,1)S(1)}, u32[]{:S(2)}) copy-start(bf16[48,4,128]{2,1,0:T(4,128)(2,1)S(1)} %collective-permute-done.first) | copy-start | bytes 147460
  7.1 7.6 %collective-permute-start.1 = (bf16[5,16,128]{2,1,0:T(8,128)(2,1)S(1)}, bf16[5,16,128]{2,1,0:T(8,128)(2,1)S(1)}, u32[]{:S(2)}, u32[]{:S(2)}) collective-permute-start(bf16[5,16,128]{2,1,0:T(8,128)(2,1)S(1)} %fusion.6), channel_id=1, source_target_pairs={{0,8},{1,9},{2,10},{3,11},{4,12},{5,13},{6,14},{7,15},{8,16},{9,17... | collective-permute-start | bytes 61448 | tf_op jit(solution)/shard_map/ppermute | solution.py:63
  13.4 5.7 %collective-permute-start.2 = (bf16[5,16,128]{2,1,0:T(8,128)(2,1)S(1)}, bf16[5,16,128]{2,1,0:T(8,128)(2,1)S(1)}, u32[]{:S(2)}, u32[]{:S(2)}) collective-permute-start(bf16[5,16,128]{2,1,0:T(8,128)(2,1)S(1)} %fusion.8), channel_id=1, source_target_pairs={{8,0},{9,1},{10,2},{11,3},{12,4},{13,5},{14,6},{15,7},{16,8},{17,9... | collective-permute-start | bytes 61448 | tf_op jit(solution)/shard_map/ppermute | solution.py:63
  14.8 4.3 %slice-start = ((bf16[48,4,128]{2,1,0:T(4,128)(2,1)}), bf16[32,4,128]{2,1,0:T(4,128)(2,1)S(1)}, s32[]{:S(2)}) async-start(bf16[48,4,128]{2,1,0:T(4,128)(2,1)} %copy-done.4), calls=%async_computation | async-start | bytes 65536 | tf_op jit(solution)/shard_map/slice | solution.py:536
  19.3 10.3 %copy-start.3 = (bf16[3,3,128,128]{3,2,1,0:T(8,128)(2,1)S(1)}, bf16[3,3,128,128]{3,2,1,0:T(8,128)(2,1)}, u32[]{:S(2)}) copy-start(bf16[3,3,128,128]{3,2,1,0:T(8,128)(2,1)} %param.16) | copy-start | bytes 884740
  19.3 6.7 %collective-permute-start.4 = (bf16[103,4,128]{2,1,0:T(4,128)(2,1)S(1)}, bf16[103,4,128]{2,1,0:T(4,128)(2,1)S(1)}, u32[]{:S(2)}, u32[]{:S(2)}) collective-permute-start(bf16[103,4,128]{2,1,0:T(4,128)(2,1)S(1)} %get-tuple-element.70), channel_id=1, source_target_pairs={{1,0},{2,1},{3,2},{4,3},{5,4},{6,5},{7,6},{9,8},{10,9},{11,10},{12... | collective-permute-start | bytes 316424 | tf_op jit(solution)/shard_map/ppermute | solution.py:63
  20.8 8.9 %collective-permute-start.3 = (bf16[103,4,128]{2,1,0:T(4,128)(2,1)S(1)}, bf16[103,4,128]{2,1,0:T(4,128)(2,1)S(1)}, u32[]{:S(2)}, u32[]{:S(2)}) collective-permute-start(bf16[103,4,128]{2,1,0:T(4,128)(2,1)S(1)} %get-tuple-element.71), channel_id=1, source_target_pairs={{0,1},{1,2},{2,3},{3,4},{4,5},{5,6},{6,7},{8,9},{9,10},{10,11},{11... | collective-permute-start | bytes 316424 | tf_op jit(solution)/shard_map/ppermute | solution.py:63
  25.3 4.3 %copy-start.5 = (bf16[48,4,128]{2,1,0:T(4,128)(2,1)S(1)}, bf16[48,4,128]{2,1,0:T(4,128)(2,1)}, u32[]{:S(2)}) copy-start(bf16[48,4,128]{2,1,0:T(4,128)(2,1)} %copy-done.4) | copy-start | bytes 147460
  25.3 4.3 %copy-start.6 = (bf16[256,256]{1,0:T(8,128)(2,1)S(1)}, bf16[256,256]{1,0:T(8,128)(2,1)}, u32[]{:S(2)}) copy-start(bf16[256,256]{1,0:T(8,128)(2,1)} %w2.1) | copy-start | bytes 393220
  25.4 4.3 %copy-start.7 = (bf16[128,256]{1,0:T(8,128)(2,1)S(1)}, bf16[128,256]{1,0:T(8,128)(2,1)}, u32[]{:S(2)}) copy-start(bf16[128,256]{1,0:T(8,128)(2,1)} %w1.1) | copy-start | bytes 196612
  44.4 2.0 %collective-permute-start.5 = (bf16[4,4,128,128]{3,2,1,0:T(8,128)(2,1)S(1)}, bf16[4,4,128,128]{3,2,1,0:T(8,128)(2,1)S(1)}, u32[]{:S(2)}, u32[]{:S(2)}) collective-permute-start(bf16[4,4,128,128]{3,2,1,0:T(8,128)(2,1)S(1)} %get-tuple-element.31), channel_id=1, source_target_pairs={{0,8},{1,9},{2,10},{3,11},{4,12},{5,13},{6,14},{7,15},{8,0},{9,1},... | collective-permute-start | bytes 1572872 | tf_op jit(solution)/shard_map/ppermute | solution.py:63
  46.5 6.4 %collective-permute-start.6 = (bf16[4,128,128]{2,1,0:T(8,128)(2,1)S(1)}, bf16[4,128,128]{2,1,0:T(8,128)(2,1)S(1)}, u32[]{:S(2)}, u32[]{:S(2)}) collective-permute-start(bf16[4,128,128]{2,1,0:T(8,128)(2,1)S(1)} %get-tuple-element.33), channel_id=1, source_target_pairs={{0,1},{1,0},{2,3},{3,2},{4,5},{5,4},{6,7},{7,6},{8,9},{9,8},{10,11... | collective-permute-start | bytes 393224 | tf_op jit(solution)/shard_map/ppermute | solution.py:63
  49.0 6.4 %collective-permute-start.7 = (bf16[4,128,128]{2,1,0:T(8,128)(2,1)S(1)}, bf16[4,128,128]{2,1,0:T(8,128)(2,1)S(1)}, u32[]{:S(2)}, u32[]{:S(2)}) collective-permute-start(bf16[4,128,128]{2,1,0:T(8,128)(2,1)S(1)} %get-tuple-element.34), channel_id=1, source_target_pairs={{0,16},{1,17},{2,18},{3,19},{4,20},{5,21},{6,22},{7,23},{8,24},{9,... | collective-permute-start | bytes 393224 | tf_op jit(solution)/shard_map/ppermute | solution.py:63
  49.3 7.6 %collective-permute-start.8 = (bf16[4,128,128]{2,1,0:T(8,128)(2,1)S(1)}, bf16[4,128,128]{2,1,0:T(8,128)(2,1)S(1)}, u32[]{:S(2)}, u32[]{:S(2)}) collective-permute-start(bf16[4,128,128]{2,1,0:T(8,128)(2,1)S(1)} %get-tuple-element.35), channel_id=1, source_target_pairs={{0,17},{1,16},{2,19},{3,18},{4,21},{5,20},{6,23},{7,22},{8,25},{9,... | collective-permute-start | bytes 393224 | tf_op jit(solution)/shard_map/ppermute | solution.py:63
  57.0 4.8 %collective-permute-start.9 = (bf16[144,128]{1,0:T(8,128)(2,1)S(1)}, bf16[144,128]{1,0:T(8,128)(2,1)S(1)}, u32[]{:S(2)}, u32[]{:S(2)}) collective-permute-start(bf16[144,128]{1,0:T(8,128)(2,1)S(1)} %get-tuple-element.37), channel_id=1, source_target_pairs={{0,2},{1,3},{2,0},{3,1},{4,6},{5,7},{6,4},{7,5},{8,10},{9,11},{10,... | collective-permute-start | bytes 110600 | tf_op jit(solution)/shard_map/ppermute | solution.py:63
  59.4 4.9 %collective-permute-start.10 = (bf16[144,128]{1,0:T(8,128)(2,1)S(1)}, bf16[144,128]{1,0:T(8,128)(2,1)S(1)}, u32[]{:S(2)}, u32[]{:S(2)}) collective-permute-start(bf16[144,128]{1,0:T(8,128)(2,1)S(1)} %get-tuple-element.38), channel_id=1, source_target_pairs={{0,4},{1,5},{2,6},{3,7},{4,0},{5,1},{6,2},{7,3},{8,12},{9,13},{10,... | collective-permute-start | bytes 110600 | tf_op jit(solution)/shard_map/ppermute | solution.py:63
  59.4 5.8 %collective-permute-start.11 = (bf16[144,128]{1,0:T(8,128)(2,1)S(1)}, bf16[144,128]{1,0:T(8,128)(2,1)S(1)}, u32[]{:S(2)}, u32[]{:S(2)}) collective-permute-start(bf16[144,128]{1,0:T(8,128)(2,1)S(1)} %get-tuple-element.39), channel_id=1, source_target_pairs={{0,6},{1,7},{2,4},{3,5},{4,2},{5,3},{6,0},{7,1},{8,14},{9,15},{10,... | collective-permute-start | bytes 110600 | tf_op jit(solution)/shard_map/ppermute | solution.py:63
  65.7 4.5 %collective-permute-start.12 = (bf16[144,128]{1,0:T(8,128)(2,1)S(1)}, bf16[144,128]{1,0:T(8,128)(2,1)S(1)}, u32[]{:S(2)}, u32[]{:S(2)}) collective-permute-start(bf16[144,128]{1,0:T(8,128)(2,1)S(1)} %get-tuple-element.41), channel_id=1, source_target_pairs={{0,2},{1,3},{2,0},{3,1},{4,6},{5,7},{6,4},{7,5},{8,10},{9,11},{10,... | collective-permute-start | bytes 110600 | tf_op jit(solution)/shard_map/ppermute | solution.py:63
  65.8 4.9 %collective-permute-start.13 = (bf16[144,128]{1,0:T(8,128)(2,1)S(1)}, bf16[144,128]{1,0:T(8,128)(2,1)S(1)}, u32[]{:S(2)}, u32[]{:S(2)}) collective-permute-start(bf16[144,128]{1,0:T(8,128)(2,1)S(1)} %get-tuple-element.42), channel_id=1, source_target_pairs={{0,4},{1,5},{2,6},{3,7},{4,0},{5,1},{6,2},{7,3},{8,12},{9,13},{10,... | collective-permute-start | bytes 110600 | tf_op jit(solution)/shard_map/ppermute | solution.py:63
  68.8 5.8 %collective-permute-start.14 = (bf16[144,128]{1,0:T(8,128)(2,1)S(1)}, bf16[144,128]{1,0:T(8,128)(2,1)S(1)}, u32[]{:S(2)}, u32[]{:S(2)}) collective-permute-start(bf16[144,128]{1,0:T(8,128)(2,1)S(1)} %get-tuple-element.43), channel_id=1, source_target_pairs={{0,6},{1,7},{2,4},{3,5},{4,2},{5,3},{6,0},{7,1},{8,14},{9,15},{10,... | collective-permute-start | bytes 110600 | tf_op jit(solution)/shard_map/ppermute | solution.py:63
  74.6 6.1 %collective-permute-start.17 = (bf16[4,144,128]{2,1,0:T(8,128)(2,1)S(1)}, bf16[4,144,128]{2,1,0:T(8,128)(2,1)S(1)}, u32[]{:S(2)}, u32[]{:S(2)}) collective-permute-start(bf16[4,144,128]{2,1,0:T(8,128)(2,1)S(1)} %pad_maximum_fusion.1.refs_0_), channel_id=1, source_target_pairs={{0,17},{1,16},{2,19},{3,18},{4,21},{5,20},{6,23},{7,22},{8,25},{9,... | collective-permute-start | bytes 442376 | tf_op jit(solution)/shard_map/ppermute | solution.py:63
  75.9 6.2 %collective-permute-start.16 = (bf16[4,144,128]{2,1,0:T(8,128)(2,1)S(1)}, bf16[4,144,128]{2,1,0:T(8,128)(2,1)S(1)}, u32[]{:S(2)}, u32[]{:S(2)}) collective-permute-start(bf16[4,144,128]{2,1,0:T(8,128)(2,1)S(1)} %pad_maximum_fusion.1.refs_0_), channel_id=1, source_target_pairs={{0,16},{1,17},{2,18},{3,19},{4,20},{5,21},{6,22},{7,23},{8,24},{9,... | collective-permute-start | bytes 442376 | tf_op jit(solution)/shard_map/ppermute | solution.py:63
  77.4 5.1 %collective-permute-start.15 = (bf16[4,144,128]{2,1,0:T(8,128)(2,1)S(1)}, bf16[4,144,128]{2,1,0:T(8,128)(2,1)S(1)}, u32[]{:S(2)}, u32[]{:S(2)}) collective-permute-start(bf16[4,144,128]{2,1,0:T(8,128)(2,1)S(1)} %pad_maximum_fusion.1.refs_0_), channel_id=1, source_target_pairs={{0,1},{1,0},{2,3},{3,2},{4,5},{5,4},{6,7},{7,6},{8,9},{9,8},{10,11... | collective-permute-start | bytes 442376 | tf_op jit(solution)/shard_map/ppermute | solution.py:63
  78.1 4.6 %collective-permute-start.18 = (bf16[4,144,128]{2,1,0:T(8,128)(2,1)S(1)}, bf16[4,144,128]{2,1,0:T(8,128)(2,1)S(1)}, u32[]{:S(2)}, u32[]{:S(2)}) collective-permute-start(bf16[4,144,128]{2,1,0:T(8,128)(2,1)S(1)} %pad_maximum_fusion.1.refs_0_), channel_id=1, source_target_pairs={{0,8},{1,9},{2,10},{3,11},{4,12},{5,13},{6,14},{7,15},{8,0},{9,1},... | collective-permute-start | bytes 442376 | tf_op jit(solution)/shard_map/ppermute | solution.py:63
  80.7 2.0 %collective-permute-start.21 = (bf16[4,144,128]{2,1,0:T(8,128)(2,1)S(1)}, bf16[4,144,128]{2,1,0:T(8,128)(2,1)S(1)}, u32[]{:S(2)}, u32[]{:S(2)}) collective-permute-start(bf16[4,144,128]{2,1,0:T(8,128)(2,1)S(1)} %collective-permute-done.17.refs_3_), channel_id=1, source_target_pairs={{0,8},{1,9},{2,10},{3,11},{4,12},{5,13},{6,14},{7,15},{8,0},{9,1},... | collective-permute-start | bytes 442376 | tf_op jit(solution)/shard_map/ppermute | solution.py:63
  82.1 1.4 %collective-permute-start.20 = (bf16[4,144,128]{2,1,0:T(8,128)(2,1)S(1)}, bf16[4,144,128]{2,1,0:T(8,128)(2,1)S(1)}, u32[]{:S(2)}, u32[]{:S(2)}) collective-permute-start(bf16[4,144,128]{2,1,0:T(8,128)(2,1)S(1)} %collective-permute-done.16.refs_2_), channel_id=1, source_target_pairs={{0,8},{1,9},{2,10},{3,11},{4,12},{5,13},{6,14},{7,15},{8,0},{9,1},... | collective-permute-start | bytes 442376 | tf_op jit(solution)/shard_map/ppermute | solution.py:63
  82.5 1.4 %collective-permute-start.19 = (bf16[4,144,128]{2,1,0:T(8,128)(2,1)S(1)}, bf16[4,144,128]{2,1,0:T(8,128)(2,1)S(1)}, u32[]{:S(2)}, u32[]{:S(2)}) collective-permute-start(bf16[4,144,128]{2,1,0:T(8,128)(2,1)S(1)} %collective-permute-done.15.refs_1_), channel_id=1, source_target_pairs={{0,8},{1,9},{2,10},{3,11},{4,12},{5,13},{6,14},{7,15},{8,0},{9,1},... | collective-permute-start | bytes 442376 | tf_op jit(solution)/shard_map/ppermute | solution.py:63

commit v7 on v6

--- a/solution.py
+++ b/solution.py
@@ -81,7 +81,7 @@
         self.yz_rows = max(1, ncols * depth // 2 // chips)
         self.yz_shares = ncols * depth // 2 // self.yz_rows
         self.xz_slot = -(-self.xz_rows // 8) * 8
-        even = lambda rows: -(-rows // 16) * 16
+        even = lambda rows: -(-rows // 8) * 8
         self.xz = self.each
         self.small = self.xz + self.xz_slot
         self.yz = self.small + 2
@@ -416,10 +416,9 @@
     tail[0:2, :] = total[shares.mid_small : shares.mid_yz]
     for j in range(2 * layers):
         tail[2 + j * size : 2 + (j + 1) * size, :] = by_col[j, 0:size, :]
-    common = total[: shares.each].astype(BF16)
     for t, out in enumerate(outs):
-        out[0 : shares.each, :] = common
-        out[shares.each :, :] = jnp.concatenate([by_row[(layer ^ t) // 2], tail[...]], axis=0).astype(BF16)
+        pieces = [total[: shares.each], by_row[(layer ^ t) // 2], tail[...]]
+        out[...] = jnp.concatenate(pieces, axis=0).astype(BF16)
 
 
 def last_kernel(shares, classes, place, *refs):
@@ -433,8 +432,9 @@
         for t in range(shares.layers):
             index = (plane ^ k) * shares.layers + (layer ^ t)
             for half, block in ((core, halves[k]), (1 - core, halves[shares.planes + k])):
-                whole[half, index] = block[t, 0:each, :]
-                rest[half, index] = block[t, each:, :].astype(F32)
+                value = block[t].astype(F32)
+                whole[half, index] = value[0:each].astype(BF16)
+                rest[half, index] = value[each:]
 
     def take(start, ref, lead, lanes):
         for side, index, row, offset, rows in shares.split(start, width if lead is not None else ref.shape[0]):
@@ -490,16 +490,8 @@
     hidden, classes = w3.shape
     count = grid.count
     side = grid.iy % count
-    emb = time_embedding(timestep, width)
-    temb = jnp.dot(emb, time_weight.astype(F32), precision=lax.Precision.HIGHEST)
     flat_one = conv1_weight.reshape(9 * width, width)
     flat_two = conv2_weight.reshape(9 * width, width)
-    back_flat = jnp.transpose(conv2_weight[::-1, ::-1], (0, 1, 3, 2)).reshape(9 * width, width)
-    w3_wide = jnp.stack(
-        [jnp.pad(w3, ((0, 0), (CLASS_ROWS * k, LANES - classes - CLASS_ROWS * k))) for k in range(depth)]
-    )
-    chunks = nrows // 16
-    labels_by_depth = labels.astype(F32).reshape(chunks, -1, depth).transpose(0, 2, 1)
 
     up = lambda i, j: (i + 1, j)
     down = lambda i, j: (i - 1, j)
@@ -522,6 +514,9 @@
 
     above = grid.move(row(xy_noisy[nrows - REACH :], labels[nrows - 1 :], first[ncols + share - 1]), up)
     below = grid.move(row(xy_noisy[:REACH], labels[:1], first[ncols]), down)
+    above, late_conv2, late_time, late_w3, late_labels, late_step = lax.optimization_barrier(
+        (above, conv2_weight, time_weight, w3, labels, timestep)
+    )
     edge_row = jnp.where(side == 0, below[4:, :depth], above[4:, :depth])
 
     def column(at, where):
@@ -537,6 +532,15 @@
 
     before = grid.move(column(ncols - 1, slice(ncols - REACH, ncols)), right)
     after = grid.move(column(0, slice(0, REACH)), left)
+
+    emb = time_embedding(late_step, width)
+    temb = jnp.dot(emb, late_time.astype(F32), precision=lax.Precision.HIGHEST)
+    back_flat = jnp.transpose(late_conv2[::-1, ::-1], (0, 1, 3, 2)).reshape(9 * width, width)
+    w3_wide = jnp.stack(
+        [jnp.pad(late_w3, ((0, 0), (CLASS_ROWS * k, LANES - classes - CLASS_ROWS * k))) for k in range(depth)]
+    )
+    chunks = nrows // 16
+    labels_by_depth = late_labels.astype(F32).reshape(chunks, -1, depth).transpose(0, 2, 1)
 
     core = grid.ix % 2
     flags = jnp.stack(

time: 86.3 us -> 85.9 us (level)
    unnamed x30 -> x29, local copies, waits for them, and re-layouts: 2.9 us -> 2.7 us
  transfers between devices with their start and end apart: 22 -> 22, of which waited for: 16 -> 15; matrix products, arithmetic and copies ran while one was open for 2% -> 2% of each run, Pallas kernels for 0% -> 0%
where the time goes in v7:
time: 85.9 us; the launch traced here: 85.3 us
  starting transfers between devices  31.9 us (37%)
  waiting for transfers between devices  29 us (34%)
  Pallas kernels  17.4 us (20%)
  local copies, waits for them, and re-layouts  4.58 us (5%)
  between operations  1.8 us (2%)
    ppermute x22, starting transfers between devices, move(): return lax.ppermute(array, BOTH, pairs)  31.9 us
    ppermute x22, waiting for transfers between devices, move(): return lax.ppermute(array, BOTH, pairs)  29 us
    pallas_call x1, Pallas kernels, local(): pl.pallas_call(functools.partial(main_kernel, classes, shares), out_shape...  14.7 us
    unnamed x29, local copies, waits for them, and re-layouts  2.7 us
    pallas_call x1, Pallas kernels, local(): pl.pallas_call(functools.partial(last_kernel, shares, classes), out_shape...  1.94 us
  transfers between devices with their start and end apart: 22, of which 15 were waited for; matrix products, arithmetic and copies ran while one was open for 2% of the time, Pallas kernels for 0%

profile of v7, /device:TPU:0, one launch (start us, length us, event | category | flops | bytes accessed | tf_op | source)
XLA Modules:
  0.0 85.3 jit_solution(16251216578152473644)
XLA Ops:
  1.4 0.3 copy-done
  1.7 0.8 constant_dynamic-slice_fusion.1
  2.6 0.7 collective-permute-start
  3.3 0.7 copy-done.8
  4.0 0.3 copy.30
  4.8 6.6 %collective-permute-start.1 = (bf16[5,16,128]{2,1,0:T(8,128)(2,1)S(1)}, bf16[5,16,128]{2,1,0:T(8,128)(2,1)S(1)}, u32[]{:S(2)}, u32[]{:S(2)}) collective-permute-start(bf16[5,16,128]{2,1,0:T(8,128)(2,1)S(1)} %fusion.6), channel_id=1, source_target_pairs={{0,8},{1,9},{2,10},{3,11},{4,12},{5,13},{6,14},{7,15},{8,16},{9,17... | collective-permute-start | bytes 61448 | tf_op jit(solution)/shard_map/ppermute | solution.py:63
  11.3 1.3 %collective-permute-start.2 = (bf16[5,16,128]{2,1,0:T(8,128)(2,1)S(1)}, bf16[5,16,128]{2,1,0:T(8,128)(2,1)S(1)}, u32[]{:S(2)}, u32[]{:S(2)}) collective-permute-start(bf16[5,16,128]{2,1,0:T(8,128)(2,1)S(1)} %fusion.8), channel_id=1, source_target_pairs={{8,0},{9,1},{10,2},{11,3},{12,4},{13,5},{14,6},{15,7},{16,8},{17,9... | collective-permute-start | bytes 61448 | tf_op jit(solution)/shard_map/ppermute | solution.py:63
  12.8 0.7 copy-done.10
  13.5 0.1 copy.38
  13.8 0.1 reshape.50
  13.9 5.2 %collective-permute-done.2.below = bf16[5,16,128]{2,1,0:T(8,128)(2,1)S(1)} collective-permute-done((bf16[5,16,128]{2,1,0:T(8,128)(2,1)S(1)}, bf16[5,16,128]{2,1,0:T(8,128)(2,1)S(1)}, u32[]{:S(2)}, u32[]{:S(2)}) %collective-permute-start.2) | collective-permute-done | bytes 20512 | tf_op jit(solution)/shard_map/ppermute | solution.py:63
  19.1 0.2 pad_maximum_fusion.2
  19.3 1.3 %collective-permute-start.4 = (bf16[103,4,128]{2,1,0:T(4,128)(2,1)S(1)}, bf16[103,4,128]{2,1,0:T(4,128)(2,1)S(1)}, u32[]{:S(2)}, u32[]{:S(2)}) collective-permute-start(bf16[103,4,128]{2,1,0:T(4,128)(2,1)S(1)} %get-tuple-element.82), channel_id=1, source_target_pairs={{1,0},{2,1},{3,2},{4,3},{5,4},{6,5},{7,6},{9,8},{10,9},{11,10},{12... | collective-permute-start | bytes 316424 | tf_op jit(solution)/shard_map/ppermute | solution.py:63
  20.6 4.6 %collective-permute-start.3 = (bf16[103,4,128]{2,1,0:T(4,128)(2,1)S(1)}, bf16[103,4,128]{2,1,0:T(4,128)(2,1)S(1)}, u32[]{:S(2)}, u32[]{:S(2)}) collective-permute-start(bf16[103,4,128]{2,1,0:T(4,128)(2,1)S(1)} %get-tuple-element.83), channel_id=1, source_target_pairs={{0,1},{1,2},{2,3},{3,4},{4,5},{5,6},{6,7},{8,9},{9,10},{10,11},{11... | collective-permute-start | bytes 316424 | tf_op jit(solution)/shard_map/ppermute | solution.py:63
  25.2 0.1 pad_bitcast_fusion.3
  25.4 0.2 copy.37
  25.6 0.5 copy-done.9
  26.1 0.1 fusion.18.temb
  26.3 3.2 %collective-permute-done.3.before = bf16[103,4,128]{2,1,0:T(4,128)(2,1)S(1)} collective-permute-done((bf16[103,4,128]{2,1,0:T(4,128)(2,1)S(1)}, bf16[103,4,128]{2,1,0:T(4,128)(2,1)S(1)}, u32[]{:S(2)}, u32[]{:S(2)}) %collective-permute-start.3) | collective-permute-done | bytes 105504 | tf_op jit(solution)/shard_map/ppermute | solution.py:63
  29.5 14.7 %tile.1 = (bf16[4,4,120,128]{3,2,1,0:T(8,128)(2,1)S(1)}, bf16[4,4,120,128]{3,2,1,0:T(8,128)(2,1)S(1)}) custom-call(s32[10]{0:T(128)S(1)} %stack.70.place, bf16[64,16,128]{2,1,0:T(8,128)(2,1)S(1)} %copy-done.2, bf16[5,16,128]{2,1,0:T(8,128)(2,1)S(1)} %collective-permute-done.1.above, bf16[5,16,128]{2,1,0:T(8,128)(2,1)S(1)} %collective-permute-done.2.below, ...), custom_call_target="tpu_custom_call" | custom-call | tf_op jit(solution)/shard_map/tile/pallas_call | solution.py:566
  44.2 0.4 collective-permute-start.5
  44.6 1.6 %collective-permute-done.5.other = bf16[4,4,120,128]{3,2,1,0:T(8,128)(2,1)S(1)} collective-permute-done((bf16[4,4,120,128]{3,2,1,0:T(8,128)(2,1)S(1)}, bf16[4,4,120,128]{3,2,1,0:T(8,128)(2,1)S(1)}, u32[]{:S(2)}, u32[]{:S(2)}) %collective-permute-start.5) | collective-permute-done | bytes 491552 | tf_op jit(solution)/shard_map/ppermute | solution.py:63
  46.1 0.1 cores.1
  46.3 2.6 %collective-permute-start.6 = (bf16[4,120,128]{2,1,0:T(8,128)(2,1)S(1)}, bf16[4,120,128]{2,1,0:T(8,128)(2,1)S(1)}, u32[]{:S(2)}, u32[]{:S(2)}) collective-permute-start(bf16[4,120,128]{2,1,0:T(8,128)(2,1)S(1)} %get-tuple-element.45), channel_id=1, source_target_pairs={{0,1},{1,0},{2,3},{3,2},{4,5},{5,4},{6,7},{7,6},{8,9},{9,8},{10,11... | collective-permute-start | bytes 368648 | tf_op jit(solution)/shard_map/ppermute | solution.py:63
  48.8 0.8 collective-permute-start.7
  49.6 0.8 collective-permute-start.8
  50.4 2.1 %collective-permute-done.6.refs_1_ = bf16[4,120,128]{2,1,0:T(8,128)(2,1)S(1)} collective-permute-done((bf16[4,120,128]{2,1,0:T(8,128)(2,1)S(1)}, bf16[4,120,128]{2,1,0:T(8,128)(2,1)S(1)}, u32[]{:S(2)}, u32[]{:S(2)}) %collective-permute-start.6) | collective-permute-done | bytes 122912 | tf_op jit(solution)/shard_map/ppermute | solution.py:63
  52.4 2.6 %collective-permute-done.7.refs_2_ = bf16[4,120,128]{2,1,0:T(8,128)(2,1)S(1)} collective-permute-done((bf16[4,120,128]{2,1,0:T(8,128)(2,1)S(1)}, bf16[4,120,128]{2,1,0:T(8,128)(2,1)S(1)}, u32[]{:S(2)}, u32[]{:S(2)}) %collective-permute-start.7) | collective-permute-done | bytes 122912 | tf_op jit(solution)/shard_map/ppermute | solution.py:63
  55.0 1.3 %collective-permute-done.8.refs_3_ = bf16[4,120,128]{2,1,0:T(8,128)(2,1)S(1)} collective-permute-done((bf16[4,120,128]{2,1,0:T(8,128)(2,1)S(1)}, bf16[4,120,128]{2,1,0:T(8,128)(2,1)S(1)}, u32[]{:S(2)}, u32[]{:S(2)}) %collective-permute-start.8) | collective-permute-done | bytes 122912 | tf_op jit(solution)/shard_map/ppermute | solution.py:63
  56.4 2.6 %collective-permute-start.9 = (bf16[136,128]{1,0:T(8,128)(2,1)S(1)}, bf16[136,128]{1,0:T(8,128)(2,1)S(1)}, u32[]{:S(2)}, u32[]{:S(2)}) collective-permute-start(bf16[136,128]{1,0:T(8,128)(2,1)S(1)} %get-tuple-element.49), channel_id=1, source_target_pairs={{0,2},{1,3},{2,0},{3,1},{4,6},{5,7},{6,4},{7,5},{8,10},{9,11},{10,... | collective-permute-start | bytes 104456 | tf_op jit(solution)/shard_map/ppermute | solution.py:63
  59.0 2.4 %collective-permute-start.11 = (bf16[136,128]{1,0:T(8,128)(2,1)S(1)}, bf16[136,128]{1,0:T(8,128)(2,1)S(1)}, u32[]{:S(2)}, u32[]{:S(2)}) collective-permute-start(bf16[136,128]{1,0:T(8,128)(2,1)S(1)} %get-tuple-element.51), channel_id=1, source_target_pairs={{0,6},{1,7},{2,4},{3,5},{4,2},{5,3},{6,0},{7,1},{8,14},{9,15},{10,... | collective-permute-start | bytes 104456 | tf_op jit(solution)/shard_map/ppermute | solution.py:63
  61.4 2.4 %collective-permute-done.10.refs_2_ = bf16[136,128]{1,0:T(8,128)(2,1)S(1)} collective-permute-done((bf16[136,128]{1,0:T(8,128)(2,1)S(1)}, bf16[136,128]{1,0:T(8,128)(2,1)S(1)}, u32[]{:S(2)}, u32[]{:S(2)}) %collective-permute-start.10) | collective-permute-done | bytes 34848 | tf_op jit(solution)/shard_map/ppermute | solution.py:63
  63.8 0.9 %collective-permute-done.11.refs_3_ = bf16[136,128]{1,0:T(8,128)(2,1)S(1)} collective-permute-done((bf16[136,128]{1,0:T(8,128)(2,1)S(1)}, bf16[136,128]{1,0:T(8,128)(2,1)S(1)}, u32[]{:S(2)}, u32[]{:S(2)}) %collective-permute-start.11) | collective-permute-done | bytes 34848 | tf_op jit(solution)/shard_map/ppermute | solution.py:63
  64.7 0.6 layers.1
  65.4 3.0 %collective-permute-start.13 = (bf16[136,128]{1,0:T(8,128)(2,1)S(1)}, bf16[136,128]{1,0:T(8,128)(2,1)S(1)}, u32[]{:S(2)}, u32[]{:S(2)}) collective-permute-start(bf16[136,128]{1,0:T(8,128)(2,1)S(1)} %get-tuple-element.54), channel_id=1, source_target_pairs={{0,4},{1,5},{2,6},{3,7},{4,0},{5,1},{6,2},{7,3},{8,12},{9,13},{10,... | collective-permute-start | bytes 104456 | tf_op jit(solution)/shard_map/ppermute | solution.py:63
  68.4 1.4 %collective-permute-start.14 = (bf16[136,128]{1,0:T(8,128)(2,1)S(1)}, bf16[136,128]{1,0:T(8,128)(2,1)S(1)}, u32[]{:S(2)}, u32[]{:S(2)}) collective-permute-start(bf16[136,128]{1,0:T(8,128)(2,1)S(1)} %get-tuple-element.55), channel_id=1, source_target_pairs={{0,6},{1,7},{2,4},{3,5},{4,2},{5,3},{6,0},{7,1},{8,14},{9,15},{10,... | collective-permute-start | bytes 104456 | tf_op jit(solution)/shard_map/ppermute | solution.py:63
  69.8 0.5 collective-permute-done.13
  70.3 3.8 %collective-permute-done.14 = bf16[136,128]{1,0:T(8,128)(2,1)S(1)} collective-permute-done((bf16[136,128]{1,0:T(8,128)(2,1)S(1)}, bf16[136,128]{1,0:T(8,128)(2,1)S(1)}, u32[]{:S(2)}, u32[]{:S(2)}) %collective-permute-start.14) | collective-permute-done | bytes 34848 | tf_op jit(solution)/shard_map/ppermute | solution.py:63
  74.2 1.6 %collective-permute-start.17 = (bf16[4,136,128]{2,1,0:T(8,128)(2,1)S(1)}, bf16[4,136,128]{2,1,0:T(8,128)(2,1)S(1)}, u32[]{:S(2)}, u32[]{:S(2)}) collective-permute-start(bf16[4,136,128]{2,1,0:T(8,128)(2,1)S(1)} %pad_maximum_fusion.1.refs_0_), channel_id=1, source_target_pairs={{0,17},{1,16},{2,19},{3,18},{4,21},{5,20},{6,23},{7,22},{8,25},{9,... | collective-permute-start | bytes 417800 | tf_op jit(solution)/shard_map/ppermute | solution.py:63
  75.8 1.2 %collective-permute-start.16 = (bf16[4,136,128]{2,1,0:T(8,128)(2,1)S(1)}, bf16[4,136,128]{2,1,0:T(8,128)(2,1)S(1)}, u32[]{:S(2)}, u32[]{:S(2)}) collective-permute-start(bf16[4,136,128]{2,1,0:T(8,128)(2,1)S(1)} %pad_maximum_fusion.1.refs_0_), channel_id=1, source_target_pairs={{0,16},{1,17},{2,18},{3,19},{4,20},{5,21},{6,22},{7,23},{8,24},{9,... | collective-permute-start | bytes 417800 | tf_op jit(solution)/shard_map/ppermute | solution.py:63
  76.9 0.8 collective-permute-start.15
  77.7 2.5 %collective-permute-done.17.refs_3_ = bf16[4,136,128]{2,1,0:T(8,128)(2,1)S(1)} collective-permute-done((bf16[4,136,128]{2,1,0:T(8,128)(2,1)S(1)}, bf16[4,136,128]{2,1,0:T(8,128)(2,1)S(1)}, u32[]{:S(2)}, u32[]{:S(2)}) %collective-permute-start.17) | collective-permute-done | bytes 139296 | tf_op jit(solution)/shard_map/ppermute | solution.py:63
  80.2 1.3 %collective-permute-done.16.refs_2_ = bf16[4,136,128]{2,1,0:T(8,128)(2,1)S(1)} collective-permute-done((bf16[4,136,128]{2,1,0:T(8,128)(2,1)S(1)}, bf16[4,136,128]{2,1,0:T(8,128)(2,1)S(1)}, u32[]{:S(2)}, u32[]{:S(2)}) %collective-permute-start.16) | collective-permute-done | bytes 139296 | tf_op jit(solution)/shard_map/ppermute | solution.py:63
  81.5 0.5 collective-permute-done.15.refs_1_
  82.0 0.1 copy.42.refs_8_
  82.1 0.7 collective-permute-done.20.refs_6_
  82.8 0.5 collective-permute-done.19.refs_5_
  83.4 1.9 %spread.1 = (f32[9,128,128]{2,1,0:T(8,128)}, f32[9,128,128]{2,1,0:T(8,128)}, f32[128,128]{1,0:T(8,128)}, f32[128,256]{1,0:T(8,128)}, f32[256,256]{1,0:T(8,128)},...) custom-call(s32[10]{0:T(128)S(1)} %stack.70.place, ...), custom_call_target="tpu_custom_call" | custom-call | tf_op jit(solution)/shard_map/spread/pallas_call | solution.py:642
  (64 shorter events, 1.1 us)
Async XLA Ops:
  0.6 1.1 %copy-start = (bf16[32,64,128]{2,1,0:T(8,128)(2,1)S(1)}, bf16[32,64,128]{2,1,0:T(8,128)(2,1)}, u32[]{:S(2)}) copy-start(bf16[32,64,128]{2,1,0:T(8,128)(2,1)} %param.12) | copy-start | bytes 1572868
  0.6 2.6 %copy-start.2 = (bf16[64,16,128]{2,1,0:T(8,128)(2,1)S(1)}, bf16[64,16,128]{2,1,0:T(8,128)(2,1)}, u32[]{:S(2)}) copy-start(bf16[64,16,128]{2,1,0:T(8,128)(2,1)} %xy.1) | copy-start | bytes 786436
  2.6 2.1 %collective-permute-start = (bf16[48,4,128]{2,1,0:T(4,128)(2,1)S(1)}, bf16[48,4,128]{2,1,0:T(4,128)(2,1)S(1)}, u32[]{:S(2)}, u32[]{:S(2)}) collective-permute-start(bf16[48,4,128]{2,1,0:T(4,128)(2,1)S(1)} %pad_maximum_fusion.6), channel_id=1, source_target_pairs={{0,0},{1,1},{2,8},{3,9},{4,16},{5,17},{6,24},{7,25},{8,2},{9,3},{1... | collective-permute-start | bytes 147464 | tf_op jit(solution)/shard_map/ppermute | solution.py:63
  3.2 0.8 copy-start.8
  4.7 8.0 %copy-start.4 = (bf16[48,4,128]{2,1,0:T(4,128)(2,1)}, bf16[48,4,128]{2,1,0:T(4,128)(2,1)S(1)}, u32[]{:S(2)}) copy-start(bf16[48,4,128]{2,1,0:T(4,128)(2,1)S(1)} %collective-permute-done.first) | copy-start | bytes 147460
  4.8 7.9 %collective-permute-start.1 = (bf16[5,16,128]{2,1,0:T(8,128)(2,1)S(1)}, bf16[5,16,128]{2,1,0:T(8,128)(2,1)S(1)}, u32[]{:S(2)}, u32[]{:S(2)}) collective-permute-start(bf16[5,16,128]{2,1,0:T(8,128)(2,1)S(1)} %fusion.6), channel_id=1, source_target_pairs={{0,8},{1,9},{2,10},{3,11},{4,12},{5,13},{6,14},{7,15},{8,16},{9,17... | collective-permute-start | bytes 61448 | tf_op jit(solution)/shard_map/ppermute | solution.py:63
  11.3 7.7 %collective-permute-start.2 = (bf16[5,16,128]{2,1,0:T(8,128)(2,1)S(1)}, bf16[5,16,128]{2,1,0:T(8,128)(2,1)S(1)}, u32[]{:S(2)}, u32[]{:S(2)}) collective-permute-start(bf16[5,16,128]{2,1,0:T(8,128)(2,1)S(1)} %fusion.8), channel_id=1, source_target_pairs={{8,0},{9,1},{10,2},{11,3},{12,4},{13,5},{14,6},{15,7},{16,8},{17,9... | collective-permute-start | bytes 61448 | tf_op jit(solution)/shard_map/ppermute | solution.py:63
  12.8 0.7 copy-start.10
  13.9 5.2 %slice-start = ((bf16[48,4,128]{2,1,0:T(4,128)(2,1)}), bf16[32,4,128]{2,1,0:T(4,128)(2,1)S(1)}, s32[]{:S(2)}) async-start(bf16[48,4,128]{2,1,0:T(4,128)(2,1)} %copy-done.4), calls=%async_computation | async-start | bytes 65536 | tf_op jit(solution)/shard_map/slice | solution.py:531
  19.1 6.2 %copy-start.1 = (bf16[3,3,128,128]{3,2,1,0:T(8,128)(2,1)S(1)}, bf16[3,3,128,128]{3,2,1,0:T(8,128)(2,1)}, u32[]{:S(2)}) copy-start(bf16[3,3,128,128]{3,2,1,0:T(8,128)(2,1)} %param.17) | copy-start | bytes 884740
  19.3 7.0 %collective-permute-start.4 = (bf16[103,4,128]{2,1,0:T(4,128)(2,1)S(1)}, bf16[103,4,128]{2,1,0:T(4,128)(2,1)S(1)}, u32[]{:S(2)}, u32[]{:S(2)}) collective-permute-start(bf16[103,4,128]{2,1,0:T(4,128)(2,1)S(1)} %get-tuple-element.82), channel_id=1, source_target_pairs={{1,0},{2,1},{3,2},{4,3},{5,4},{6,5},{7,6},{9,8},{10,9},{11,10},{12... | collective-permute-start | bytes 316424 | tf_op jit(solution)/shard_map/ppermute | solution.py:63
  20.6 8.9 %collective-permute-start.3 = (bf16[103,4,128]{2,1,0:T(4,128)(2,1)S(1)}, bf16[103,4,128]{2,1,0:T(4,128)(2,1)S(1)}, u32[]{:S(2)}, u32[]{:S(2)}) collective-permute-start(bf16[103,4,128]{2,1,0:T(4,128)(2,1)S(1)} %get-tuple-element.83), channel_id=1, source_target_pairs={{0,1},{1,2},{2,3},{3,4},{4,5},{5,6},{6,7},{8,9},{9,10},{10,11},{11... | collective-permute-start | bytes 316424 | tf_op jit(solution)/shard_map/ppermute | solution.py:63
  25.4 0.8 copy-start.9
  26.1 3.4 %copy-start.3 = (bf16[3,3,128,128]{3,2,1,0:T(8,128)(2,1)S(1)}, bf16[3,3,128,128]{3,2,1,0:T(8,128)(2,1)}, u32[]{:S(2)}) copy-start(bf16[3,3,128,128]{3,2,1,0:T(8,128)(2,1)} %param.16) | copy-start | bytes 884740
  26.2 3.3 %copy-start.5 = (bf16[48,4,128]{2,1,0:T(4,128)(2,1)S(1)}, bf16[48,4,128]{2,1,0:T(4,128)(2,1)}, u32[]{:S(2)}) copy-start(bf16[48,4,128]{2,1,0:T(4,128)(2,1)} %copy-done.4) | copy-start | bytes 147460
  26.2 3.3 %copy-start.6 = (bf16[256,256]{1,0:T(8,128)(2,1)S(1)}, bf16[256,256]{1,0:T(8,128)(2,1)}, u32[]{:S(2)}) copy-start(bf16[256,256]{1,0:T(8,128)(2,1)} %w2.1) | copy-start | bytes 393220
  26.2 3.3 %copy-start.7 = (bf16[128,256]{1,0:T(8,128)(2,1)S(1)}, bf16[128,256]{1,0:T(8,128)(2,1)}, u32[]{:S(2)}) copy-start(bf16[128,256]{1,0:T(8,128)(2,1)} %w1.1) | copy-start | bytes 196612
  44.2 1.9 %collective-permute-start.5 = (bf16[4,4,120,128]{3,2,1,0:T(8,128)(2,1)S(1)}, bf16[4,4,120,128]{3,2,1,0:T(8,128)(2,1)S(1)}, u32[]{:S(2)}, u32[]{:S(2)}) collective-permute-start(bf16[4,4,120,128]{3,2,1,0:T(8,128)(2,1)S(1)} %get-tuple-element.43), channel_id=1, source_target_pairs={{0,8},{1,9},{2,10},{3,11},{4,12},{5,13},{6,14},{7,15},{8,0},{9,1},... | collective-permute-start | bytes 1474568 | tf_op jit(solution)/shard_map/ppermute | solution.py:63
  46.3 6.2 %collective-permute-start.6 = (bf16[4,120,128]{2,1,0:T(8,128)(2,1)S(1)}, bf16[4,120,128]{2,1,0:T(8,128)(2,1)S(1)}, u32[]{:S(2)}, u32[]{:S(2)}) collective-permute-start(bf16[4,120,128]{2,1,0:T(8,128)(2,1)S(1)} %get-tuple-element.45), channel_id=1, source_target_pairs={{0,1},{1,0},{2,3},{3,2},{4,5},{5,4},{6,7},{7,6},{8,9},{9,8},{10,11... | collective-permute-start | bytes 368648 | tf_op jit(solution)/shard_map/ppermute | solution.py:63
  48.8 6.2 %collective-permute-start.7 = (bf16[4,120,128]{2,1,0:T(8,128)(2,1)S(1)}, bf16[4,120,128]{2,1,0:T(8,128)(2,1)S(1)}, u32[]{:S(2)}, u32[]{:S(2)}) collective-permute-start(bf16[4,120,128]{2,1,0:T(8,128)(2,1)S(1)} %get-tuple-element.46), channel_id=1, source_target_pairs={{0,16},{1,17},{2,18},{3,19},{4,20},{5,21},{6,22},{7,23},{8,24},{9,... | collective-permute-start | bytes 368648 | tf_op jit(solution)/shard_map/ppermute | solution.py:63
  49.6 6.8 %collective-permute-start.8 = (bf16[4,120,128]{2,1,0:T(8,128)(2,1)S(1)}, bf16[4,120,128]{2,1,0:T(8,128)(2,1)S(1)}, u32[]{:S(2)}, u32[]{:S(2)}) collective-permute-start(bf16[4,120,128]{2,1,0:T(8,128)(2,1)S(1)} %get-tuple-element.47), channel_id=1, source_target_pairs={{0,17},{1,16},{2,19},{3,18},{4,21},{5,20},{6,23},{7,22},{8,25},{9,... | collective-permute-start | bytes 368648 | tf_op jit(solution)/shard_map/ppermute | solution.py:63
  56.4 5.0 %collective-permute-start.9 = (bf16[136,128]{1,0:T(8,128)(2,1)S(1)}, bf16[136,128]{1,0:T(8,128)(2,1)S(1)}, u32[]{:S(2)}, u32[]{:S(2)}) collective-permute-start(bf16[136,128]{1,0:T(8,128)(2,1)S(1)} %get-tuple-element.49), channel_id=1, source_target_pairs={{0,2},{1,3},{2,0},{3,1},{4,6},{5,7},{6,4},{7,5},{8,10},{9,11},{10,... | collective-permute-start | bytes 104456 | tf_op jit(solution)/shard_map/ppermute | solution.py:63
  59.0 4.8 %collective-permute-start.10 = (bf16[136,128]{1,0:T(8,128)(2,1)S(1)}, bf16[136,128]{1,0:T(8,128)(2,1)S(1)}, u32[]{:S(2)}, u32[]{:S(2)}) collective-permute-start(bf16[136,128]{1,0:T(8,128)(2,1)S(1)} %get-tuple-element.50), channel_id=1, source_target_pairs={{0,4},{1,5},{2,6},{3,7},{4,0},{5,1},{6,2},{7,3},{8,12},{9,13},{10,... | collective-permute-start | bytes 104456 | tf_op jit(solution)/shard_map/ppermute | solution.py:63
  59.0 5.7 %collective-permute-start.11 = (bf16[136,128]{1,0:T(8,128)(2,1)S(1)}, bf16[136,128]{1,0:T(8,128)(2,1)S(1)}, u32[]{:S(2)}, u32[]{:S(2)}) collective-permute-start(bf16[136,128]{1,0:T(8,128)(2,1)S(1)} %get-tuple-element.51), channel_id=1, source_target_pairs={{0,6},{1,7},{2,4},{3,5},{4,2},{5,3},{6,0},{7,1},{8,14},{9,15},{10,... | collective-permute-start | bytes 104456 | tf_op jit(solution)/shard_map/ppermute | solution.py:63
  65.3 4.5 %collective-permute-start.12 = (bf16[136,128]{1,0:T(8,128)(2,1)S(1)}, bf16[136,128]{1,0:T(8,128)(2,1)S(1)}, u32[]{:S(2)}, u32[]{:S(2)}) collective-permute-start(bf16[136,128]{1,0:T(8,128)(2,1)S(1)} %get-tuple-element.53), channel_id=1, source_target_pairs={{0,2},{1,3},{2,0},{3,1},{4,6},{5,7},{6,4},{7,5},{8,10},{9,11},{10,... | collective-permute-start | bytes 104456 | tf_op jit(solution)/shard_map/ppermute | solution.py:63
  65.4 4.9 %collective-permute-start.13 = (bf16[136,128]{1,0:T(8,128)(2,1)S(1)}, bf16[136,128]{1,0:T(8,128)(2,1)S(1)}, u32[]{:S(2)}, u32[]{:S(2)}) collective-permute-start(bf16[136,128]{1,0:T(8,128)(2,1)S(1)} %get-tuple-element.54), channel_id=1, source_target_pairs={{0,4},{1,5},{2,6},{3,7},{4,0},{5,1},{6,2},{7,3},{8,12},{9,13},{10,... | collective-permute-start | bytes 104456 | tf_op jit(solution)/shard_map/ppermute | solution.py:63
  68.4 5.7 %collective-permute-start.14 = (bf16[136,128]{1,0:T(8,128)(2,1)S(1)}, bf16[136,128]{1,0:T(8,128)(2,1)S(1)}, u32[]{:S(2)}, u32[]{:S(2)}) collective-permute-start(bf16[136,128]{1,0:T(8,128)(2,1)S(1)} %get-tuple-element.55), channel_id=1, source_target_pairs={{0,6},{1,7},{2,4},{3,5},{4,2},{5,3},{6,0},{7,1},{8,14},{9,15},{10,... | collective-permute-start | bytes 104456 | tf_op jit(solution)/shard_map/ppermute | solution.py:63
  74.2 6.0 %collective-permute-start.17 = (bf16[4,136,128]{2,1,0:T(8,128)(2,1)S(1)}, bf16[4,136,128]{2,1,0:T(8,128)(2,1)S(1)}, u32[]{:S(2)}, u32[]{:S(2)}) collective-permute-start(bf16[4,136,128]{2,1,0:T(8,128)(2,1)S(1)} %pad_maximum_fusion.1.refs_0_), channel_id=1, source_target_pairs={{0,17},{1,16},{2,19},{3,18},{4,21},{5,20},{6,23},{7,22},{8,25},{9,... | collective-permute-start | bytes 417800 | tf_op jit(solution)/shard_map/ppermute | solution.py:63
  75.8 5.7 %collective-permute-start.16 = (bf16[4,136,128]{2,1,0:T(8,128)(2,1)S(1)}, bf16[4,136,128]{2,1,0:T(8,128)(2,1)S(1)}, u32[]{:S(2)}, u32[]{:S(2)}) collective-permute-start(bf16[4,136,128]{2,1,0:T(8,128)(2,1)S(1)} %pad_maximum_fusion.1.refs_0_), channel_id=1, source_target_pairs={{0,16},{1,17},{2,18},{3,19},{4,20},{5,21},{6,22},{7,23},{8,24},{9,... | collective-permute-start | bytes 417800 | tf_op jit(solution)/shard_map/ppermute | solution.py:63
  76.9 5.1 %collective-permute-start.15 = (bf16[4,136,128]{2,1,0:T(8,128)(2,1)S(1)}, bf16[4,136,128]{2,1,0:T(8,128)(2,1)S(1)}, u32[]{:S(2)}, u32[]{:S(2)}) collective-permute-start(bf16[4,136,128]{2,1,0:T(8,128)(2,1)S(1)} %pad_maximum_fusion.1.refs_0_), channel_id=1, source_target_pairs={{0,1},{1,0},{2,3},{3,2},{4,5},{5,4},{6,7},{7,6},{8,9},{9,8},{10,11... | collective-permute-start | bytes 417800 | tf_op jit(solution)/shard_map/ppermute | solution.py:63
  77.7 4.4 %collective-permute-start.18 = (bf16[4,136,128]{2,1,0:T(8,128)(2,1)S(1)}, bf16[4,136,128]{2,1,0:T(8,128)(2,1)S(1)}, u32[]{:S(2)}, u32[]{:S(2)}) collective-permute-start(bf16[4,136,128]{2,1,0:T(8,128)(2,1)S(1)} %pad_maximum_fusion.1.refs_0_), channel_id=1, source_target_pairs={{0,8},{1,9},{2,10},{3,11},{4,12},{5,13},{6,14},{7,15},{8,0},{9,1},... | collective-permute-start | bytes 417800 | tf_op jit(solution)/shard_map/ppermute | solution.py:63
  80.2 2.0 %collective-permute-start.21 = (bf16[4,136,128]{2,1,0:T(8,128)(2,1)S(1)}, bf16[4,136,128]{2,1,0:T(8,128)(2,1)S(1)}, u32[]{:S(2)}, u32[]{:S(2)}) collective-permute-start(bf16[4,136,128]{2,1,0:T(8,128)(2,1)S(1)} %collective-permute-done.17.refs_3_), channel_id=1, source_target_pairs={{0,8},{1,9},{2,10},{3,11},{4,12},{5,13},{6,14},{7,15},{8,0},{9,1},... | collective-permute-start | bytes 417800 | tf_op jit(solution)/shard_map/ppermute | solution.py:63
  81.5 1.4 %collective-permute-start.20 = (bf16[4,136,128]{2,1,0:T(8,128)(2,1)S(1)}, bf16[4,136,128]{2,1,0:T(8,128)(2,1)S(1)}, u32[]{:S(2)}, u32[]{:S(2)}) collective-permute-start(bf16[4,136,128]{2,1,0:T(8,128)(2,1)S(1)} %collective-permute-done.16.refs_2_), channel_id=1, source_target_pairs={{0,8},{1,9},{2,10},{3,11},{4,12},{5,13},{6,14},{7,15},{8,0},{9,1},... | collective-permute-start | bytes 417800 | tf_op jit(solution)/shard_map/ppermute | solution.py:63
  82.0 1.4 %collective-permute-start.19 = (bf16[4,136,128]{2,1,0:T(8,128)(2,1)S(1)}, bf16[4,136,128]{2,1,0:T(8,128)(2,1)S(1)}, u32[]{:S(2)}, u32[]{:S(2)}) collective-permute-start(bf16[4,136,128]{2,1,0:T(8,128)(2,1)S(1)} %collective-permute-done.15.refs_1_), channel_id=1, source_target_pairs={{0,8},{1,9},{2,10},{3,11},{4,12},{5,13},{6,14},{7,15},{8,0},{9,1},... | collective-permute-start | bytes 417800 | tf_op jit(solution)/shard_map/ppermute | solution.py:63

commit v8 on v7

--- a/solution.py
+++ b/solution.py
@@ -326,9 +326,7 @@
             packed[half, index, row : row + rows, :] = block[offset : offset + rows]
 
     def weight_gradient(start, dout):
-        grad = dot_tn(dout, patch[0 : nrows * ncols])
-        for tap in range(9):
-            put(start + tap * width, grad[:, tap * width : (tap + 1) * width].T)
+        put(start, dot_tn(patch[0 : nrows * ncols, 0 : 9 * width], dout))
 
     packed[...] = jnp.zeros_like(packed)
 
@@ -539,7 +537,7 @@
     w3_wide = jnp.stack(
         [jnp.pad(late_w3, ((0, 0), (CLASS_ROWS * k, LANES - classes - CLASS_ROWS * k))) for k in range(depth)]
     )
-    chunks = nrows // 16
+    chunks = nrows // 32
     labels_by_depth = late_labels.astype(F32).reshape(chunks, -1, depth).transpose(0, 2, 1)
 
     core = grid.ix % 2

time: 85.9 us -> 85.6 us (level)
  no operation moved by 1% of the time
where the time goes in v8:
time: 85.6 us; the launch traced here: 85 us
  starting transfers between devices  31.9 us (37%)
  waiting for transfers between devices  29 us (34%)
  Pallas kernels  17.1 us (20%)
  local copies, waits for them, and re-layouts  4.58 us (5%)
  between operations  1.81 us (2%)
    ppermute x22, starting transfers between devices, move(): return lax.ppermute(array, BOTH, pairs)  31.9 us
    ppermute x22, waiting for transfers between devices, move(): return lax.ppermute(array, BOTH, pairs)  29 us
    pallas_call x1, Pallas kernels, local(): pl.pallas_call(functools.partial(main_kernel, classes, shares), out_shape...  14.4 us
    unnamed x29, local copies, waits for them, and re-layouts  2.7 us
    pallas_call x1, Pallas kernels, local(): pl.pallas_call(functools.partial(last_kernel, shares, classes), out_shape...  1.94 us
  transfers between devices with their start and end apart: 22, of which 15 were waited for; matrix products, arithmetic and copies ran while one was open for 2% of the time, Pallas kernels for 0%

profile of v8, /device:TPU:0, one launch (start us, length us, event | category | flops | bytes accessed | tf_op | source)
XLA Modules:
  0.0 85.0 jit_solution(8361333320238974423)
XLA Ops:
  1.4 0.3 copy-done
  1.7 0.8 constant_dynamic-slice_fusion.1
  2.6 0.7 collective-permute-start
  3.3 0.7 copy-done.8
  4.0 0.3 copy.30
  4.8 6.6 %collective-permute-start.1 = (bf16[5,16,128]{2,1,0:T(8,128)(2,1)S(1)}, bf16[5,16,128]{2,1,0:T(8,128)(2,1)S(1)}, u32[]{:S(2)}, u32[]{:S(2)}) collective-permute-start(bf16[5,16,128]{2,1,0:T(8,128)(2,1)S(1)} %fusion.6), channel_id=1, source_target_pairs={{0,8},{1,9},{2,10},{3,11},{4,12},{5,13},{6,14},{7,15},{8,16},{9,17... | collective-permute-start | bytes 61448 | tf_op jit(solution)/shard_map/ppermute | solution.py:63
  11.3 1.3 %collective-permute-start.2 = (bf16[5,16,128]{2,1,0:T(8,128)(2,1)S(1)}, bf16[5,16,128]{2,1,0:T(8,128)(2,1)S(1)}, u32[]{:S(2)}, u32[]{:S(2)}) collective-permute-start(bf16[5,16,128]{2,1,0:T(8,128)(2,1)S(1)} %fusion.8), channel_id=1, source_target_pairs={{8,0},{9,1},{10,2},{11,3},{12,4},{13,5},{14,6},{15,7},{16,8},{17,9... | collective-permute-start | bytes 61448 | tf_op jit(solution)/shard_map/ppermute | solution.py:63
  12.8 0.7 copy-done.10
  13.5 0.1 copy.38
  13.8 0.1 reshape.50
  13.9 5.2 %collective-permute-done.2.below = bf16[5,16,128]{2,1,0:T(8,128)(2,1)S(1)} collective-permute-done((bf16[5,16,128]{2,1,0:T(8,128)(2,1)S(1)}, bf16[5,16,128]{2,1,0:T(8,128)(2,1)S(1)}, u32[]{:S(2)}, u32[]{:S(2)}) %collective-permute-start.2) | collective-permute-done | bytes 20512 | tf_op jit(solution)/shard_map/ppermute | solution.py:63
  19.1 0.2 pad_maximum_fusion.2
  19.3 1.3 %collective-permute-start.4 = (bf16[103,4,128]{2,1,0:T(4,128)(2,1)S(1)}, bf16[103,4,128]{2,1,0:T(4,128)(2,1)S(1)}, u32[]{:S(2)}, u32[]{:S(2)}) collective-permute-start(bf16[103,4,128]{2,1,0:T(4,128)(2,1)S(1)} %get-tuple-element.82), channel_id=1, source_target_pairs={{1,0},{2,1},{3,2},{4,3},{5,4},{6,5},{7,6},{9,8},{10,9},{11,10},{12... | collective-permute-start | bytes 316424 | tf_op jit(solution)/shard_map/ppermute | solution.py:63
  20.6 4.6 %collective-permute-start.3 = (bf16[103,4,128]{2,1,0:T(4,128)(2,1)S(1)}, bf16[103,4,128]{2,1,0:T(4,128)(2,1)S(1)}, u32[]{:S(2)}, u32[]{:S(2)}) collective-permute-start(bf16[103,4,128]{2,1,0:T(4,128)(2,1)S(1)} %get-tuple-element.83), channel_id=1, source_target_pairs={{0,1},{1,2},{2,3},{3,4},{4,5},{5,6},{6,7},{8,9},{9,10},{10,11},{11... | collective-permute-start | bytes 316424 | tf_op jit(solution)/shard_map/ppermute | solution.py:63
  25.2 0.1 pad_bitcast_fusion.3
  25.4 0.2 copy.37
  25.6 0.5 copy-done.9
  26.1 0.1 fusion.18.temb
  26.3 3.2 %collective-permute-done.3.before = bf16[103,4,128]{2,1,0:T(4,128)(2,1)S(1)} collective-permute-done((bf16[103,4,128]{2,1,0:T(4,128)(2,1)S(1)}, bf16[103,4,128]{2,1,0:T(4,128)(2,1)S(1)}, u32[]{:S(2)}, u32[]{:S(2)}) %collective-permute-start.3) | collective-permute-done | bytes 105504 | tf_op jit(solution)/shard_map/ppermute | solution.py:63
  29.5 14.4 %tile.1 = (bf16[4,4,120,128]{3,2,1,0:T(8,128)(2,1)S(1)}, bf16[4,4,120,128]{3,2,1,0:T(8,128)(2,1)S(1)}) custom-call(s32[10]{0:T(128)S(1)} %stack.70.place, bf16[64,16,128]{2,1,0:T(8,128)(2,1)S(1)} %copy-done.2, bf16[5,16,128]{2,1,0:T(8,128)(2,1)S(1)} %collective-permute-done.1.above, bf16[5,16,128]{2,1,0:T(8,128)(2,1)S(1)} %collective-permute-done.2.below, ...), custom_call_target="tpu_custom_call" | custom-call | tf_op jit(solution)/shard_map/tile/pallas_call | solution.py:564
  43.9 0.4 collective-permute-start.5
  44.3 1.5 %collective-permute-done.5.other = bf16[4,4,120,128]{3,2,1,0:T(8,128)(2,1)S(1)} collective-permute-done((bf16[4,4,120,128]{3,2,1,0:T(8,128)(2,1)S(1)}, bf16[4,4,120,128]{3,2,1,0:T(8,128)(2,1)S(1)}, u32[]{:S(2)}, u32[]{:S(2)}) %collective-permute-start.5) | collective-permute-done | bytes 491552 | tf_op jit(solution)/shard_map/ppermute | solution.py:63
  45.8 0.1 cores.1
  46.0 2.6 %collective-permute-start.6 = (bf16[4,120,128]{2,1,0:T(8,128)(2,1)S(1)}, bf16[4,120,128]{2,1,0:T(8,128)(2,1)S(1)}, u32[]{:S(2)}, u32[]{:S(2)}) collective-permute-start(bf16[4,120,128]{2,1,0:T(8,128)(2,1)S(1)} %get-tuple-element.45), channel_id=1, source_target_pairs={{0,1},{1,0},{2,3},{3,2},{4,5},{5,4},{6,7},{7,6},{8,9},{9,8},{10,11... | collective-permute-start | bytes 368648 | tf_op jit(solution)/shard_map/ppermute | solution.py:63
  48.5 0.8 collective-permute-start.7
  49.3 0.8 collective-permute-start.8
  50.0 2.1 %collective-permute-done.6.refs_1_ = bf16[4,120,128]{2,1,0:T(8,128)(2,1)S(1)} collective-permute-done((bf16[4,120,128]{2,1,0:T(8,128)(2,1)S(1)}, bf16[4,120,128]{2,1,0:T(8,128)(2,1)S(1)}, u32[]{:S(2)}, u32[]{:S(2)}) %collective-permute-start.6) | collective-permute-done | bytes 122912 | tf_op jit(solution)/shard_map/ppermute | solution.py:63
  52.1 2.6 %collective-permute-done.7.refs_2_ = bf16[4,120,128]{2,1,0:T(8,128)(2,1)S(1)} collective-permute-done((bf16[4,120,128]{2,1,0:T(8,128)(2,1)S(1)}, bf16[4,120,128]{2,1,0:T(8,128)(2,1)S(1)}, u32[]{:S(2)}, u32[]{:S(2)}) %collective-permute-start.7) | collective-permute-done | bytes 122912 | tf_op jit(solution)/shard_map/ppermute | solution.py:63
  54.7 1.3 %collective-permute-done.8.refs_3_ = bf16[4,120,128]{2,1,0:T(8,128)(2,1)S(1)} collective-permute-done((bf16[4,120,128]{2,1,0:T(8,128)(2,1)S(1)}, bf16[4,120,128]{2,1,0:T(8,128)(2,1)S(1)}, u32[]{:S(2)}, u32[]{:S(2)}) %collective-permute-start.8) | collective-permute-done | bytes 122912 | tf_op jit(solution)/shard_map/ppermute | solution.py:63
  56.1 2.6 %collective-permute-start.9 = (bf16[136,128]{1,0:T(8,128)(2,1)S(1)}, bf16[136,128]{1,0:T(8,128)(2,1)S(1)}, u32[]{:S(2)}, u32[]{:S(2)}) collective-permute-start(bf16[136,128]{1,0:T(8,128)(2,1)S(1)} %get-tuple-element.49), channel_id=1, source_target_pairs={{0,2},{1,3},{2,0},{3,1},{4,6},{5,7},{6,4},{7,5},{8,10},{9,11},{10,... | collective-permute-start | bytes 104456 | tf_op jit(solution)/shard_map/ppermute | solution.py:63
  58.7 2.4 %collective-permute-start.11 = (bf16[136,128]{1,0:T(8,128)(2,1)S(1)}, bf16[136,128]{1,0:T(8,128)(2,1)S(1)}, u32[]{:S(2)}, u32[]{:S(2)}) collective-permute-start(bf16[136,128]{1,0:T(8,128)(2,1)S(1)} %get-tuple-element.51), channel_id=1, source_target_pairs={{0,6},{1,7},{2,4},{3,5},{4,2},{5,3},{6,0},{7,1},{8,14},{9,15},{10,... | collective-permute-start | bytes 104456 | tf_op jit(solution)/shard_map/ppermute | solution.py:63
  61.1 2.4 %collective-permute-done.10.refs_2_ = bf16[136,128]{1,0:T(8,128)(2,1)S(1)} collective-permute-done((bf16[136,128]{1,0:T(8,128)(2,1)S(1)}, bf16[136,128]{1,0:T(8,128)(2,1)S(1)}, u32[]{:S(2)}, u32[]{:S(2)}) %collective-permute-start.10) | collective-permute-done | bytes 34848 | tf_op jit(solution)/shard_map/ppermute | solution.py:63
  63.5 0.9 %collective-permute-done.11.refs_3_ = bf16[136,128]{1,0:T(8,128)(2,1)S(1)} collective-permute-done((bf16[136,128]{1,0:T(8,128)(2,1)S(1)}, bf16[136,128]{1,0:T(8,128)(2,1)S(1)}, u32[]{:S(2)}, u32[]{:S(2)}) %collective-permute-start.11) | collective-permute-done | bytes 34848 | tf_op jit(solution)/shard_map/ppermute | solution.py:63
  64.4 0.6 layers.1
  65.1 3.0 %collective-permute-start.13 = (bf16[136,128]{1,0:T(8,128)(2,1)S(1)}, bf16[136,128]{1,0:T(8,128)(2,1)S(1)}, u32[]{:S(2)}, u32[]{:S(2)}) collective-permute-start(bf16[136,128]{1,0:T(8,128)(2,1)S(1)} %get-tuple-element.54), channel_id=1, source_target_pairs={{0,4},{1,5},{2,6},{3,7},{4,0},{5,1},{6,2},{7,3},{8,12},{9,13},{10,... | collective-permute-start | bytes 104456 | tf_op jit(solution)/shard_map/ppermute | solution.py:63
  68.1 1.4 %collective-permute-start.14 = (bf16[136,128]{1,0:T(8,128)(2,1)S(1)}, bf16[136,128]{1,0:T(8,128)(2,1)S(1)}, u32[]{:S(2)}, u32[]{:S(2)}) collective-permute-start(bf16[136,128]{1,0:T(8,128)(2,1)S(1)} %get-tuple-element.55), channel_id=1, source_target_pairs={{0,6},{1,7},{2,4},{3,5},{4,2},{5,3},{6,0},{7,1},{8,14},{9,15},{10,... | collective-permute-start | bytes 104456 | tf_op jit(solution)/shard_map/ppermute | solution.py:63
  69.5 0.5 collective-permute-done.13
  70.0 3.8 %collective-permute-done.14 = bf16[136,128]{1,0:T(8,128)(2,1)S(1)} collective-permute-done((bf16[136,128]{1,0:T(8,128)(2,1)S(1)}, bf16[136,128]{1,0:T(8,128)(2,1)S(1)}, u32[]{:S(2)}, u32[]{:S(2)}) %collective-permute-start.14) | collective-permute-done | bytes 34848 | tf_op jit(solution)/shard_map/ppermute | solution.py:63
  73.9 1.6 %collective-permute-start.17 = (bf16[4,136,128]{2,1,0:T(8,128)(2,1)S(1)}, bf16[4,136,128]{2,1,0:T(8,128)(2,1)S(1)}, u32[]{:S(2)}, u32[]{:S(2)}) collective-permute-start(bf16[4,136,128]{2,1,0:T(8,128)(2,1)S(1)} %pad_maximum_fusion.1.refs_0_), channel_id=1, source_target_pairs={{0,17},{1,16},{2,19},{3,18},{4,21},{5,20},{6,23},{7,22},{8,25},{9,... | collective-permute-start | bytes 417800 | tf_op jit(solution)/shard_map/ppermute | solution.py:63
  75.5 1.2 %collective-permute-start.16 = (bf16[4,136,128]{2,1,0:T(8,128)(2,1)S(1)}, bf16[4,136,128]{2,1,0:T(8,128)(2,1)S(1)}, u32[]{:S(2)}, u32[]{:S(2)}) collective-permute-start(bf16[4,136,128]{2,1,0:T(8,128)(2,1)S(1)} %pad_maximum_fusion.1.refs_0_), channel_id=1, source_target_pairs={{0,16},{1,17},{2,18},{3,19},{4,20},{5,21},{6,22},{7,23},{8,24},{9,... | collective-permute-start | bytes 417800 | tf_op jit(solution)/shard_map/ppermute | solution.py:63
  76.6 0.8 collective-permute-start.15
  77.4 2.5 %collective-permute-done.17.refs_3_ = bf16[4,136,128]{2,1,0:T(8,128)(2,1)S(1)} collective-permute-done((bf16[4,136,128]{2,1,0:T(8,128)(2,1)S(1)}, bf16[4,136,128]{2,1,0:T(8,128)(2,1)S(1)}, u32[]{:S(2)}, u32[]{:S(2)}) %collective-permute-start.17) | collective-permute-done | bytes 139296 | tf_op jit(solution)/shard_map/ppermute | solution.py:63
  79.9 1.3 %collective-permute-done.16.refs_2_ = bf16[4,136,128]{2,1,0:T(8,128)(2,1)S(1)} collective-permute-done((bf16[4,136,128]{2,1,0:T(8,128)(2,1)S(1)}, bf16[4,136,128]{2,1,0:T(8,128)(2,1)S(1)}, u32[]{:S(2)}, u32[]{:S(2)}) %collective-permute-start.16) | collective-permute-done | bytes 139296 | tf_op jit(solution)/shard_map/ppermute | solution.py:63
  81.2 0.5 collective-permute-done.15.refs_1_
  81.7 0.1 copy.42.refs_8_
  81.8 0.7 collective-permute-done.20.refs_6_
  82.5 0.5 collective-permute-done.19.refs_5_
  83.1 1.9 %spread.1 = (f32[9,128,128]{2,1,0:T(8,128)}, f32[9,128,128]{2,1,0:T(8,128)}, f32[128,128]{1,0:T(8,128)}, f32[128,256]{1,0:T(8,128)}, f32[256,256]{1,0:T(8,128)},...) custom-call(s32[10]{0:T(128)S(1)} %stack.70.place, ...), custom_call_target="tpu_custom_call" | custom-call | tf_op jit(solution)/shard_map/spread/pallas_call | solution.py:640
  (64 shorter events, 1.1 us)
Async XLA Ops:
  0.6 1.1 %copy-start = (bf16[32,64,128]{2,1,0:T(8,128)(2,1)S(1)}, bf16[32,64,128]{2,1,0:T(8,128)(2,1)}, u32[]{:S(2)}) copy-start(bf16[32,64,128]{2,1,0:T(8,128)(2,1)} %param.12) | copy-start | bytes 1572868
  0.6 2.6 %copy-start.2 = (bf16[64,16,128]{2,1,0:T(8,128)(2,1)S(1)}, bf16[64,16,128]{2,1,0:T(8,128)(2,1)}, u32[]{:S(2)}) copy-start(bf16[64,16,128]{2,1,0:T(8,128)(2,1)} %xy.1) | copy-start | bytes 786436
  2.6 2.1 %collective-permute-start = (bf16[48,4,128]{2,1,0:T(4,128)(2,1)S(1)}, bf16[48,4,128]{2,1,0:T(4,128)(2,1)S(1)}, u32[]{:S(2)}, u32[]{:S(2)}) collective-permute-start(bf16[48,4,128]{2,1,0:T(4,128)(2,1)S(1)} %pad_maximum_fusion.6), channel_id=1, source_target_pairs={{0,0},{1,1},{2,8},{3,9},{4,16},{5,17},{6,24},{7,25},{8,2},{9,3},{1... | collective-permute-start | bytes 147464 | tf_op jit(solution)/shard_map/ppermute | solution.py:63
  3.2 0.8 copy-start.8
  4.7 8.0 %copy-start.4 = (bf16[48,4,128]{2,1,0:T(4,128)(2,1)}, bf16[48,4,128]{2,1,0:T(4,128)(2,1)S(1)}, u32[]{:S(2)}) copy-start(bf16[48,4,128]{2,1,0:T(4,128)(2,1)S(1)} %collective-permute-done.first) | copy-start | bytes 147460
  4.8 7.9 %collective-permute-start.1 = (bf16[5,16,128]{2,1,0:T(8,128)(2,1)S(1)}, bf16[5,16,128]{2,1,0:T(8,128)(2,1)S(1)}, u32[]{:S(2)}, u32[]{:S(2)}) collective-permute-start(bf16[5,16,128]{2,1,0:T(8,128)(2,1)S(1)} %fusion.6), channel_id=1, source_target_pairs={{0,8},{1,9},{2,10},{3,11},{4,12},{5,13},{6,14},{7,15},{8,16},{9,17... | collective-permute-start | bytes 61448 | tf_op jit(solution)/shard_map/ppermute | solution.py:63
  11.3 7.7 %collective-permute-start.2 = (bf16[5,16,128]{2,1,0:T(8,128)(2,1)S(1)}, bf16[5,16,128]{2,1,0:T(8,128)(2,1)S(1)}, u32[]{:S(2)}, u32[]{:S(2)}) collective-permute-start(bf16[5,16,128]{2,1,0:T(8,128)(2,1)S(1)} %fusion.8), channel_id=1, source_target_pairs={{8,0},{9,1},{10,2},{11,3},{12,4},{13,5},{14,6},{15,7},{16,8},{17,9... | collective-permute-start | bytes 61448 | tf_op jit(solution)/shard_map/ppermute | solution.py:63
  12.8 0.7 copy-start.10
  13.9 5.2 %slice-start = ((bf16[48,4,128]{2,1,0:T(4,128)(2,1)}), bf16[32,4,128]{2,1,0:T(4,128)(2,1)S(1)}, s32[]{:S(2)}) async-start(bf16[48,4,128]{2,1,0:T(4,128)(2,1)} %copy-done.4), calls=%async_computation | async-start | bytes 65536 | tf_op jit(solution)/shard_map/slice | solution.py:529
  19.1 6.2 %copy-start.1 = (bf16[3,3,128,128]{3,2,1,0:T(8,128)(2,1)S(1)}, bf16[3,3,128,128]{3,2,1,0:T(8,128)(2,1)}, u32[]{:S(2)}) copy-start(bf16[3,3,128,128]{3,2,1,0:T(8,128)(2,1)} %param.17) | copy-start | bytes 884740
  19.3 7.0 %collective-permute-start.4 = (bf16[103,4,128]{2,1,0:T(4,128)(2,1)S(1)}, bf16[103,4,128]{2,1,0:T(4,128)(2,1)S(1)}, u32[]{:S(2)}, u32[]{:S(2)}) collective-permute-start(bf16[103,4,128]{2,1,0:T(4,128)(2,1)S(1)} %get-tuple-element.82), channel_id=1, source_target_pairs={{1,0},{2,1},{3,2},{4,3},{5,4},{6,5},{7,6},{9,8},{10,9},{11,10},{12... | collective-permute-start | bytes 316424 | tf_op jit(solution)/shard_map/ppermute | solution.py:63
  20.6 8.9 %collective-permute-start.3 = (bf16[103,4,128]{2,1,0:T(4,128)(2,1)S(1)}, bf16[103,4,128]{2,1,0:T(4,128)(2,1)S(1)}, u32[]{:S(2)}, u32[]{:S(2)}) collective-permute-start(bf16[103,4,128]{2,1,0:T(4,128)(2,1)S(1)} %get-tuple-element.83), channel_id=1, source_target_pairs={{0,1},{1,2},{2,3},{3,4},{4,5},{5,6},{6,7},{8,9},{9,10},{10,11},{11... | collective-permute-start | bytes 316424 | tf_op jit(solution)/shard_map/ppermute | solution.py:63
  25.4 0.8 copy-start.9
  26.1 3.4 %copy-start.3 = (bf16[3,3,128,128]{3,2,1,0:T(8,128)(2,1)S(1)}, bf16[3,3,128,128]{3,2,1,0:T(8,128)(2,1)}, u32[]{:S(2)}) copy-start(bf16[3,3,128,128]{3,2,1,0:T(8,128)(2,1)} %param.16) | copy-start | bytes 884740
  26.2 3.3 %copy-start.5 = (bf16[48,4,128]{2,1,0:T(4,128)(2,1)S(1)}, bf16[48,4,128]{2,1,0:T(4,128)(2,1)}, u32[]{:S(2)}) copy-start(bf16[48,4,128]{2,1,0:T(4,128)(2,1)} %copy-done.4) | copy-start | bytes 147460
  26.2 3.3 %copy-start.6 = (bf16[256,256]{1,0:T(8,128)(2,1)S(1)}, bf16[256,256]{1,0:T(8,128)(2,1)}, u32[]{:S(2)}) copy-start(bf16[256,256]{1,0:T(8,128)(2,1)} %w2.1) | copy-start | bytes 393220
  26.2 3.3 %copy-start.7 = (bf16[128,256]{1,0:T(8,128)(2,1)S(1)}, bf16[128,256]{1,0:T(8,128)(2,1)}, u32[]{:S(2)}) copy-start(bf16[128,256]{1,0:T(8,128)(2,1)} %w1.1) | copy-start | bytes 196612
  43.9 1.9 %collective-permute-start.5 = (bf16[4,4,120,128]{3,2,1,0:T(8,128)(2,1)S(1)}, bf16[4,4,120,128]{3,2,1,0:T(8,128)(2,1)S(1)}, u32[]{:S(2)}, u32[]{:S(2)}) collective-permute-start(bf16[4,4,120,128]{3,2,1,0:T(8,128)(2,1)S(1)} %get-tuple-element.43), channel_id=1, source_target_pairs={{0,8},{1,9},{2,10},{3,11},{4,12},{5,13},{6,14},{7,15},{8,0},{9,1},... | collective-permute-start | bytes 1474568 | tf_op jit(solution)/shard_map/ppermute | solution.py:63
  46.0 6.2 %collective-permute-start.6 = (bf16[4,120,128]{2,1,0:T(8,128)(2,1)S(1)}, bf16[4,120,128]{2,1,0:T(8,128)(2,1)S(1)}, u32[]{:S(2)}, u32[]{:S(2)}) collective-permute-start(bf16[4,120,128]{2,1,0:T(8,128)(2,1)S(1)} %get-tuple-element.45), channel_id=1, source_target_pairs={{0,1},{1,0},{2,3},{3,2},{4,5},{5,4},{6,7},{7,6},{8,9},{9,8},{10,11... | collective-permute-start | bytes 368648 | tf_op jit(solution)/shard_map/ppermute | solution.py:63
  48.5 6.2 %collective-permute-start.7 = (bf16[4,120,128]{2,1,0:T(8,128)(2,1)S(1)}, bf16[4,120,128]{2,1,0:T(8,128)(2,1)S(1)}, u32[]{:S(2)}, u32[]{:S(2)}) collective-permute-start(bf16[4,120,128]{2,1,0:T(8,128)(2,1)S(1)} %get-tuple-element.46), channel_id=1, source_target_pairs={{0,16},{1,17},{2,18},{3,19},{4,20},{5,21},{6,22},{7,23},{8,24},{9,... | collective-permute-start | bytes 368648 | tf_op jit(solution)/shard_map/ppermute | solution.py:63
  49.3 6.7 %collective-permute-start.8 = (bf16[4,120,128]{2,1,0:T(8,128)(2,1)S(1)}, bf16[4,120,128]{2,1,0:T(8,128)(2,1)S(1)}, u32[]{:S(2)}, u32[]{:S(2)}) collective-permute-start(bf16[4,120,128]{2,1,0:T(8,128)(2,1)S(1)} %get-tuple-element.47), channel_id=1, source_target_pairs={{0,17},{1,16},{2,19},{3,18},{4,21},{5,20},{6,23},{7,22},{8,25},{9,... | collective-permute-start | bytes 368648 | tf_op jit(solution)/shard_map/ppermute | solution.py:63
  56.1 5.0 %collective-permute-start.9 = (bf16[136,128]{1,0:T(8,128)(2,1)S(1)}, bf16[136,128]{1,0:T(8,128)(2,1)S(1)}, u32[]{:S(2)}, u32[]{:S(2)}) collective-permute-start(bf16[136,128]{1,0:T(8,128)(2,1)S(1)} %get-tuple-element.49), channel_id=1, source_target_pairs={{0,2},{1,3},{2,0},{3,1},{4,6},{5,7},{6,4},{7,5},{8,10},{9,11},{10,... | collective-permute-start | bytes 104456 | tf_op jit(solution)/shard_map/ppermute | solution.py:63
  58.7 4.8 %collective-permute-start.10 = (bf16[136,128]{1,0:T(8,128)(2,1)S(1)}, bf16[136,128]{1,0:T(8,128)(2,1)S(1)}, u32[]{:S(2)}, u32[]{:S(2)}) collective-permute-start(bf16[136,128]{1,0:T(8,128)(2,1)S(1)} %get-tuple-element.50), channel_id=1, source_target_pairs={{0,4},{1,5},{2,6},{3,7},{4,0},{5,1},{6,2},{7,3},{8,12},{9,13},{10,... | collective-permute-start | bytes 104456 | tf_op jit(solution)/shard_map/ppermute | solution.py:63
  58.7 5.7 %collective-permute-start.11 = (bf16[136,128]{1,0:T(8,128)(2,1)S(1)}, bf16[136,128]{1,0:T(8,128)(2,1)S(1)}, u32[]{:S(2)}, u32[]{:S(2)}) collective-permute-start(bf16[136,128]{1,0:T(8,128)(2,1)S(1)} %get-tuple-element.51), channel_id=1, source_target_pairs={{0,6},{1,7},{2,4},{3,5},{4,2},{5,3},{6,0},{7,1},{8,14},{9,15},{10,... | collective-permute-start | bytes 104456 | tf_op jit(solution)/shard_map/ppermute | solution.py:63
  65.0 4.5 %collective-permute-start.12 = (bf16[136,128]{1,0:T(8,128)(2,1)S(1)}, bf16[136,128]{1,0:T(8,128)(2,1)S(1)}, u32[]{:S(2)}, u32[]{:S(2)}) collective-permute-start(bf16[136,128]{1,0:T(8,128)(2,1)S(1)} %get-tuple-element.53), channel_id=1, source_target_pairs={{0,2},{1,3},{2,0},{3,1},{4,6},{5,7},{6,4},{7,5},{8,10},{9,11},{10,... | collective-permute-start | bytes 104456 | tf_op jit(solution)/shard_map/ppermute | solution.py:63
  65.1 4.9 %collective-permute-start.13 = (bf16[136,128]{1,0:T(8,128)(2,1)S(1)}, bf16[136,128]{1,0:T(8,128)(2,1)S(1)}, u32[]{:S(2)}, u32[]{:S(2)}) collective-permute-start(bf16[136,128]{1,0:T(8,128)(2,1)S(1)} %get-tuple-element.54), channel_id=1, source_target_pairs={{0,4},{1,5},{2,6},{3,7},{4,0},{5,1},{6,2},{7,3},{8,12},{9,13},{10,... | collective-permute-start | bytes 104456 | tf_op jit(solution)/shard_map/ppermute | solution.py:63
  68.1 5.7 %collective-permute-start.14 = (bf16[136,128]{1,0:T(8,128)(2,1)S(1)}, bf16[136,128]{1,0:T(8,128)(2,1)S(1)}, u32[]{:S(2)}, u32[]{:S(2)}) collective-permute-start(bf16[136,128]{1,0:T(8,128)(2,1)S(1)} %get-tuple-element.55), channel_id=1, source_target_pairs={{0,6},{1,7},{2,4},{3,5},{4,2},{5,3},{6,0},{7,1},{8,14},{9,15},{10,... | collective-permute-start | bytes 104456 | tf_op jit(solution)/shard_map/ppermute | solution.py:63
  73.9 6.0 %collective-permute-start.17 = (bf16[4,136,128]{2,1,0:T(8,128)(2,1)S(1)}, bf16[4,136,128]{2,1,0:T(8,128)(2,1)S(1)}, u32[]{:S(2)}, u32[]{:S(2)}) collective-permute-start(bf16[4,136,128]{2,1,0:T(8,128)(2,1)S(1)} %pad_maximum_fusion.1.refs_0_), channel_id=1, source_target_pairs={{0,17},{1,16},{2,19},{3,18},{4,21},{5,20},{6,23},{7,22},{8,25},{9,... | collective-permute-start | bytes 417800 | tf_op jit(solution)/shard_map/ppermute | solution.py:63
  75.5 5.7 %collective-permute-start.16 = (bf16[4,136,128]{2,1,0:T(8,128)(2,1)S(1)}, bf16[4,136,128]{2,1,0:T(8,128)(2,1)S(1)}, u32[]{:S(2)}, u32[]{:S(2)}) collective-permute-start(bf16[4,136,128]{2,1,0:T(8,128)(2,1)S(1)} %pad_maximum_fusion.1.refs_0_), channel_id=1, source_target_pairs={{0,16},{1,17},{2,18},{3,19},{4,20},{5,21},{6,22},{7,23},{8,24},{9,... | collective-permute-start | bytes 417800 | tf_op jit(solution)/shard_map/ppermute | solution.py:63
  76.6 5.1 %collective-permute-start.15 = (bf16[4,136,128]{2,1,0:T(8,128)(2,1)S(1)}, bf16[4,136,128]{2,1,0:T(8,128)(2,1)S(1)}, u32[]{:S(2)}, u32[]{:S(2)}) collective-permute-start(bf16[4,136,128]{2,1,0:T(8,128)(2,1)S(1)} %pad_maximum_fusion.1.refs_0_), channel_id=1, source_target_pairs={{0,1},{1,0},{2,3},{3,2},{4,5},{5,4},{6,7},{7,6},{8,9},{9,8},{10,11... | collective-permute-start | bytes 417800 | tf_op jit(solution)/shard_map/ppermute | solution.py:63
  77.4 4.4 %collective-permute-start.18 = (bf16[4,136,128]{2,1,0:T(8,128)(2,1)S(1)}, bf16[4,136,128]{2,1,0:T(8,128)(2,1)S(1)}, u32[]{:S(2)}, u32[]{:S(2)}) collective-permute-start(bf16[4,136,128]{2,1,0:T(8,128)(2,1)S(1)} %pad_maximum_fusion.1.refs_0_), channel_id=1, source_target_pairs={{0,8},{1,9},{2,10},{3,11},{4,12},{5,13},{6,14},{7,15},{8,0},{9,1},... | collective-permute-start | bytes 417800 | tf_op jit(solution)/shard_map/ppermute | solution.py:63
  79.9 1.9 %collective-permute-start.21 = (bf16[4,136,128]{2,1,0:T(8,128)(2,1)S(1)}, bf16[4,136,128]{2,1,0:T(8,128)(2,1)S(1)}, u32[]{:S(2)}, u32[]{:S(2)}) collective-permute-start(bf16[4,136,128]{2,1,0:T(8,128)(2,1)S(1)} %collective-permute-done.17.refs_3_), channel_id=1, source_target_pairs={{0,8},{1,9},{2,10},{3,11},{4,12},{5,13},{6,14},{7,15},{8,0},{9,1},... | collective-permute-start | bytes 417800 | tf_op jit(solution)/shard_map/ppermute | solution.py:63
  81.2 1.4 %collective-permute-start.20 = (bf16[4,136,128]{2,1,0:T(8,128)(2,1)S(1)}, bf16[4,136,128]{2,1,0:T(8,128)(2,1)S(1)}, u32[]{:S(2)}, u32[]{:S(2)}) collective-permute-start(bf16[4,136,128]{2,1,0:T(8,128)(2,1)S(1)} %collective-permute-done.16.refs_2_), channel_id=1, source_target_pairs={{0,8},{1,9},{2,10},{3,11},{4,12},{5,13},{6,14},{7,15},{8,0},{9,1},... | collective-permute-start | bytes 417800 | tf_op jit(solution)/shard_map/ppermute | solution.py:63
  81.7 1.4 %collective-permute-start.19 = (bf16[4,136,128]{2,1,0:T(8,128)(2,1)S(1)}, bf16[4,136,128]{2,1,0:T(8,128)(2,1)S(1)}, u32[]{:S(2)}, u32[]{:S(2)}) collective-permute-start(bf16[4,136,128]{2,1,0:T(8,128)(2,1)S(1)} %collective-permute-done.15.refs_1_), channel_id=1, source_target_pairs={{0,8},{1,9},{2,10},{3,11},{4,12},{5,13},{6,14},{7,15},{8,0},{9,1},... | collective-permute-start | bytes 417800 | tf_op jit(solution)/shard_map/ppermute | solution.py:63
